TPU v7x, 32 devices: a whole 2x2x4 slice. The times are simulated.
32 devices in a mesh: dp: 2 (over y), context: 4 (over z), expert: 4 (over x, core).
Axes of the slice: x: 2, y: 2, z: 4, core: 2. Of those that a mesh axis runs over, the one named last changes fastest.
Arguments:
- block_input: bfloat16 [8192, 2048], P(('dp', 'context', 'expert')), may hold values from -6 to 6
- teacher_states: float32 [8192, 2048], P(('dp', 'context', 'expert')), may hold values from -6 to 6
- seq_lengths: int32 [2], P('dp'), may hold values from 1024 to 4096, as said below
- expert_routes: int32 [8192, 8], P(('dp', 'context', 'expert')), may hold values from 0 to 15, all different within a row; in each aligned block of 256 rows (0 to 255, 256 to 511, ...) at most 160 rows name the same one
- attn_gain: float32 [2048], replicated, may hold values from 0.5 to 1.5
- query_weight: bfloat16 [2048, 2048], P(None, 'expert'), may hold values from -0.125 to 0.125
- key_weight: bfloat16 [2048, 2048], P(None, 'expert'), may hold values from -0.125 to 0.125
- value_weight: bfloat16 [2048, 2048], P(None, 'expert'), may hold values from -0.125 to 0.125
- query_gain: float32 [2048], P('expert'), may hold values from 0.5 to 1.5
- key_gain: float32 [2048], P('expert'), may hold values from 0.5 to 1.5
- output_weight: bfloat16 [2048, 2048], P('expert'), may hold values from -4 to 4
- ffn_gain: float32 [2048], replicated, may hold values from 0.5 to 1.5
- router_weight: bfloat16 [2048, 16], replicated, may hold values from -0.0625 to 0.0625
- gate_weight: bfloat16 [16, 2048, 1024], P(('context', 'expert'), None, 'dp'), may hold values from -0.125 to 0.125
- up_weight: bfloat16 [16, 2048, 1024], P(('context', 'expert'), None, 'dp'), may hold values from -0.125 to 0.125
- down_weight: bfloat16 [16, 1024, 2048], P(('context', 'expert'), 'dp'), may hold values from -4 to 4
Outputs:
- block_output: bfloat16 [8192, 2048], P(('dp', 'context', 'expert'))
- loss_value: float32 [], replicated
- input_grad: float32 [8192, 2048], P(('dp', 'context', 'expert'))
- attn_gain_grad: float32 [2048], replicated
- query_weight_grad: float32 [2048, 2048], P(None, 'expert')
- key_weight_grad: float32 [2048, 2048], P(None, 'expert')
- value_weight_grad: float32 [2048, 2048], P(None, 'expert')
- query_gain_grad: float32 [2048], P('expert')
- key_gain_grad: float32 [2048], P('expert')
- output_weight_grad: float32 [2048, 2048], P('expert')
- ffn_gain_grad: float32 [2048], replicated
- router_weight_grad: float32 [2048, 16], replicated
- gate_weight_grad: float32 [16, 2048, 1024], P(('context', 'expert'), None, 'dp')
- up_weight_grad: float32 [16, 2048, 1024], P(('context', 'expert'), None, 'dp')
- down_weight_grad: float32 [16, 1024, 2048], P(('context', 'expert'), 'dp')
Inputs may be any that keep to these rules, and one draw needn't show every extreme that they name: The first seq_lengths[s] of the 4096 positions of sequence s are valid tokens, the rest padding; at least one sequence is entirely valid. `expert_routes`: each row names 8 different experts. Within the rows of one device (aligned blocks of 256 rows) no expert is named more than 160 times, a bound that some block reaches.
All inputs are finite; a program needn't handle non-finite values.
Results may differ from a plain program's by a relative error of at most 0.02.
Values may be sent and summed in bfloat16 or wider, within the bound.
No kernel may reach another device: no remote copies, remote signals or barrier semaphores. Data moves between devices by JAX's collectives and lax.ppermute only.
A program may use at most 448 MiB of HBM per device.

v0:
```python
import jax
import jax.numpy as jnp
from jax import lax
from jax.sharding import PartitionSpec as P

HEADS = 16
HD = 128
TOPK = 8


EPSILON = 1e-05
ROPE_BASE = 10000.0
NEGATIVE = -1e30


def rms_scale(values):
    return lax.rsqrt(jnp.mean(values * values, axis=-1, keepdims=True) + EPSILON)


def rope_tables(positions):
    exponent = jnp.arange(HD // 2, dtype=jnp.float32) * (2.0 / HD)
    angles = positions.astype(jnp.float32)[:, None] * (ROPE_BASE ** (-exponent))[None, :]
    return (jnp.cos(angles), jnp.sin(angles))


def rotate(values, cosine, sine_part):
    halfway = values.shape[-1] // 2
    leading = values[..., :halfway]
    trailing = values[..., halfway:]
    cos_wide = cosine[:, None, :]
    sin_wide = sine_part[:, None, :]
    return jnp.concatenate(
        [leading * cos_wide - trailing * sin_wide, trailing * cos_wide + leading * sin_wide],
        axis=-1,
    )


def rotate_back(gradient, cosine, sine_part):
    halfway = gradient.shape[-1] // 2
    leading = gradient[..., :halfway]
    trailing = gradient[..., halfway:]
    cos_wide = cosine[:, None, :]
    sin_wide = sine_part[:, None, :]
    return jnp.concatenate(
        [leading * cos_wide + trailing * sin_wide, trailing * cos_wide - leading * sin_wide],
        axis=-1,
    )


def silu_parts(gate_part):
    sigmoid = jax.nn.sigmoid(gate_part)
    return (gate_part * sigmoid, sigmoid * (1.0 + gate_part * (1.0 - sigmoid)))


def gather_tokens(rows):
    return lax.all_gather(rows, "expert", axis=0, tiled=True)


def sum_tokens(term, rows):
    return lax.psum_scatter(
        term(jnp.int32(0), lax.axis_size("expert") * rows).astype(jnp.bfloat16),
        "expert",
        scatter_dimension=0,
        tiled=True,
    ).astype(jnp.float32)


def head_totals(pair):
    return lax.psum((pair[0], pair[1]), "expert")


def to_experts(buffer):
    return lax.all_to_all(buffer, ("context", "expert"), split_axis=1, concat_axis=0, tiled=True)


def to_owners(buffer):
    return lax.all_to_all(buffer, ("context", "expert"), split_axis=0, concat_axis=1, tiled=True)


def rows_over_dp(rows):
    return lax.all_gather(rows, "dp", axis=0, tiled=True)


def sum_over_dp(term, rows):
    return lax.psum_scatter(
        term(jnp.int32(0), lax.axis_size("dp") * rows).astype(jnp.bfloat16),
        "dp",
        scatter_dimension=0,
        tiled=True,
    ).astype(jnp.float32)


def contract_rows(left, right):
    return lax.dot_general(
        left, right, (((0,), (0,)), ((), ())), preferred_element_type=jnp.float32
    )


def contract_last(left, right):
    return lax.dot_general(
        left, right, (((1,), (1,)), ((), ())), preferred_element_type=jnp.float32
    )


def per_device(
    block_input,
    teacher_states,
    seq_lengths,
    expert_routes,
    attn_gain,
    query_weight,
    key_weight,
    value_weight,
    query_gain,
    key_gain,
    output_weight,
    ffn_gain,
    router_weight,
    gate_weight,
    up_weight,
    down_weight,
):
    tok_rows = block_input.shape[0]
    width = block_input.shape[1]
    head_width = query_weight.shape[1]
    heads_here = head_width // HD
    experts_all = router_weight.shape[1]
    capacity = 5 * tok_rows * TOPK // (4 * experts_all)
    context_size = lax.axis_size("context")
    expert_size = lax.axis_size("expert")
    token_count_all = tok_rows * lax.axis_size("dp") * context_size * expert_size
    block_rows = tok_rows * expert_size
    length = seq_lengths[0]
    block_start = lax.axis_index("context") * block_rows
    own_start = block_start + lax.axis_index("expert") * tok_rows
    score_scale = HD ** (-0.5)
    tokens = block_input.astype(jnp.float32)
    inverse_one = rms_scale(tokens)
    normed = (tokens * inverse_one * attn_gain).astype(jnp.bfloat16)
    block_normed = gather_tokens(normed)
    joint_weight = jnp.concatenate([query_weight, key_weight, value_weight], axis=1)
    projected = jnp.dot(block_normed, joint_weight, preferred_element_type=jnp.float32)
    query_raw = projected[:, :head_width]
    key_raw = projected[:, head_width : 2 * head_width]
    value_raw = projected[:, 2 * head_width :]
    query_total, key_total = head_totals(
        (jnp.sum(query_raw * query_raw, axis=-1), jnp.sum(key_raw * key_raw, axis=-1))
    )
    query_inv = lax.rsqrt(query_total / (HEADS * HD) + EPSILON)[:, None]
    key_inv = lax.rsqrt(key_total / (HEADS * HD) + EPSILON)[:, None]
    query_normed = query_raw * query_inv * query_gain
    key_normed = key_raw * key_inv * key_gain
    cosine, sine_part = rope_tables(block_start + jnp.arange(block_rows, dtype=jnp.int32))
    query_rot = rotate(query_normed.reshape(block_rows, heads_here, HD), cosine, sine_part).astype(
        jnp.bfloat16
    )
    key_rot = rotate(key_normed.reshape(block_rows, heads_here, HD), cosine, sine_part).astype(
        jnp.bfloat16
    )
    value_low = value_raw.reshape(block_rows, heads_here, HD).astype(jnp.bfloat16)
    all_keys, all_values = (
        lax.all_gather(key_rot, "context", axis=0, tiled=True),
        lax.all_gather(value_low, "context", axis=0, tiled=True),
    )
    seq_total = all_keys.shape[0]
    key_pos = jnp.arange(seq_total, dtype=jnp.int32)
    query_block = min(512, block_rows)
    count_blocks = block_rows // query_block
    starts = jnp.arange(count_blocks, dtype=jnp.int32) * query_block
    query_blocks = query_rot.reshape(count_blocks, query_block, heads_here, HD)

    def scores_for(query_part, offset):
        raw_scores = (
            jnp.einsum("qhd,khd->hqk", query_part, all_keys, preferred_element_type=jnp.float32)
            * score_scale
        )
        query_pos = block_start + offset + jnp.arange(query_block, dtype=jnp.int32)
        allowed = (key_pos[None, :] <= query_pos[:, None]) & (key_pos[None, :] < length)
        return (jnp.where(allowed[None], raw_scores, NEGATIVE), allowed)

    def forward_block(packed):
        query_part, offset = packed
        masked, allowed = scores_for(query_part, offset)
        highest = jnp.max(masked, axis=-1, keepdims=True)
        weights = jnp.exp(masked - highest)
        totals = jnp.sum(weights, axis=-1, keepdims=True)
        probabilities = (weights / totals).astype(jnp.bfloat16)
        context = jnp.einsum(
            "hqk,khd->qhd", probabilities, all_values, preferred_element_type=jnp.float32
        )
        return (context, (highest + jnp.log(totals))[..., 0])

    context_f, log_sums = lax.map(forward_block, (query_blocks, starts))
    context_low = context_f.reshape(block_rows, head_width).astype(jnp.bfloat16)

    def attn_term(offset, amount):
        return jnp.dot(context_low, output_weight, preferred_element_type=jnp.float32)

    attn_out = sum_tokens(attn_term, tok_rows)
    residual = tokens + attn_out
    inverse_two = rms_scale(residual)
    ffn_in = (residual * inverse_two * ffn_gain).astype(jnp.bfloat16)
    logits = jnp.dot(ffn_in, router_weight, preferred_element_type=jnp.float32)
    weights_router = jnp.exp(logits - jnp.max(logits, axis=-1, keepdims=True))
    router_probs = weights_router / jnp.sum(weights_router, axis=-1, keepdims=True)
    choose = (
        expert_routes[:, :, None] == jnp.arange(experts_all, dtype=jnp.int32)[None, None, :]
    ).astype(jnp.float32)
    gate_values = jnp.sum(choose * router_probs[:, None, :], axis=-1)
    flat_experts = expert_routes.reshape(-1)
    onehot = choose.reshape(-1, experts_all).astype(jnp.int32)
    earlier = jnp.cumsum(onehot, axis=0) - onehot
    flat_slots = jnp.sum(earlier * onehot, axis=-1)
    repeated = jnp.repeat(ffn_in, TOPK, axis=0)
    dispatch_buf = (
        jnp.zeros((capacity, experts_all, width), jnp.bfloat16)
        .at[flat_slots, flat_experts]
        .set(repeated)
    )
    expert_rows = to_experts(dispatch_buf)
    own_rows = expert_rows.shape[0]
    all_rows = rows_over_dp(expert_rows)
    gate_part = jnp.einsum(
        "red,edf->ref", all_rows, gate_weight, preferred_element_type=jnp.float32
    )
    up_part = jnp.einsum("red,edf->ref", all_rows, up_weight, preferred_element_type=jnp.float32)
    silu_value, silu_slope = silu_parts(gate_part)
    hidden = (silu_value * up_part).astype(jnp.bfloat16)

    def down_term(offset, amount):
        return jnp.einsum("ref,efd->red", hidden, down_weight, preferred_element_type=jnp.float32)

    expert_out = sum_over_dp(down_term, own_rows).astype(jnp.bfloat16)
    returned = to_owners(expert_out)
    picked = returned[flat_slots, flat_experts].astype(jnp.float32).reshape(tok_rows, TOPK, width)
    mixture = jnp.sum(picked * gate_values[:, :, None], axis=1)
    output_full = residual + mixture
    own_pos = own_start + jnp.arange(tok_rows, dtype=jnp.int32)
    valid = (own_pos < length).astype(jnp.float32)
    difference = output_full - teacher_states
    local_loss = jnp.sum(jnp.sum(difference * difference, axis=-1) * valid)
    loss_total, count_total = lax.psum((local_loss, jnp.sum(valid)), ("dp", "context", "expert"))
    loss_value = loss_total / count_total
    grad_out = difference * (valid * (token_count_all / count_total))[:, None]
    grad_gates = jnp.sum(picked * grad_out[:, None, :], axis=-1)
    grad_rows_out = (
        (grad_out[:, None, :] * gate_values[:, :, None]).astype(jnp.bfloat16).reshape(-1, width)
    )
    grad_buf = (
        jnp.zeros((capacity, experts_all, width), jnp.bfloat16)
        .at[flat_slots, flat_experts]
        .set(grad_rows_out)
    )
    grad_expert = to_experts(grad_buf)
    grad_all = rows_over_dp(grad_expert)
    down_total = jnp.einsum("ref,red->efd", hidden, grad_all, preferred_element_type=jnp.float32)
    grad_hidden = jnp.einsum(
        "red,efd->ref", grad_all, down_weight, preferred_element_type=jnp.float32
    )
    grad_gate = (grad_hidden * up_part * silu_slope).astype(jnp.bfloat16)
    grad_up = (grad_hidden * silu_value).astype(jnp.bfloat16)
    gate_total = jnp.einsum("red,ref->edf", all_rows, grad_gate, preferred_element_type=jnp.float32)
    up_total = jnp.einsum("red,ref->edf", all_rows, grad_up, preferred_element_type=jnp.float32)

    def back_term(offset, amount):
        return jnp.einsum(
            "ref,edf->red", grad_gate, gate_weight, preferred_element_type=jnp.float32
        ) + jnp.einsum("ref,edf->red", grad_up, up_weight, preferred_element_type=jnp.float32)

    grad_expert_rows = sum_over_dp(back_term, own_rows).astype(jnp.bfloat16)
    grad_back = to_owners(grad_expert_rows)
    grad_ffn_experts = jnp.sum(
        grad_back[flat_slots, flat_experts].astype(jnp.float32).reshape(tok_rows, TOPK, width),
        axis=1,
    )
    grad_router_probs = jnp.sum(choose * grad_gates[:, :, None], axis=1)
    grad_logits = router_probs * (
        grad_router_probs - jnp.sum(router_probs * grad_router_probs, axis=-1, keepdims=True)
    )
    router_grad = lax.dot_general(
        ffn_in.astype(jnp.float32),
        grad_logits,
        (((0,), (0,)), ((), ())),
        precision=lax.Precision.HIGHEST,
    )
    grad_ffn = grad_ffn_experts + lax.dot_general(
        grad_logits,
        router_weight.astype(jnp.float32),
        (((1,), (1,)), ((), ())),
        precision=lax.Precision.HIGHEST,
    )
    ffn_gain_grad = jnp.sum(residual * inverse_two * grad_ffn, axis=0)
    weighted_two = grad_ffn * ffn_gain
    grad_residual = (
        grad_out
        + inverse_two * weighted_two
        - residual * inverse_two**3 * jnp.mean(residual * weighted_two, axis=-1, keepdims=True)
    )
    block_grad = gather_tokens(grad_residual.astype(jnp.bfloat16))
    output_grad = contract_rows(context_low, block_grad)
    grad_context = contract_last(block_grad, output_weight).astype(jnp.bfloat16)
    grad_blocks = grad_context.reshape(count_blocks, query_block, heads_here, HD)

    def backward_block(running, packed):
        key_acc, value_acc = running
        query_part, grad_part, log_part, offset = packed
        masked, allowed = scores_for(query_part, offset)
        probabilities = jnp.where(allowed[None], jnp.exp(masked - log_part[..., None]), 0.0)
        grad_probs = jnp.einsum(
            "qhd,khd->hqk", grad_part, all_values, preferred_element_type=jnp.float32
        )
        row_dot = jnp.sum(probabilities * grad_probs, axis=-1, keepdims=True)
        grad_scores = (probabilities * (grad_probs - row_dot)).astype(jnp.bfloat16)
        query_grad = (
            jnp.einsum("hqk,khd->qhd", grad_scores, all_keys, preferred_element_type=jnp.float32)
            * score_scale
        )
        key_acc = (
            key_acc
            + jnp.einsum(
                "hqk,qhd->khd", grad_scores, query_part, preferred_element_type=jnp.float32
            )
            * score_scale
        )
        value_acc = value_acc + jnp.einsum(
            "hqk,qhd->khd",
            probabilities.astype(jnp.bfloat16),
            grad_part,
            preferred_element_type=jnp.float32,
        )
        return ((key_acc, value_acc), query_grad)

    zeros_keys = jnp.zeros((seq_total, heads_here, HD), jnp.float32)
    (key_acc, value_acc), query_grads = lax.scan(
        backward_block, (zeros_keys, zeros_keys), (query_blocks, grad_blocks, log_sums, starts)
    )
    key_grad_rot, value_grad = (
        lax.psum_scatter(
            key_acc.astype(jnp.bfloat16), "context", scatter_dimension=0, tiled=True
        ).astype(jnp.float32),
        lax.psum_scatter(
            value_acc.astype(jnp.bfloat16), "context", scatter_dimension=0, tiled=True
        ).astype(jnp.float32),
    )
    grad_query_normed = rotate_back(
        query_grads.reshape(block_rows, heads_here, HD), cosine, sine_part
    ).reshape(block_rows, head_width)
    grad_key_normed = rotate_back(key_grad_rot, cosine, sine_part).reshape(block_rows, head_width)
    query_gain_grad = jnp.sum(query_raw * query_inv * grad_query_normed, axis=0)
    key_gain_grad = jnp.sum(key_raw * key_inv * grad_key_normed, axis=0)
    query_dot_all, key_dot_all = head_totals(
        (
            jnp.sum(query_raw * query_gain * grad_query_normed, axis=-1),
            jnp.sum(key_raw * key_gain * grad_key_normed, axis=-1),
        )
    )
    grad_query = (
        query_inv * query_gain * grad_query_normed
        - query_raw * query_inv**3 * (query_dot_all / (HEADS * HD))[:, None]
    ).astype(jnp.bfloat16)
    grad_key = (
        key_inv * key_gain * grad_key_normed
        - key_raw * key_inv**3 * (key_dot_all / (HEADS * HD))[:, None]
    ).astype(jnp.bfloat16)
    grad_value = value_grad.reshape(block_rows, head_width).astype(jnp.bfloat16)
    grad_joint = jnp.concatenate([grad_query, grad_key, grad_value], axis=1)
    joint_grad = contract_rows(block_normed, grad_joint)

    def input_term(offset, amount):
        return contract_last(grad_joint, joint_weight)

    grad_normed = sum_tokens(input_term, tok_rows)
    attn_gain_grad = jnp.sum(tokens * inverse_one * grad_normed, axis=0)
    weighted_one = grad_normed * attn_gain
    input_grad = (
        grad_residual
        + inverse_one * weighted_one
        - tokens * inverse_one**3 * jnp.mean(tokens * weighted_one, axis=-1, keepdims=True)
    )
    (
        joint_total,
        output_total,
        query_gain_total,
        key_gain_total,
        attn_partial,
        ffn_partial,
        router_partial,
    ) = (
        lax.psum(joint_grad.astype(jnp.bfloat16), ("dp", "context")).astype(jnp.float32),
        lax.psum(output_grad.astype(jnp.bfloat16), ("dp", "context")).astype(jnp.float32),
        lax.psum(query_gain_grad.astype(jnp.bfloat16), ("dp", "context")).astype(jnp.float32),
        lax.psum(key_gain_grad.astype(jnp.bfloat16), ("dp", "context")).astype(jnp.float32),
        lax.psum(attn_gain_grad.astype(jnp.bfloat16), ("dp", "context")).astype(jnp.float32),
        lax.psum(ffn_gain_grad.astype(jnp.bfloat16), ("dp", "context")).astype(jnp.float32),
        lax.psum(router_grad.astype(jnp.bfloat16), ("dp", "context")).astype(jnp.float32),
    )
    attn_total, ffn_total, router_total = (
        lax.psum(attn_partial.astype(jnp.bfloat16), "expert").astype(jnp.float32),
        lax.psum(ffn_partial.astype(jnp.bfloat16), "expert").astype(jnp.float32),
        lax.psum(router_partial.astype(jnp.bfloat16), "expert").astype(jnp.float32),
    )
    return (
        output_full.astype(jnp.bfloat16),
        loss_value,
        input_grad,
        attn_total,
        joint_total[:, :head_width],
        joint_total[:, head_width : 2 * head_width],
        joint_total[:, 2 * head_width :],
        query_gain_total,
        key_gain_total,
        output_total,
        ffn_total,
        router_total,
        gate_total,
        up_total,
        down_total,
    )


def solution(mesh):
    placed = (
        P(("dp", "context", "expert"), None),
        P(("dp", "context", "expert"), None),
        P("dp"),
        P(("dp", "context", "expert"), None),
        P(),
        P(None, "expert"),
        P(None, "expert"),
        P(None, "expert"),
        P("expert"),
        P("expert"),
        P("expert", None),
        P(),
        P(),
        P(("context", "expert"), None, "dp"),
        P(("context", "expert"), None, "dp"),
        P(("context", "expert"), "dp", None),
    )
    return jax.shard_map(
        per_device,
        mesh=mesh,
        in_specs=placed,
        out_specs=(
            P(("dp", "context", "expert"), None),
            P(),
            P(("dp", "context", "expert"), None),
            P(),
            P(None, "expert"),
            P(None, "expert"),
            P(None, "expert"),
            P("expert"),
            P("expert"),
            P("expert", None),
            P(),
            P(),
            P(("context", "expert"), None, "dp"),
            P(("context", "expert"), None, "dp"),
            P(("context", "expert"), "dp", None),
        ),
        check_vma=False,
    )
```

profile of v0, /device:TPU:0, one launch (start us, length us, event | category | flops | bytes accessed | tf_op | source)
XLA Modules:
  0.0 3640.7 jit_solution(4024163344542784451)
XLA Ops:
  19.1 30.9 all-gather.7.cloned.1.call-done
  98.1 46.6 %all-gather.11.cloned.1.call-done = bf16[4096,4,128]{2,0,1:T(8,128)(2,1)} async-done(((bf16[1024,4,128]{2,0,1:T(8,128)(2,1)}), bf16[4096,4,128]{2,0,1:T(8,128)(2,1)}) %all-gather.11.cloned.1.call-update) | async-done | bytes 4194320 | tf_op jit(solution)/shard_map/all_gather | solution.py:163
  144.7 81.5 %all-gather.9.cloned.1.call-done = bf16[4096,4,128]{2,0,1:T(8,128)(2,1)} async-done(((bf16[1024,4,128]{2,0,1:T(8,128)(2,1)}), bf16[4096,4,128]{2,0,1:T(8,128)(2,1)}) %all-gather.9.cloned.1.call-update) | async-done | bytes 4194320 | tf_op jit(solution)/shard_map/all_gather | solution.py:162
  226.2 108.2 %while.30 = (s32[]{:T(128)}, bf16[2,512,4,128]{3,1,2,0:T(8,128)(2,1)}, f32[2,4,512]{2,1,0:T(4,128)S(1)}, s32[2]{0:T(128)S(1)}, s32[]{:T(128)}, /*index=5*/s32[]{...) while((s32[]{:T(128)}, ...), condition=%wide.region_8.9_spmd.clone.clone, body=%wide.region_5.8_spmd.clone.clone.sunk | while | flops 4399827456 | bytes 127479992 | solution.py:193
  230.1 16.7 fusion.172
  246.8 15.1 fusion.173
  261.9 18.3 fusion.174
  283.9 16.7 fusion.172
  300.6 15.1 fusion.173
  315.7 18.3 fusion.174
  350.2 36.4 reduce-scatter.11.cloned.1.call-done
  391.4 18.4 scatter_custom_fusion
  409.9 13.8 copy.190
  423.6 231.9 %all_to_all.72 = bf16[160,16,2048]{2,0,1:T(8,128)(2,1)} all-to-all(bf16[160,16,2048]{2,0,1:T(8,128)(2,1)} %copy.190), channel_id=1, replica_groups=mesh['dp'=2,'context'=4,'expert'=4] {'context','expert'}, dimensions={1} | all-to-all | bytes 20971520 | tf_op jit(solution)/shard_map/all_to_all | solution.py:73
  655.8 248.5 %all-gather.13.cloned.1.call-done = bf16[5120,1,2048]{2,0,1:T(8,128)(2,1)} async-done(((bf16[2560,1,2048]{2,0,1:T(8,128)(2,1)}), bf16[5120,1,2048]{2,0,1:T(8,128)(2,1)}) %all-gather.13.cloned.1.call-update) | async-done | bytes 20971536 | tf_op jit(solution)/shard_map/all_gather | solution.py:81
  904.3 15.3 fusion.42
  919.6 21.4 fusion.44
  950.0 16.6 convolution_convert_fusion
  966.7 234.4 %reduce-scatter.19.cloned.1.call-done = bf16[1,16,327680]{2,1,0:T(8,128)(2,1)} async-done(((bf16[1,32,327680]{2,1,0:T(8,128)(2,1)}), bf16[1,16,327680]{2,1,0:T(8,128)(2,1)}) %reduce-scatter.19.cloned.1.call-update) | async-done | bytes 10485776
  1201.5 15.2 reduce.12
  1216.7 16.0 reshape.497
  1239.8 246.9 %psum.115 = f32[]{:T(128)} all-reduce(f32[]{:T(128)} %convert_reduce_fusion.1), channel_id=1, replica_groups=mesh['dp'=2,'context'=4,'expert'=4] {'dp','context','expert'}, use_global_device_ids=true, to_apply=%region_24.25 | all-reduce | flops 1 | bytes 8 | tf_op jit(solution)/shard_map/psum | solution.py:242
  1489.3 18.4 reshape.498
  1507.7 16.2 copy.212
  1523.9 13.6 copy.277
  1537.6 50.6 %gather_fusion = bf16[2048,2048]{1,0:T(8,128)(2,1)} fusion(bf16[160,16,2048]{2,1,0:T(8,128)(2,1)} %bitcast.338, s32[2048]{0:T(1024)S(1)} %bitcast.340), kind=kCustom, calls=%fused_computation | custom fusion | bytes 16793600 | tf_op jit(solution)/shard_map/gather | solution.py:235
  1588.2 12.6 fusion.46
  1605.3 19.3 scatter_custom_fusion.1
  1624.6 13.8 copy.195
  1638.3 232.6 %all_to_all.73 = bf16[160,16,2048]{2,0,1:T(8,128)(2,1)} all-to-all(bf16[160,16,2048]{2,0,1:T(8,128)(2,1)} %copy.195), channel_id=1, replica_groups=mesh['dp'=2,'context'=4,'expert'=4] {'context','expert'}, dimensions={1} | all-to-all | bytes 20971520 | tf_op jit(solution)/shard_map/all_to_all | solution.py:73
  1871.5 248.0 %all-gather.15.cloned.1.call-done = bf16[5120,1,2048]{2,0,1:T(8,128)(2,1)} async-done(((bf16[2560,1,2048]{2,0,1:T(8,128)(2,1)}), bf16[5120,1,2048]{2,0,1:T(8,128)(2,1)}) %all-gather.15.cloned.1.call-update) | async-done | bytes 20971536 | tf_op jit(solution)/shard_map/all_gather | solution.py:81
  2119.5 23.4 fusion.65
  2142.8 22.1 fusion.67
  2165.0 24.6 add_convert_fusion
  2189.6 234.4 %reduce-scatter.21.cloned.1.call-done = bf16[1,16,327680]{2,1,0:T(8,128)(2,1)} async-done(((bf16[1,32,327680]{2,1,0:T(8,128)(2,1)}), bf16[1,16,327680]{2,1,0:T(8,128)(2,1)}) %reduce-scatter.21.cloned.1.call-update) | async-done | bytes 10485776
  2424.0 15.0 reduce.13
  2439.0 16.0 reshape.499
  2466.2 181.9 %all-to-all-done.3 = bf16[16,2,163840]{2,1,0:T(2,128)(2,1)} async-done(((bf16[16,2,163840]{2,1,0:T(2,128)(2,1)}), bf16[16,2,163840]{2,1,0:T(2,128)(2,1)}, u32[]{:S(2)}, u32[]{:S(2)}) %all-to-all-start.3) | async-done | bytes 10485792 | tf_op jit(solution)/shard_map/all_to_all | solution.py:77
  2648.1 18.6 reshape.500
  2666.7 16.2 copy.213
  2682.9 13.8 copy.276
  2696.7 50.9 %gather_fusion.1 = bf16[2048,2048]{1,0:T(8,128)(2,1)} fusion(bf16[160,16,2048]{2,1,0:T(8,128)(2,1)} %bitcast.339, s32[2048]{0:T(1024)S(1)} %bitcast.341), kind=kCustom, calls=%fused_computation.1 | custom fusion | bytes 16793600 | tf_op jit(solution)/shard_map/gather | solution.py:273
  2768.3 73.8 %all-gather.17.cloned.1.call-done = bf16[1024,2048]{1,0:T(8,128)(2,1)} async-done(((bf16[256,2048]{1,0:T(8,128)(2,1)}), bf16[1024,2048]{1,0:T(8,128)(2,1)}) %all-gather.17.cloned.1.call-update) | async-done | bytes 4194320 | tf_op jit(solution)/shard_map/all_gather | solution.py:56
  2847.7 242.6 %while.31 = (s32[]{:T(128)}, f32[4096,4,128]{0,2,1:T(8,128)}, f32[4096,4,128]{0,2,1:T(8,128)}, f32[2,512,4,128]{3,1,0,2:T(8,128)}, bf16[2,512,4,128]{3,1,2,0:T(8...) while((s32[]{:T(128)}, f32[4096,4,128]{0,2,1:T(8,128)}, ...), condition=%wide.region_34.35_spmd.clone.clone, body=%wide.region_32.34_spmd.clone.clone.sunk | while | flops 10903357440 | bytes 318836992 | solution.py:334
  2852.0 15.3 fusion.183
  2867.3 20.4 bitcast_add_fusion.5
  2887.7 26.8 multiply_reduce_fusion.10
  2914.5 27.7 multiply_convert_fusion.3
  2942.2 12.4 fusion.185
  2971.1 15.3 fusion.183
  2986.4 21.9 bitcast_add_fusion.5
  3008.2 26.8 multiply_reduce_fusion.10
  3035.0 27.7 multiply_convert_fusion.3
  3062.7 12.4 fusion.185
  3075.1 14.7 bitcast_add_fusion.4
  3103.7 70.8 %reduce-scatter.13.cloned.1.call-done = bf16[1024,4,128]{2,0,1:T(8,128)(2,1)} async-done(((bf16[4096,4,128]{2,0,1:T(8,128)(2,1)}), bf16[1024,4,128]{2,0,1:T(8,128)(2,1)}) %reduce-scatter.13.cloned.1.call-update) | async-done | bytes 1048592 | tf_op jit(solution)/shard_map/reduce_scatter | solution.py:338
  3190.2 64.4 %reduce-scatter.15.cloned.1.call-done = bf16[1024,4,128]{0,2,1:T(8,128)(2,1)} async-done(((bf16[4096,4,128]{0,2,1:T(8,128)(2,1)}), bf16[1024,4,128]{0,2,1:T(8,128)(2,1)}) %reduce-scatter.15.cloned.1.call-update) | async-done | bytes 1048592 | tf_op jit(solution)/shard_map/reduce_scatter | solution.py:341
  3291.8 18.8 fusion.80
  3310.5 18.2 fusion.72
  3329.4 17.7 fusion.77
  3347.1 44.0 %psum.114 = f32[]{:T(128)} all-reduce(f32[]{:T(128)} %select_reduce_fusion.2), channel_id=1, replica_groups=mesh['dp'=2,'context'=4,'expert'=4] {'dp','context','expert'}, use_global_device_ids=true, to_apply=%region_22.23 | all-reduce | flops 1 | bytes 8 | tf_op jit(solution)/shard_map/psum | solution.py:242
  3394.8 40.6 %all-reduce.2 = (bf16[2048]{0:T(1024)(128)(2,1)S(1)}, bf16[512]{0:T(512)(128)(2,1)S(1)}, bf16[512]{0:T(512)(128)(2,1)S(1)}, bf16[2048]{0:T(1024)(128)(2,1)S(1)}) all-reduce(bf16[2048]{0:T(1024)(128)(2,1)S(1)} %get-tuple-element.367, ...), channel_id=1, replica_groups=mesh['dp'=2,'context'=4,'expert'=4] {'dp','context'}, use_global_device_ids=true, to_apply=%region_44.45 | all-reduce | flops 5120 | bytes 20480 | tf_op jit(solution)/shard_map/psum | solution.py:393
  3447.7 151.3 %all-reduce.10.cloned.1.call-done = (bf16[2048,1536]{1,0:T(8,128)(2,1)}, bf16[512,2048]{1,0:T(8,128)(2,1)}, bf16[2048,16]{0,1:T(8,128)(2,1)}) async-done(((bf16[2048,1536]{1,0:T(8,128)(2,1)}, bf16[512,2048]{1,0:T(8,128)(2,1)}, bf16[2048,16]{0,1:T(8,128)(2,1)}), (bf16[2048,1536]{1,0:T(8,128)(2,1)}, bf16[512,2048]{1,0:T(8,128)(2,1)}, bf16[2048,16]{0,1:T(8,128)(2,1)})) %all-reduce.10.cloned.1.call-update) | async-done | bytes 8454160 | tf_op jit(solution)/shard_map/psum | solution.py:389
  3609.9 21.4 all-reduce.8.cloned.1.call-done
  (332 shorter events, 259.3 us)
Async XLA Ops:
  7.2 942.8 %copy-start = (bf16[1,512,2048]{2,1,0:T(8,128)(2,1)S(1)}, bf16[1,512,2048]{2,1,0:T(8,128)(2,1)}, u32[]{:S(2)}) copy-start(bf16[1,512,2048]{2,1,0:T(8,128)(2,1)} %param.35) | copy-start | bytes 6291460
  7.2 42.7 %all-gather.7.cloned.1.call-start = ((), (), s32[]{:S(2)}) async-start(), calls=%async_computation.10 | async-start | bytes 5242880 | tf_op jit(solution)/shard_map/all_gather | solution.py:56
  12.6 132.1 %all-gather.11.cloned.1.call-start = ((), (), s32[]{:S(2)}) async-start(), calls=%async_computation.12 | async-start | bytes 5242880 | tf_op jit(solution)/shard_map/all_gather | solution.py:163
  62.6 13.3 copy-start.55
  62.6 13.3 copy-start.57
  63.8 162.4 %all-gather.9.cloned.1.call-start = ((), (), s32[]{:S(2)}) async-start(), calls=%async_computation.11 | async-start | bytes 5242880 | tf_op jit(solution)/shard_map/all_gather | solution.py:162
  65.7 25.4 copy-start.24
  65.7 25.4 copy-start.26
  95.1 291.5 %reduce-scatter.11.cloned.1.call-start = ((), (), s32[]{:S(2)}) async-start(), calls=%async_computation.13 | async-start | bytes 5242880 | tf_op jit(solution)/shard_map/reduce_scatter | solution.py:60
  230.1 16.7 copy-start.2
  283.9 16.7 copy-start.2
  334.4 9.0 copy-start.81
  343.4 6.7 copy-start.76
  343.4 43.2 %copy-start.5 = (bf16[256,2048]{1,0:T(8,128)(2,1)S(1)}, bf16[256,2048]{1,0:T(8,128)(2,1)}, u32[]{:S(2)}) copy-start(bf16[256,2048]{1,0:T(8,128)(2,1)} %param.20) | copy-start | bytes 3145732
  343.4 45.4 %copy-start.49 = (f32[2048]{0:T(1024)S(1)}, f32[2048]{0:T(1024)}, u32[]{:S(2)}) copy-start(f32[2048]{0:T(1024)} %param.31) | copy-start | bytes 24580
  343.4 560.9 %all-gather.13.cloned.1.call-start = ((), (), s32[]{:S(2)}) async-start(), calls=%async_computation.14 | async-start | bytes 31457280 | tf_op jit(solution)/shard_map/all_gather | solution.py:81
  350.0 1187.6 %copy-start.3 = (s32[2048,1]{0,1:T(1,128)}, s32[2048,1]{0,1:T(1,128)S(1)}, u32[]{:S(2)}) copy-start(s32[2048,1]{0,1:T(1,128)S(1)} %get-tuple-element.456) | copy-start | bytes 24580
  350.2 59.6 %copy-start.72 = (s32[2048]{0:T(1024)}, s32[2048]{0:T(1024)S(1)}, u32[]{:S(2)}) copy-start(s32[2048]{0:T(1024)S(1)} %broadcast_select_fusion) | copy-start | bytes 24580
  388.8 21.0 copy-start.61
  655.6 545.4 %reduce-scatter.19.cloned.1.call-start = ((), (), s32[]{:S(2)}) async-start(), calls=%async_computation.21 | async-start | bytes 31457280
  904.3 15.3 copy-start.79
  919.6 21.4 copy-start.23
  1232.7 254.7 %copy-start.19 = (bf16[256,2048]{1,0:T(8,128)(2,1)S(1)}, bf16[256,2048]{1,0:T(8,128)(2,1)}, u32[]{:S(2)}) copy-start(bf16[256,2048]{1,0:T(8,128)(2,1)} %multiply_convert_fusion.1) | copy-start | bytes 3145732
  1232.7 254.7 %copy-start.35 = (bf16[2048,16]{0,1:T(8,128)(2,1)S(1)}, bf16[2048,16]{0,1:T(8,128)(2,1)}, u32[]{:S(2)}) copy-start(bf16[2048,16]{0,1:T(8,128)(2,1)} %param.32) | copy-start | bytes 196612
  1232.7 256.6 %all-to-all-start.1 = ((bf16[16,2,163840]{2,1,0:T(2,128)(2,1)}), bf16[16,2,163840]{2,1,0:T(2,128)(2,1)}, u32[]{:S(2)}, u32[]{:S(2)}) async-start(bf16[16,2,163840]{2,1,0:T(2,128)(2,1)} %reshape.497), calls=%async_computation.2 | async-start | bytes 20971520 | tf_op jit(solution)/shard_map/all_to_all | solution.py:77
  1238.5 880.9 %all-gather.15.cloned.1.call-start = ((), (), s32[]{:S(2)}) async-start(), calls=%async_computation.15 | async-start | bytes 31457280 | tf_op jit(solution)/shard_map/all_gather | solution.py:81
  1588.2 12.6 copy-start.6
  1871.0 553.0 %reduce-scatter.21.cloned.1.call-start = ((), (), s32[]{:S(2)}) async-start(), calls=%async_computation.22 | async-start | bytes 31457280
  2142.8 22.1 copy-start.80
  2455.0 193.0 %all-to-all-start.3 = ((bf16[16,2,163840]{2,1,0:T(2,128)(2,1)}), bf16[16,2,163840]{2,1,0:T(2,128)(2,1)}, u32[]{:S(2)}, u32[]{:S(2)}) async-start(bf16[16,2,163840]{2,1,0:T(2,128)(2,1)} %reshape.499), calls=%async_computation.4 | async-start | bytes 20971520 | tf_op jit(solution)/shard_map/all_to_all | solution.py:77
  2460.9 381.3 %all-gather.17.cloned.1.call-start = ((), (), s32[]{:S(2)}) async-start(), calls=%async_computation.16 | async-start | bytes 5242880 | tf_op jit(solution)/shard_map/all_gather | solution.py:56
  2466.2 293.0 %copy-start.42 = (f32[256,16]{0,1:T(8,128)}, f32[256,16]{0,1:T(8,128)S(1)}, u32[]{:S(2)}) copy-start(f32[256,16]{0,1:T(8,128)S(1)} %select_reduce_fusion) | copy-start | bytes 49156
  2466.2 293.0 %copy-start.70 = (f32[256]{0:T(256)}, f32[256]{0:T(256)S(1)}, u32[]{:S(2)}) copy-start(f32[256]{0:T(256)S(1)} %multiply_reduce_fusion.8) | copy-start | bytes 3076
  2682.9 13.8 copy-start.4
  2747.7 11.5 copy-start.7
  2747.7 11.5 copy-start.13
  2747.7 11.5 copy-start.36
  2747.7 11.5 copy-start.40
  2747.7 11.5 copy-start.50
  2747.7 11.5 copy-start.62
  2768.2 406.2 %reduce-scatter.13.cloned.1.call-start = ((), (), s32[]{:S(2)}) async-start(), calls=%async_computation.17 | async-start | bytes 5242880 | tf_op jit(solution)/shard_map/reduce_scatter | solution.py:338
  2768.3 79.4 %copy-start.9 = (bf16[2,512,4,128]{3,1,2,0:T(8,128)(2,1)S(1)}, bf16[2,512,4,128]{3,1,2,0:T(8,128)(2,1)}, u32[]{:S(2)}) copy-start(bf16[2,512,4,128]{3,1,2,0:T(8,128)(2,1)} %get-tuple-element.703) | copy-start | bytes 3145732
  2768.3 79.4 %copy-start.45 = (f32[2,4,512]{2,1,0:T(4,128)S(1)}, f32[2,4,512]{2,1,0:T(4,128)}, u32[]{:S(2)}) copy-start(f32[2,4,512]{2,1,0:T(4,128)} %copy-done.44) | copy-start | bytes 49156
  2768.3 79.4 %copy-start.82 = (s32[2]{0:T(128)S(1)}, s32[2]{0:T(128)}, u32[]{:S(2)}) copy-start(s32[2]{0:T(128)} %copy-done.81) | copy-start | bytes 28
  2954.6 12.4 copy-start.22
  3075.1 14.7 copy-start.22
  3097.5 157.1 %reduce-scatter.15.cloned.1.call-start = ((), (), s32[]{:S(2)}) async-start(), calls=%async_computation.18 | async-start | bytes 5242880 | tf_op jit(solution)/shard_map/reduce_scatter | solution.py:341
  3103.6 72.4 %copy-start.25 = (f32[1024,64]{1,0:T(8,128)S(1)}, f32[1024,64]{1,0:T(8,128)}, u32[]{:S(2)}) copy-start(f32[1024,64]{1,0:T(8,128)} %copy-done.24) | copy-start | bytes 786436
  3103.6 72.4 %copy-start.27 = (f32[1024,64]{1,0:T(8,128)S(1)}, f32[1024,64]{1,0:T(8,128)}, u32[]{:S(2)}) copy-start(f32[1024,64]{1,0:T(8,128)} %copy-done.26) | copy-start | bytes 786436
  3103.6 288.8 %reduce-scatter.17.cloned.1.call-start = ((), (), s32[]{:S(2)}) async-start(), calls=%async_computation.19 | async-start | bytes 5242880 | tf_op jit(solution)/shard_map/reduce_scatter | solution.py:60
  3179.9 76.3 %copy-start.64 = (f32[1024]{0:T(1024)S(1)}, f32[1024]{0:T(1024)}, u32[]{:S(2)}) copy-start(f32[1024]{0:T(1024)} %get-tuple-element.463) | copy-start | bytes 12292
  3179.9 76.3 %copy-start.65 = (f32[1024]{0:T(1024)S(1)}, f32[1024]{0:T(1024)}, u32[]{:S(2)}) copy-start(f32[1024]{0:T(1024)} %get-tuple-element.473) | copy-start | bytes 12292
  3273.4 325.6 %all-reduce.10.cloned.1.call-start = ((), (), s32[]{:S(2)}) async-start(), calls=%async_computation.23 | async-start | bytes 16908288 | tf_op jit(solution)/shard_map/psum | solution.py:389
  3291.7 339.6 %all-reduce.8.cloned.1.call-start = ((), (), s32[]{:S(2)}) async-start(), calls=%async_computation.20 | async-start | bytes 131072 | tf_op jit(solution)/shard_map/psum | solution.py:400
  3291.8 37.5 %slice-start.2 = ((s8[5242880]{0:T(1024)(128)(4,1)}), s8[4194304]{0:T(1024)(128)(4,1)S(1)}, s32[]{:S(2)}) async-start(s8[5242880]{0:T(1024)(128)(4,1)} %bitcast.355), calls=%async_computation.26 | async-start | bytes 8388608
  3310.5 18.2 copy-start.75
  3310.5 18.8 slice-start.3
  3329.3 63.1 %copy-start.8 = (bf16[256,2048]{1,0:T(8,128)(2,1)S(1)}, bf16[256,2048]{1,0:T(8,128)(2,1)}, u32[]{:S(2)}) copy-start(bf16[256,2048]{1,0:T(8,128)(2,1)} %param.20) | copy-start | bytes 3145732
  3329.3 63.1 %copy-start.46 = (f32[2048]{0:T(1024)S(1)}, f32[2048]{0:T(1024)}, u32[]{:S(2)}) copy-start(f32[2048]{0:T(1024)} %param.24) | copy-start | bytes 24580
  3329.3 63.1 %copy-start.60 = (f32[256]{0:T(256)S(1)}, f32[256]{0:T(256)}, u32[]{:S(2)}) copy-start(f32[256]{0:T(256)} %copy-done.59) | copy-start | bytes 3076
  3329.3 65.4 %copy-start.63 = (bf16[2048]{0:T(1024)(128)(2,1)S(1)}, bf16[2048]{0:T(1024)(128)(2,1)}, u32[]{:S(2)}) copy-start(bf16[2048]{0:T(1024)(128)(2,1)} %get-tuple-element.364) | copy-start | bytes 12292
  3329.3 114.6 %copy-start.73 = (f32[256]{0:T(256)S(1)}, f32[256]{0:T(256)}, u32[]{:S(2)}) copy-start(f32[256]{0:T(256)} %get-tuple-element.465) | copy-start | bytes 3076
  3599.0 8.3 copy-start.29
  3599.0 33.8 copy-start.1
  (42 other events, 143.5 us)
Sparse Core Ops, SparseCore 0:
  12.7 37.1 all-gather.6
  63.9 80.7 all-gather.10
  146.8 79.2 all-gather.8
  343.6 43.0 reduce-scatter.10
  655.7 248.5 all-gather.12
  966.8 234.1 reduce-scatter.18
  1871.1 248.3 all-gather.14
  2189.7 234.2 reduce-scatter.20
  2768.3 73.7 all-gather.16
  3097.7 76.7 reduce-scatter.12
  3177.3 77.2 reduce-scatter.14
  3273.6 44.9 reduce-scatter.16
  3324.1 274.8 all-reduce.9
  3601.2 30.1 all-reduce.7
where the time goes:
time: 3650 us; the launch traced here: 3640 us
  waiting for transfers between devices  1720 us (47%)
  blocking collectives  816 us (22%)
  matrix products  482 us (13%)
  local copies, waits for them, and re-layouts  327 us (9%)
  other arithmetic  255 us (7%)
    all_gather x2, waiting for transfers between devices, rows_over_dp(): return lax.all_gather(rows, 'dp', axis=0, tiled=True)  496 us
    unnamed x16, waiting for transfers between devices  469 us
    all_to_all x2, blocking collectives, to_experts(): lax.all_to_all(buffer, ('context', 'expert'), split_axis=1, concat_axis=0...  465 us
    psum x2, blocking collectives, per_device(): lax.psum((local_loss, jnp.sum(valid)), ('dp', 'context', 'expert'))  291 us
    all_to_all x2, waiting for transfers between devices, to_owners(): lax.all_to_all(buffer, ('context', 'expert'), split_axis=0, concat_axis=1...  182 us
    psum x1, waiting for transfers between devices, per_device(): lax.psum(joint_grad.astype(jnp.bfloat16), ('dp', 'context'))  151 us
    unnamed x178, local copies, waits for them, and re-layouts  133 us
    all_gather x2, waiting for transfers between devices, gather_tokens(): return lax.all_gather(rows, 'expert', axis=0, tiled=True)  105 us
  transfers between devices with their start and end apart: 16, of which 14 were waited for; matrix products, arithmetic and copies ran while one was open for 4% of the time, Pallas kernels for 0%

commit v1 on v0

v1 whole, which is shorter than its diff:
```python
import functools
import math

import jax
import jax.numpy as jnp
from jax import lax
from jax.experimental import pallas as pl
from jax.experimental.pallas import tpu as pltpu
from jax.sharding import PartitionSpec as P

HEADS = 16
HD = 128
TOPK = 8


EPSILON = 1e-05
ROPE_BASE = 10000.0
NEGATIVE = -1e30
LOG2E = math.log2(math.e)
SCORE_SCALE = HD ** (-0.5)
TOKEN_AXES = ("context", "expert")
ALL_AXES = ("dp", "context", "expert")
VMEM_LIMIT = 48 * 2**20


def rms_scale(values):
    return lax.rsqrt(jnp.mean(values * values, axis=-1, keepdims=True) + EPSILON)


def rope_tables(positions):
    exponent = jnp.arange(HD // 2, dtype=jnp.float32) * (2.0 / HD)
    angles = positions.astype(jnp.float32)[:, None] * (ROPE_BASE ** (-exponent))[None, :]
    return (jnp.cos(angles), jnp.sin(angles))


def rotate(values, cosine, sine_part):
    halfway = values.shape[-1] // 2
    leading = values[..., :halfway]
    trailing = values[..., halfway:]
    cos_wide = cosine[:, None, :]
    sin_wide = sine_part[:, None, :]
    return jnp.concatenate(
        [leading * cos_wide - trailing * sin_wide, trailing * cos_wide + leading * sin_wide],
        axis=-1,
    )


def rotate_back(gradient, cosine, sine_part):
    return rotate(gradient, cosine, -sine_part)


def silu_parts(gate_part):
    sigmoid = jax.nn.sigmoid(gate_part)
    return (gate_part * sigmoid, sigmoid * (1.0 + gate_part * (1.0 - sigmoid)))


def contract(left, right, left_dim, right_dim):
    return lax.dot_general(
        left,
        right,
        (((left_dim,), (right_dim,)), ((), ())),
        preferred_element_type=jnp.float32,
    )


def contract_rows(left, right):
    return contract(left, right, 0, 0)


def contract_last(left, right):
    return contract(left, right, 1, 1)


def low(values):
    return values.astype(jnp.bfloat16)


def gather_block(rows):
    return lax.all_gather(rows, "expert", axis=0, tiled=True)


def gather_sequence(rows):
    return lax.all_gather(rows, TOKEN_AXES, axis=0, tiled=True)


def scatter_sequence(rows):
    return lax.psum_scatter(low(rows), TOKEN_AXES, scatter_dimension=0, tiled=True).astype(
        jnp.float32
    )


def sum_low(values, axes):
    return lax.psum(low(values), axes).astype(jnp.float32)


def sum_half_over_dp(values, axis):
    size = lax.axis_size("dp")
    if size != 2:
        return lax.psum_scatter(low(values), "dp", scatter_dimension=axis, tiled=True).astype(
            jnp.float32
        )
    mine = lax.axis_index("dp")
    share = values.shape[axis] // 2
    sent = lax.dynamic_slice_in_dim(values, (1 - mine) * share, share, axis)
    kept = lax.dynamic_slice_in_dim(values, mine * share, share, axis)
    return kept + lax.ppermute(low(sent), "dp", ((0, 1), (1, 0))).astype(jnp.float32)


def flash_forward_kernel(length_ref, q_ref, k_ref, v_ref, out_ref, log_ref, *, block):
    row_block = pl.program_id(0)
    length = length_ref[0]
    queries = q_ref[...]

    def step(j, carry, masked):
        highest, total, acc = carry
        rows = pl.ds(pl.multiple_of(j * block, block), block)
        scores = contract_last(queries, k_ref[rows, :])
        if masked:
            query_pos = row_block * block + lax.broadcasted_iota(jnp.int32, (block, block), 0)
            key_pos = j * block + lax.broadcasted_iota(jnp.int32, (block, block), 1)
            allowed = (key_pos <= query_pos) & (key_pos < length)
            scores = jnp.where(allowed, scores, NEGATIVE)
        higher = jnp.maximum(highest, jnp.max(scores, axis=1, keepdims=True))
        weights = jnp.exp2(scores - higher)
        decay = jnp.exp2(highest - higher)
        total = total * decay + jnp.sum(weights, axis=1, keepdims=True)
        acc = acc * decay + contract(low(weights), v_ref[rows, :], 1, 0)
        return higher, total, acc

    start = (
        jnp.full((block, 1), NEGATIVE, jnp.float32),
        jnp.zeros((block, 1), jnp.float32),
        jnp.zeros((block, HD), jnp.float32),
    )
    full = jnp.minimum(row_block, length // block)
    end = jnp.minimum(row_block + 1, (length + block - 1) // block)
    carry = lax.fori_loop(0, full, lambda j, c: step(j, c, False), start)
    highest, total, acc = lax.fori_loop(full, end, lambda j, c: step(j, c, True), carry)
    out_ref[...] = low(acc / total)
    log_ref[...] = jnp.broadcast_to(highest + jnp.log2(total), (block, HD)).T[:8, :]


def flash_forward(queries, keys, values, length, block):
    rows = queries.shape[0]
    whole = pl.BlockSpec((rows, HD), lambda i, _: (0, 0))
    part = pl.BlockSpec((block, HD), lambda i, _: (i, 0))
    return pl.pallas_call(
        functools.partial(flash_forward_kernel, block=block),
        grid_spec=pltpu.PrefetchScalarGridSpec(
            num_scalar_prefetch=1,
            grid=(rows // block,),
            in_specs=[part, whole, whole],
            out_specs=[part, pl.BlockSpec((8, block), lambda i, _: (0, i))],
        ),
        out_shape=[
            jax.ShapeDtypeStruct((rows, HD), jnp.bfloat16),
            jax.ShapeDtypeStruct((8, rows), jnp.float32),
        ],
        compiler_params=pltpu.CompilerParams(vmem_limit_bytes=VMEM_LIMIT),
        cost_estimate=pl.CostEstimate(
            flops=8 * rows * rows * HD // 2,
            bytes_accessed=8 * rows * HD,
            transcendentals=rows * rows // 2,
        ),
    )(length, queries, keys, values)


def flash_backward_kernel(
    length_ref, q_ref, do_ref, log_ref, delta_ref, k_ref, v_ref, dq_ref, dk_ref, dv_ref, *, block
):
    key_block = pl.program_id(0)
    count = q_ref.shape[0] // block
    length = length_ref[0]

    @pl.when(key_block == 0)
    def _():
        dq_ref[...] = jnp.zeros_like(dq_ref)

    keys = k_ref[...]
    values = v_ref[...]

    def step(i, carry, masked):
        key_acc, value_acc = carry
        rows = pl.ds(pl.multiple_of(i * block, block), block)
        queries = q_ref[rows, :]
        grads = do_ref[rows, :]
        weights = jnp.exp2(contract_last(keys, queries) - log_ref[0:1, rows])
        if masked:
            query_pos = i * block + lax.broadcasted_iota(jnp.int32, (block, block), 1)
            key_pos = key_block * block + lax.broadcasted_iota(jnp.int32, (block, block), 0)
            allowed = (key_pos <= query_pos) & (key_pos < length)
            weights = jnp.where(allowed, weights, 0.0)
        grad_weights = contract_last(values, grads)
        grad_scores = low(weights * (grad_weights - delta_ref[0:1, rows]))
        value_acc = value_acc + contract(low(weights), grads, 1, 0)
        key_acc = key_acc + contract(grad_scores, queries, 1, 0)
        dq_ref[rows, :] += contract_rows(grad_scores, keys)
        return key_acc, value_acc

    zeros = jnp.zeros((block, HD), jnp.float32)
    beyond = key_block * block >= length
    ragged = (key_block + 1) * block > length
    start = jnp.where(beyond, count, key_block)
    masked_end = jnp.where(ragged, count, key_block + 1)
    carry = lax.fori_loop(start, masked_end, lambda i, c: step(i, c, True), (zeros, zeros))
    key_acc, value_acc = lax.fori_loop(
        masked_end, count, lambda i, c: step(i, c, False), carry
    )
    dk_ref[...] = key_acc * (1.0 / LOG2E)
    dv_ref[...] = value_acc

    @pl.when(key_block == count - 1)
    def _():
        dq_ref[...] = dq_ref[...] * SCORE_SCALE


def flash_backward(queries, keys, values, grads, logs, delta, length, block):
    rows = queries.shape[0]
    whole = pl.BlockSpec((rows, HD), lambda j, _: (0, 0))
    part = pl.BlockSpec((block, HD), lambda j, _: (j, 0))
    return pl.pallas_call(
        functools.partial(flash_backward_kernel, block=block),
        grid_spec=pltpu.PrefetchScalarGridSpec(
            num_scalar_prefetch=1,
            grid=(rows // block,),
            in_specs=[
                whole,
                whole,
                pl.BlockSpec((8, rows), lambda j, _: (0, 0)),
                pl.BlockSpec((1, rows), lambda j, _: (0, 0)),
                part,
                part,
            ],
            out_specs=[whole, part, part],
        ),
        out_shape=[jax.ShapeDtypeStruct((rows, HD), jnp.float32)] * 3,
        compiler_params=pltpu.CompilerParams(vmem_limit_bytes=VMEM_LIMIT),
        cost_estimate=pl.CostEstimate(
            flops=20 * rows * rows * HD // 2,
            bytes_accessed=20 * rows * HD,
            transcendentals=rows * rows // 2,
        ),
    )(length, queries, grads, logs, delta, keys, values)


class HeadAttention:
    def __init__(self, normed, length, weights, gains, output_weight):
        self.tok_rows = normed.shape[0]
        self.output_weight = output_weight
        self.length = length.reshape(1)
        head = lax.axis_index("context")

        def mine(array):
            return lax.dynamic_slice_in_dim(array, head * HD, HD, array.ndim - 1)

        self.weight = jnp.concatenate([mine(w) for w in weights], axis=1)
        self.query_gain, self.key_gain = (mine(g) for g in gains)
        self.normed = gather_sequence(normed)
        rows = self.normed.shape[0]
        self.block = math.gcd(1024, rows)
        self.tables = rope_tables(jnp.arange(rows, dtype=jnp.int32))
        projected = jnp.dot(self.normed, self.weight, preferred_element_type=jnp.float32)
        self.query_raw = projected[:, :HD]
        self.key_raw = projected[:, HD : 2 * HD]
        self.values = low(projected[:, 2 * HD :])
        totals = lax.psum(
            jnp.stack([jnp.sum(self.query_raw**2, axis=-1), jnp.sum(self.key_raw**2, axis=-1)]),
            TOKEN_AXES,
        )
        inverse = lax.rsqrt(totals / (HEADS * HD) + EPSILON)
        self.query_inv, self.key_inv = (inverse[0][:, None], inverse[1][:, None])
        turned = self.turn(self.query_raw * self.query_inv * self.query_gain, rotate)
        self.queries = low(turned * (SCORE_SCALE * LOG2E))
        self.keys = low(self.turn(self.key_raw * self.key_inv * self.key_gain, rotate))
        self.context, self.logs = flash_forward(
            self.queries, self.keys, self.values, self.length, self.block
        )
        self.context_block = self.to_block(self.context)

    def turn(self, values, how):
        return how(values[:, None, :], *self.tables)[:, 0, :]

    def to_block(self, rows):
        return lax.all_to_all(rows, "context", split_axis=0, concat_axis=1, tiled=True)

    def to_heads(self, rows):
        return lax.all_to_all(rows, "context", split_axis=1, concat_axis=0, tiled=True)

    def output(self):
        term = jnp.dot(
            self.context_block, self.output_weight, preferred_element_type=jnp.float32
        )
        return lax.psum_scatter(low(term), "expert", scatter_dimension=0, tiled=True).astype(
            jnp.float32
        )

    def backward(self, grad_attn):
        block_grad = gather_block(grad_attn)
        grad_context = self.to_heads(low(contract_last(block_grad, self.output_weight)))
        output_total = sum_low(
            contract_rows(self.context_block, block_grad), ("dp", "context")
        )
        delta = jnp.sum(
            grad_context.astype(jnp.float32) * self.context.astype(jnp.float32), axis=-1
        )[None]
        query_grad, key_grad, value_grad = flash_backward(
            self.queries,
            self.keys,
            self.values,
            grad_context,
            self.logs,
            delta,
            self.length,
            self.block,
        )
        grad_query_normed = self.turn(query_grad, rotate_back)
        grad_key_normed = self.turn(key_grad, rotate_back)
        gain_grads = jnp.concatenate(
            [
                jnp.sum(self.query_raw * self.query_inv * grad_query_normed, axis=0),
                jnp.sum(self.key_raw * self.key_inv * grad_key_normed, axis=0),
            ]
        )
        dots = lax.psum(
            jnp.stack(
                [
                    jnp.sum(self.query_raw * self.query_gain * grad_query_normed, axis=-1),
                    jnp.sum(self.key_raw * self.key_gain * grad_key_normed, axis=-1),
                ]
            ),
            TOKEN_AXES,
        ) / (HEADS * HD)
        grad_query = (
            self.query_inv * self.query_gain * grad_query_normed
            - self.query_raw * self.query_inv**3 * dots[0][:, None]
        )
        grad_key = (
            self.key_inv * self.key_gain * grad_key_normed
            - self.key_raw * self.key_inv**3 * dots[1][:, None]
        )
        grad_joint = low(jnp.concatenate([grad_query, grad_key, value_grad], axis=1))
        grad_normed = scatter_sequence(contract_last(grad_joint, self.weight))
        joint_grad = contract_rows(self.normed, grad_joint)
        joint_total = lax.all_gather(low(sum_low(joint_grad, "dp")), "context", axis=0)
        gains_total = lax.all_gather(lax.psum(gain_grads, "dp"), "context", axis=0)

        def spread(part):
            part = part.astype(jnp.float32)
            return jnp.moveaxis(part, 0, -2).reshape(part.shape[1:-1] + (-1,))

        return (
            grad_normed,
            *(spread(joint_total[..., i * HD : (i + 1) * HD]) for i in range(3)),
            *(spread(gains_total[..., i * HD : (i + 1) * HD]) for i in range(2)),
            output_total,
        )


class BlockAttention:
    def __init__(self, normed, length, weights, gains, output_weight):
        self.tok_rows = normed.shape[0]
        self.output_weight = output_weight
        self.length = length
        self.query_gain, self.key_gain = gains
        self.head_width = head_width = weights[0].shape[1]
        self.heads = head_width // HD
        self.weight = jnp.concatenate(weights, axis=1)
        self.normed = gather_block(normed)
        self.rows = rows = self.normed.shape[0]
        self.block_start = lax.axis_index("context") * rows
        projected = jnp.dot(self.normed, self.weight, preferred_element_type=jnp.float32)
        self.query_raw = projected[:, :head_width]
        self.key_raw = projected[:, head_width : 2 * head_width]
        value_raw = projected[:, 2 * head_width :]
        query_total, key_total = lax.psum(
            (jnp.sum(self.query_raw**2, axis=-1), jnp.sum(self.key_raw**2, axis=-1)), "expert"
        )
        self.query_inv = lax.rsqrt(query_total / (HEADS * HD) + EPSILON)[:, None]
        self.key_inv = lax.rsqrt(key_total / (HEADS * HD) + EPSILON)[:, None]
        self.tables = rope_tables(self.block_start + jnp.arange(rows, dtype=jnp.int32))
        query_rot = self.turn(self.query_raw * self.query_inv * self.query_gain, rotate)
        key_rot = self.turn(self.key_raw * self.key_inv * self.key_gain, rotate)
        self.keys, self.values = (
            lax.all_gather(low(key_rot), "context", axis=0, tiled=True),
            lax.all_gather(
                low(value_raw.reshape(rows, self.heads, HD)), "context", axis=0, tiled=True
            ),
        )
        self.query_block = min(512, rows)
        self.count = rows // self.query_block
        self.starts = jnp.arange(self.count, dtype=jnp.int32) * self.query_block
        self.queries = self.in_blocks(low(query_rot))

        def forward_block(packed):
            query_part, offset = packed
            masked, _ = self.scores_for(query_part, offset)
            highest = jnp.max(masked, axis=-1, keepdims=True)
            scores = jnp.exp(masked - highest)
            totals = jnp.sum(scores, axis=-1, keepdims=True)
            context = jnp.einsum(
                "hqk,khd->qhd",
                low(scores / totals),
                self.values,
                preferred_element_type=jnp.float32,
            )
            return (context, (highest + jnp.log(totals))[..., 0])

        context, self.logs = lax.map(forward_block, (self.queries, self.starts))
        self.context = low(context.reshape(rows, head_width))

    def turn(self, values, how):
        return how(values.reshape(self.rows, self.heads, HD), *self.tables)

    def in_blocks(self, values):
        return values.reshape(self.count, self.query_block, self.heads, HD)

    def scores_for(self, query_part, offset):
        raw_scores = (
            jnp.einsum("qhd,khd->hqk", query_part, self.keys, preferred_element_type=jnp.float32)
            * SCORE_SCALE
        )
        key_pos = jnp.arange(self.keys.shape[0], dtype=jnp.int32)
        query_pos = self.block_start + offset + jnp.arange(self.query_block, dtype=jnp.int32)
        allowed = (key_pos[None, :] <= query_pos[:, None]) & (key_pos[None, :] < self.length)
        return (jnp.where(allowed[None], raw_scores, NEGATIVE), allowed)

    def output(self):
        term = jnp.dot(self.context, self.output_weight, preferred_element_type=jnp.float32)
        return lax.psum_scatter(low(term), "expert", scatter_dimension=0, tiled=True).astype(
            jnp.float32
        )

    def backward(self, grad_attn):
        rows, heads = (self.rows, self.heads)
        block_grad = gather_block(grad_attn)
        output_total = sum_low(contract_rows(self.context, block_grad), ("dp", "context"))
        grad_blocks = self.in_blocks(low(contract_last(block_grad, self.output_weight)))

        def backward_block(running, packed):
            key_acc, value_acc = running
            query_part, grad_part, log_part, offset = packed
            masked, allowed = self.scores_for(query_part, offset)
            probs = jnp.where(allowed[None], jnp.exp(masked - log_part[..., None]), 0.0)
            grad_probs = jnp.einsum(
                "qhd,khd->hqk", grad_part, self.values, preferred_element_type=jnp.float32
            )
            row_dot = jnp.sum(probs * grad_probs, axis=-1, keepdims=True)
            grad_scores = low(probs * (grad_probs - row_dot))
            query_grad = (
                jnp.einsum(
                    "hqk,khd->qhd", grad_scores, self.keys, preferred_element_type=jnp.float32
                )
                * SCORE_SCALE
            )
            key_acc = (
                key_acc
                + jnp.einsum(
                    "hqk,qhd->khd", grad_scores, query_part, preferred_element_type=jnp.float32
                )
                * SCORE_SCALE
            )
            value_acc = value_acc + jnp.einsum(
                "hqk,qhd->khd", low(probs), grad_part, preferred_element_type=jnp.float32
            )
            return ((key_acc, value_acc), query_grad)

        zeros = jnp.zeros((self.keys.shape[0], heads, HD), jnp.float32)
        (key_acc, value_acc), query_grads = lax.scan(
            backward_block, (zeros, zeros), (self.queries, grad_blocks, self.logs, self.starts)
        )
        key_grad, value_grad = (
            lax.psum_scatter(low(acc), "context", scatter_dimension=0, tiled=True).astype(
                jnp.float32
            )
            for acc in (key_acc, value_acc)
        )
        grad_query_normed = self.turn(query_grads, rotate_back).reshape(rows, -1)
        grad_key_normed = self.turn(key_grad, rotate_back).reshape(rows, -1)
        query_dot, key_dot = lax.psum(
            (
                jnp.sum(self.query_raw * self.query_gain * grad_query_normed, axis=-1),
                jnp.sum(self.key_raw * self.key_gain * grad_key_normed, axis=-1),
            ),
            "expert",
        )
        grad_query = low(
            self.query_inv * self.query_gain * grad_query_normed
            - self.query_raw * self.query_inv**3 * (query_dot / (HEADS * HD))[:, None]
        )
        grad_key = low(
            self.key_inv * self.key_gain * grad_key_normed
            - self.key_raw * self.key_inv**3 * (key_dot / (HEADS * HD))[:, None]
        )
        grad_value = low(value_grad.reshape(rows, -1))
        grad_joint = jnp.concatenate([grad_query, grad_key, grad_value], axis=1)
        joint_total = sum_low(contract_rows(self.normed, grad_joint), ("dp", "context"))
        term = contract_last(grad_joint, self.weight)
        grad_normed = lax.psum_scatter(
            low(term), "expert", scatter_dimension=0, tiled=True
        ).astype(jnp.float32)
        gains_total = lax.psum(
            (
                jnp.sum(self.query_raw * self.query_inv * grad_query_normed, axis=0),
                jnp.sum(self.key_raw * self.key_inv * grad_key_normed, axis=0),
            ),
            ("dp", "context"),
        )
        return (grad_normed, *jnp.split(joint_total, 3, axis=1), *gains_total, output_total)


class Experts:
    def __init__(self, routes, capacity, gate_weight, up_weight, down_weight):
        tok_rows = routes.shape[0]
        expert = lax.axis_index("context") * lax.axis_size("expert") + lax.axis_index("expert")
        self.expert = expert
        everyone = lax.all_gather(routes.T, TOKEN_AXES, axis=0)
        member = jnp.any(everyone == expert, axis=1)
        token = jnp.arange(tok_rows, dtype=jnp.int32)
        before = low(token[:, None] < token[None, :])
        slots = jnp.dot(low(member), before, preferred_element_type=jnp.float32)
        slot_index = jnp.arange(capacity, dtype=jnp.int32)
        matches = slots.astype(jnp.int32)[:, None, :] == slot_index[None, :, None]
        self.picks = (matches & member[:, None, :]).astype(jnp.float32)
        self.pick = low(self.picks)
        gate_all, up_all = (
            lax.all_gather(w[0], "dp", axis=1, tiled=True) for w in (gate_weight, up_weight)
        )
        self.joint = jnp.concatenate([gate_all, up_all], axis=1)
        self.down = lax.all_gather(down_weight[0], "dp", axis=0, tiled=True)

    def rows_of(self, tokens):
        blocks = tokens.reshape(self.pick.shape[0], self.pick.shape[2], -1)
        rows = jnp.einsum("bst,btd->bsd", self.pick, blocks, preferred_element_type=jnp.float32)
        return rows.reshape(-1, blocks.shape[2])

    def tokens_of(self, pick, rows):
        blocks = low(rows).reshape(pick.shape[0], pick.shape[1], -1)
        tokens = jnp.einsum("bst,bsd->btd", pick, blocks, preferred_element_type=jnp.float32)
        return tokens.reshape(-1, blocks.shape[2])

    def forward(self, ffn_in, gates):
        everyone = lax.all_gather(gates.T, TOKEN_AXES, axis=0)
        gates_here = lax.dynamic_index_in_dim(everyone, self.expert, 1, keepdims=False)
        scaled_picks = self.picks * gates_here[:, None, :]
        self.row_gates = jnp.sum(scaled_picks, axis=-1).reshape(-1, 1)
        self.rows = low(self.rows_of(gather_sequence(ffn_in)))
        joint = low(jnp.dot(self.rows, self.joint, preferred_element_type=jnp.float32))
        self.gate_part, self.up_part = jnp.split(joint, 2, axis=1)
        silu_value, _ = silu_parts(self.gate_part.astype(jnp.float32))
        self.hidden = low(silu_value * self.up_part.astype(jnp.float32))
        self.out = low(jnp.dot(self.hidden, self.down, preferred_element_type=jnp.float32))
        return scatter_sequence(self.tokens_of(low(scaled_picks), self.out))

    def backward(self, grad_out):
        grads = self.rows_of(gather_sequence(low(grad_out)))
        gate_grads = jnp.sum(grads * self.out.astype(jnp.float32), axis=-1)
        tok_rows = self.picks.shape[2]
        gate_grads = jnp.sum(
            self.picks * gate_grads.reshape(self.picks.shape[:2])[:, :, None], axis=1
        )
        grad_gates = lax.all_to_all(
            gate_grads, TOKEN_AXES, split_axis=0, concat_axis=0, tiled=True
        ).T
        grad_rows_out = low(grads * self.row_gates)
        grad_hidden = contract_last(grad_rows_out, self.down)
        silu_value, silu_slope = silu_parts(self.gate_part.astype(jnp.float32))
        grad_joint = low(
            jnp.concatenate(
                [
                    grad_hidden * self.up_part.astype(jnp.float32) * silu_slope,
                    grad_hidden * silu_value,
                ],
                axis=1,
            )
        )
        grad_rows = contract_last(grad_joint, self.joint)
        grad_ffn = scatter_sequence(self.tokens_of(self.pick, grad_rows))
        joint_grad = contract_rows(self.rows, grad_joint)
        gate_grad, up_grad = jnp.split(joint_grad, 2, axis=1)
        down_grad = contract_rows(self.hidden, grad_rows_out)
        weight_grads = tuple(
            sum_half_over_dp(g, axis)[None]
            for g, axis in ((gate_grad, 1), (up_grad, 1), (down_grad, 0))
        )
        return grad_ffn, grad_gates, weight_grads


def per_device(
    block_input,
    teacher_states,
    seq_lengths,
    expert_routes,
    attn_gain,
    query_weight,
    key_weight,
    value_weight,
    query_gain,
    key_gain,
    output_weight,
    ffn_gain,
    router_weight,
    gate_weight,
    up_weight,
    down_weight,
):
    tok_rows = block_input.shape[0]
    experts_all = router_weight.shape[1]
    capacity = 5 * tok_rows * TOPK // (4 * experts_all)
    context_size = lax.axis_size("context")
    expert_size = lax.axis_size("expert")
    token_count_all = tok_rows * lax.axis_size("dp") * context_size * expert_size
    length = seq_lengths[0]
    own_start = (
        lax.axis_index("context") * expert_size + lax.axis_index("expert")
    ) * tok_rows
    tokens = block_input.astype(jnp.float32)
    inverse_one = rms_scale(tokens)
    normed = low(tokens * inverse_one * attn_gain)
    heads_here = query_weight.shape[1] // HD
    attention_kind = HeadAttention if heads_here == context_size else BlockAttention
    attention = attention_kind(
        normed,
        length,
        (query_weight, key_weight, value_weight),
        (query_gain, key_gain),
        output_weight,
    )
    experts = Experts(expert_routes, capacity, gate_weight, up_weight, down_weight)
    residual = tokens + attention.output()
    inverse_two = rms_scale(residual)
    ffn_in = low(residual * inverse_two * ffn_gain)
    logits = jnp.dot(ffn_in, router_weight, preferred_element_type=jnp.float32)
    weights_router = jnp.exp(logits - jnp.max(logits, axis=-1, keepdims=True))
    router_probs = weights_router / jnp.sum(weights_router, axis=-1, keepdims=True)
    expert_ids = jnp.arange(experts_all, dtype=jnp.int32)
    chosen = jnp.any(expert_routes[:, :, None] == expert_ids, axis=1)
    mixture = experts.forward(ffn_in, jnp.where(chosen, router_probs, 0.0))
    output_full = residual + mixture
    own_pos = own_start + jnp.arange(tok_rows, dtype=jnp.int32)
    valid = (own_pos < length).astype(jnp.float32)
    difference = output_full - teacher_states
    local_loss = jnp.sum(jnp.sum(difference * difference, axis=-1) * valid)
    count_total = lax.psum(length, "dp").astype(jnp.float32)
    grad_out = difference * (valid * (token_count_all / count_total))[:, None]
    grad_ffn_experts, grad_gates, expert_grads = experts.backward(grad_out)
    grad_router_probs = jnp.where(chosen, grad_gates, 0.0)
    grad_logits = router_probs * (
        grad_router_probs - jnp.sum(router_probs * grad_router_probs, axis=-1, keepdims=True)
    )
    router_grad = lax.dot_general(
        ffn_in.astype(jnp.float32),
        grad_logits,
        (((0,), (0,)), ((), ())),
        precision=lax.Precision.HIGHEST,
    )
    grad_ffn = grad_ffn_experts + lax.dot_general(
        grad_logits,
        router_weight.astype(jnp.float32),
        (((1,), (1,)), ((), ())),
        precision=lax.Precision.HIGHEST,
    )
    ffn_gain_grad = jnp.sum(residual * inverse_two * grad_ffn, axis=0)
    weighted_two = grad_ffn * ffn_gain
    grad_residual = (
        grad_out
        + inverse_two * weighted_two
        - residual * inverse_two**3 * jnp.mean(residual * weighted_two, axis=-1, keepdims=True)
    )
    (
        grad_normed,
        query_total,
        key_total,
        value_total,
        query_gain_total,
        key_gain_total,
        output_total,
    ) = attention.backward(low(grad_residual))
    attn_gain_grad = jnp.sum(tokens * inverse_one * grad_normed, axis=0)
    weighted_one = grad_normed * attn_gain
    input_grad = (
        grad_residual
        + inverse_one * weighted_one
        - tokens * inverse_one**3 * jnp.mean(tokens * weighted_one, axis=-1, keepdims=True)
    )
    loss_total, ffn_total, router_total = lax.psum(
        (local_loss, ffn_gain_grad, router_grad), ALL_AXES
    )
    attn_total = lax.psum(attn_gain_grad, ALL_AXES)
    return (
        low(output_full),
        loss_total / count_total,
        input_grad,
        attn_total,
        query_total,
        key_total,
        value_total,
        query_gain_total,
        key_gain_total,
        output_total,
        ffn_total,
        router_total,
        *expert_grads,
    )


def solution(mesh):
    rows = P(ALL_AXES, None)
    placed = (
        rows,
        rows,
        P("dp"),
        rows,
        P(),
        P(None, "expert"),
        P(None, "expert"),
        P(None, "expert"),
        P("expert"),
        P("expert"),
        P("expert", None),
        P(),
        P(),
        P(TOKEN_AXES, None, "dp"),
        P(TOKEN_AXES, None, "dp"),
        P(TOKEN_AXES, "dp", None),
    )
    return jax.shard_map(
        per_device,
        mesh=mesh,
        in_specs=placed,
        out_specs=(
            rows,
            P(),
            rows,
            P(),
            P(None, "expert"),
            P(None, "expert"),
            P(None, "expert"),
            P("expert"),
            P("expert"),
            P("expert", None),
            P(),
            P(),
            P(TOKEN_AXES, None, "dp"),
            P(TOKEN_AXES, None, "dp"),
            P(TOKEN_AXES, "dp", None),
        ),
        check_vma=False,
    )
```

time: 3650 us -> 2080 us (0.57)
  blocking collectives: 816 us -> 253 us
  waiting for transfers between devices: 1720 us -> 1290 us
  local copies, waits for them, and re-layouts: 327 us -> 69.4 us
  matrix products: 482 us -> 261 us
  other arithmetic: 255 us -> 119 us
  Pallas kernels: 0 us -> 60.3 us
    unnamed x16 -> x15, waiting for transfers between devices: 469 us -> 1.78 us
    all_to_all x2, blocking collectives: 465 us -> 34.6 us  [the longest x1 25.1 us: to_block(): lax.all_to_all(rows, 'context', split_axis=0, concat_axis=1, tiled=True)]
    reduce_scatter x4, waiting for transfers between devices: 172 us -> 524 us  [the longest x3 481 us: scatter_sequence(): lax.psum_scatter(low(rows), TOKEN_AXES, scatter_dimension=0, tiled=True)]
    dot_general x29 -> x17, matrix products: 474 us -> 252 us  [the longest x8 135 us: contract(): lax.dot_general(left, right, (((left_dim,), (right_dim,)), ((), ())), pre...]
    all_gather x6 -> x8, waiting for transfers between devices: 729 us -> 516 us  [the longest x3 333 us: gather_sequence(): return lax.all_gather(rows, TOKEN_AXES, axis=0, tiled=True)]
    psum x6 -> x5, blocking collectives: 351 us -> 166 us  [the longest x1 58.9 us: __init__(): lax.psum(jnp.stack([jnp.sum(self.query_raw ** 2, axis=-1), jnp.sum(self.k...]
    all_to_all x2 -> x1, waiting for transfers between devices: 182 us -> 26.1 us  [to_heads(): lax.all_to_all(rows, 'context', split_axis=1, concat_axis=0, tiled=True)]
    gather x2 -> x0, local copies, waits for them, and re-layouts: 102 us -> none  [the longest x1 50.9 us: per_device(): grad_back[flat_slots, flat_experts].astype(jnp.float32)]
  transfers between devices with their start and end apart: 16 -> 19, of which waited for: 14 -> 18; matrix products, arithmetic and copies ran while one was open for 4% -> 9% of each run, Pallas kernels for 0% -> 0%
where the time goes in v1:
time: 2080 us
  waiting for transfers between devices  1290 us (62%)
  matrix products  261 us (13%)
  blocking collectives  253 us (12%)
  other arithmetic  119 us (6%)
  local copies, waits for them, and re-layouts  69.4 us (3%)
  Pallas kernels  60.3 us (3%)
    reduce_scatter x3, waiting for transfers between devices, scatter_sequence(): lax.psum_scatter(low(rows), TOKEN_AXES, scatter_dimension=0, tiled=True)  481 us
    all_gather x3, waiting for transfers between devices, gather_sequence(): return lax.all_gather(rows, TOKEN_AXES, axis=0, tiled=True)  333 us
    dot_general x8, matrix products, contract(): lax.dot_general(left, right, (((left_dim,), (right_dim,)), ((), ())), pre...  135 us
    all_gather x2, waiting for transfers between devices, __init__(): lax.all_gather(w[0], 'dp', axis=1, tiled=True)  102 us
    ppermute x3, waiting for transfers between devices, sum_half_over_dp(): lax.ppermute(low(sent), 'dp', ((0, 1), (1, 0))).astype(jnp.float32)  95.6 us
    psum x1, waiting for transfers between devices, per_device(): lax.psum((local_loss, ffn_gain_grad, router_grad), ALL_AXES)  81.5 us
    psum x1, blocking collectives, __init__(): lax.psum(jnp.stack([jnp.sum(self.query_raw ** 2, axis=-1), jnp.sum(self.k...  58.9 us
    psum x1, blocking collectives, backward(): lax.psum(jnp.stack([jnp.sum(self.query_raw * self.query_gain * grad_query...  57.9 us
  transfers between devices with their start and end apart: 19, of which 18 were waited for; matrix products, arithmetic and copies ran while one was open for 9% of the time, Pallas kernels for 0%

profile of v1, /device:TPU:0, one launch (start us, length us, event | category | flops | bytes accessed | tf_op | source)
XLA Modules:
  0.0 2076.0 jit_solution(3070589110568713993)
XLA Ops:
  18.0 124.3 %all-gather.15.cloned.1.call-done = bf16[4096,2048]{1,0:T(8,128)(2,1)} async-done(((bf16[256,2048]{1,0:T(8,128)(2,1)}), bf16[4096,2048]{1,0:T(8,128)(2,1)}) %all-gather.15.cloned.1.call-update) | async-done | bytes 16777232 | tf_op jit(solution)/shard_map/all_gather | solution.py:83
  142.3 12.2 fusion.67
  158.2 58.9 %psum.70 = f32[2,4096]{1,0:T(2,128)S(1)} all-reduce(f32[2,4096]{1,0:T(2,128)S(1)} %pad_maximum_fusion.12), channel_id=1, replica_groups=mesh['dp'=2,'context'=4,'expert'=4] {'context','expert'}, use_global_device_ids=true, to_apply=%region_3.0 | all-reduce | flops 8192 | bytes 65536 | tf_op jit(solution)/shard_map/psum | solution.py:266
  217.3 4.1 multiply_bitcast_fusion
  221.4 9.2 fusion.46
  232.8 22.9 %shard_map.271 = (bf16[4096,128]{1,0:T(8,128)(2,1)S(1)}, f32[8,4096]{1,0:T(8,128)S(1)}) custom-call(s32[1]{0:T(128)} %copy.94.length_ref, bf16[4096,128]{1,0:T(8,128)(2,1)S(1)} %fusion.66.q_ref, bf16[4096,128]{1,0:T(8,128)(2,1)S(1)} %maximum_bitcast_fusion.2.k_ref, bf16[4096,128]{1,0:T(8,128)(2,1)S(1)} %copy-done.8), custom_call_target="tpu_custom_call" | custom-call | flops 8589934592 | bytes 4194304 | tf_op jit(solution)/shard_map/pallas_call | solution.py:147
  257.1 25.1 %all_to_all.50 = bf16[4,1024,128]{1,2,0:T(8,128)(2,1)S(1)} all-to-all(bf16[4,1024,128]{1,2,0:T(8,128)(2,1)} %copy.63), channel_id=1, replica_groups=mesh['dp'=2,'context'=4,'expert'=4] {'context'}, dimensions={0} | all-to-all | bytes 2097152 | tf_op jit(solution)/shard_map/all_to_all | solution.py:284
  283.2 4.4 convolution_convert_fusion.7
  287.9 43.5 %reduce-scatter.5.cloned.1.call-done = bf16[256,2048]{1,0:T(8,128)(2,1)} async-done(((bf16[1024,2048]{1,0:T(8,128)(2,1)}), bf16[256,2048]{1,0:T(8,128)(2,1)}) %reduce-scatter.5.cloned.1.call-update) | async-done | bytes 1048592 | tf_op jit(solution)/shard_map/reduce_scatter | solution.py:293
  337.7 21.4 %all-gather = s32[128,256]{1,0:T(8,128)S(1)} all-gather(s32[8,256]{1,0:T(8,128)S(1)} %bitcast.178), channel_id=2, replica_groups=mesh['dp'=2,'context'=4,'expert'=4] {'context','expert'}, dimensions={0}, use_global_device_ids=true | all-gather | bytes 139264 | tf_op jit(solution)/shard_map/all_gather | solution.py:516
  361.6 19.7 all-gather.1
  381.3 83.2 %all-gather.17.cloned.1.call-done = bf16[4096,2048]{1,0:T(8,128)(2,1)} async-done(((bf16[256,2048]{1,0:T(8,128)(2,1)}), bf16[4096,2048]{1,0:T(8,128)(2,1)}) %all-gather.17.cloned.1.call-update) | async-done | bytes 16777232 | tf_op jit(solution)/shard_map/all_gather | solution.py:83
  464.5 13.1 convolution_convert_fusion.6
  477.5 43.4 %all-gather.25.cloned.1.call-done = bf16[1,2048,1024]{2,1,0:T(8,128)(2,1)} async-done(((bf16[1,2048,512]{2,1,0:T(8,128)(2,1)}), bf16[1,2048,1024]{2,1,0:T(8,128)(2,1)}) %all-gather.25.cloned.1.call-update) | async-done | bytes 4194320 | tf_op jit(solution)/shard_map/all_gather | solution.py:526
  520.9 58.2 %all-gather.27.cloned.1.call-done = bf16[1,2048,1024]{2,1,0:T(8,128)(2,1)} async-done(((bf16[1,2048,512]{2,1,0:T(8,128)(2,1)}), bf16[1,2048,1024]{2,1,0:T(8,128)(2,1)}) %all-gather.27.cloned.1.call-update) | async-done | bytes 4194320 | tf_op jit(solution)/shard_map/all_gather | solution.py:526
  579.1 29.4 %convolution_convert_fusion.4 = bf16[2560,2048]{0,1:T(8,128)(2,1)} fusion(bf16[2560,2048]{1,0:T(8,128)(2,1)} %bitcast.150, bf16[2048,1024]{1,0:T(8,128)(2,1)} %bitcast.184, bf16[2048,1024]{1,0:T(8,128)(2,1)} %bitcast.182), kind=kOutput, calls=%fused_computation.13 | convolution fusion | flops 21496856576 | bytes 29360128 | tf_op jit(solution)/shard_map/dot_general | solution.py:547
  608.5 28.9 %all-gather.29.cloned.1.call-done = bf16[1,1024,2048]{2,1,0:T(8,128)(2,1)} async-done(((bf16[1,512,2048]{2,1,0:T(8,128)(2,1)}), bf16[1,1024,2048]{2,1,0:T(8,128)(2,1)}) %all-gather.29.cloned.1.call-update) | async-done | bytes 4194320 | tf_op jit(solution)/shard_map/all_gather | solution.py:529
  637.4 18.2 convolution_convert_fusion.5
  655.6 12.5 convolution_convert_fusion.2
  668.2 4.9 psum.72
  673.8 173.1 %reduce-scatter.7.cloned.1.call-done = bf16[256,2048]{1,0:T(8,128)(2,1)} async-done(((bf16[4096,2048]{1,0:T(8,128)(2,1)}), bf16[256,2048]{1,0:T(8,128)(2,1)}) %reduce-scatter.7.cloned.1.call-update) | async-done | bytes 1048592 | tf_op jit(solution)/shard_map/reduce_scatter | solution.py:87
  850.8 126.0 %all-gather.19.cloned.1.call-done = bf16[4096,2048]{1,0:T(8,128)(2,1)} async-done(((bf16[256,2048]{1,0:T(8,128)(2,1)}), bf16[4096,2048]{1,0:T(8,128)(2,1)}) %all-gather.19.cloned.1.call-update) | async-done | bytes 16777232 | tf_op jit(solution)/shard_map/all_gather | solution.py:83
  976.8 15.7 fusion.53
  992.5 10.9 fusion.1
  1005.2 12.8 fusion
  1018.0 21.8 %fusion.4 = (bf16[2560,1024]{0,1:T(8,128)(2,1)}, bf16[2560,1024]{0,1:T(8,128)(2,1)}) fusion(bf16[2560,2048]{0,1:T(8,128)(2,1)} %convolution_convert_fusion.4, bf16[2560,2048]{1,0:T(8,128)(2,1)} %fusion, bf16[1,1024,2048]{2,1,0:T(8,128)(2,1)S(1)} %copy-done.78), kind=kOutput, calls=%fused_computation.17 | convolution fusion | flops 10776739840 | bytes 35651584 | tf_op jit(solution)/shard_map/dot_general | solution.py:58
  1039.8 28.5 %convolution_convert_fusion.3 = bf16[2560,2048]{1,0:T(8,128)(2,1)} fusion(bf16[2560,1024]{0,1:T(8,128)(2,1)} %get-tuple-element.91, bf16[2560,1024]{0,1:T(8,128)(2,1)} %get-tuple-element.90, bf16[2048,1024]{1,0:T(8,128)(2,1)} %bitcast.185, bf16[2048,1024]{1,0:T(8,128)(2,1)} %bitcast.183), kind=kOutput, calls=%fused_computation.12 | convolution fusion | flops 21517828096 | bytes 29360128 | tf_op jit(solution)/shard_map/dot_general | solution.py:58
  1068.3 12.1 convolution_convert_fusion.1
  1080.6 9.5 all_to_all.51
  1090.1 167.3 %reduce-scatter.9.cloned.1.call-done = bf16[256,2048]{1,0:T(8,128)(2,1)} async-done(((bf16[4096,2048]{1,0:T(8,128)(2,1)}), bf16[256,2048]{1,0:T(8,128)(2,1)}) %reduce-scatter.9.cloned.1.call-update) | async-done | bytes 1048592 | tf_op jit(solution)/shard_map/reduce_scatter | solution.py:87
  1257.4 5.4 multiply_reduce_fusion
  1266.0 33.6 %all-gather.21.cloned.1.call-done = bf16[1024,2048]{1,0:T(8,128)(2,1)} async-done(((bf16[256,2048]{1,0:T(8,128)(2,1)}), bf16[1024,2048]{1,0:T(8,128)(2,1)}) %all-gather.21.cloned.1.call-update) | async-done | bytes 4194320 | tf_op jit(solution)/shard_map/all_gather | solution.py:79
  1299.6 5.5 convolution_convert_fusion.10
  1307.5 4.7 all-to-all-start.2
  1312.3 26.1 %all-to-all-done.2 = bf16[1024,4,128]{2,0,1:T(8,128)(2,1)S(1)} async-done(((bf16[1024,4,128]{2,0,1:T(8,128)(2,1)}), bf16[1024,4,128]{2,0,1:T(8,128)(2,1)S(1)}, u32[]{:S(2)}, u32[]{:S(2)}) %all-to-all-start.2) | async-done | bytes 1048608 | tf_op jit(solution)/shard_map/all_to_all | solution.py:287
  1339.9 37.4 %shard_map.272 = (f32[4096,128]{1,0:T(8,128)}, f32[4096,128]{1,0:T(8,128)}, f32[4096,128]{1,0:T(8,128)}) custom-call(s32[1]{0:T(128)} %copy.94.length_ref, bf16[4096,128]{1,0:T(8,128)(2,1)S(1)} %copy-done.7, bf16[4096,128]{1,0:T(8,128)(2,1)S(1)} %bitcast.139, f32[8,4096]{1,0:T(8,128)S(1)} %get-tuple-element.21.log_ref, f32[1,4096]{1,0:T(1,128)S(1)} %bitcast.140, ...), custom_call_target="tpu_custom_call" | custom-call | flops 21474836480 | bytes 10485760 | tf_op jit(solution)/shard_map/pallas_call | solution.py:221
  1377.4 11.4 fusion.41
  1388.9 4.2 multiply_reduce_fusion.2
  1393.1 57.9 %psum.73 = f32[2,4096]{1,0:T(2,128)S(1)} all-reduce(f32[2,4096]{1,0:T(2,128)S(1)} %pad_maximum_fusion.13), channel_id=1, replica_groups=mesh['dp'=2,'context'=4,'expert'=4] {'context','expert'}, use_global_device_ids=true, to_apply=%region_24.25 | all-reduce | flops 8192 | bytes 65536 | tf_op jit(solution)/shard_map/psum | solution.py:324
  1453.3 9.4 subtract_convert_fusion.1
  1464.0 13.5 fusion.32
  1477.5 6.4 convolution_convert_fusion.8
  1484.0 41.0 %all-reduce.5.cloned.1.call-done = bf16[1,2048,384]{2,1,0:T(8,128)(2,1)} async-done(((bf16[1,2048,384]{2,1,0:T(8,128)(2,1)}), bf16[1,2048,384]{2,1,0:T(8,128)(2,1)}) %all-reduce.5.cloned.1.call-update) | async-done | bytes 1572880 | tf_op jit(solution)/shard_map/psum | solution.py:93
  1525.1 13.1 convolution_convert_fusion
  1538.3 18.0 fusion.84
  1561.5 27.9 %fusion.10 = f32[2048,2048]{1,0:T(8,128)} fusion(bf16[2560,2048]{1,0:T(8,128)(2,1)} %bitcast.151, bf16[2560,1024]{0,1:T(8,128)(2,1)} %get-tuple-element.91, bf16[2560,1024]{0,1:T(8,128)(2,1)S(1)} %bitcast.187), kind=kOutput, calls=%fused_computation.26 | convolution fusion | flops 21495808000 | bytes 37748736 | tf_op jit(solution)/shard_map/dot_general | solution.py:58
  1589.3 7.2 fusion.88
  1606.8 13.8 collective-permute-done.2
  1620.6 5.9 add_bitcast_fusion
  1626.5 43.5 %collective-permute-done.1 = bf16[2048,512]{1,0:T(8,128)(2,1)} collective-permute-done((bf16[2048,512]{1,0:T(8,128)(2,1)}, bf16[2048,512]{1,0:T(8,128)(2,1)}, u32[]{:S(2)}, u32[]{:S(2)}) %collective-permute-start.1) | collective-permute-done | bytes 2097184 | tf_op jit(solution)/shard_map/ppermute | solution.py:106
  1670.0 5.5 add_bitcast_fusion.1
  1675.5 38.3 %collective-permute-done = bf16[2048,512]{1,0:T(8,128)(2,1)} collective-permute-done((bf16[2048,512]{1,0:T(8,128)(2,1)}, bf16[2048,512]{1,0:T(8,128)(2,1)}, u32[]{:S(2)}, u32[]{:S(2)}) %collective-permute-start) | collective-permute-done | bytes 2097184 | tf_op jit(solution)/shard_map/ppermute | solution.py:106
  1713.8 4.4 add_bitcast_fusion.2
  1718.9 4.9 psum.76
  1723.8 11.1 all-gather.5
  1735.5 4.1 convert_element_type.229
  1739.6 18.6 all-gather.23.cloned.1.call-done
  1758.3 5.7 fusion.89
  1769.9 5.9 copy.68
  1781.7 5.9 copy.69
  1793.1 5.4 copy.70
  1798.6 140.5 %reduce-scatter.11.cloned.1.call-done = bf16[256,2048]{1,0:T(8,128)(2,1)} async-done(((bf16[4096,2048]{1,0:T(8,128)(2,1)}), bf16[256,2048]{1,0:T(8,128)(2,1)}) %reduce-scatter.11.cloned.1.call-update) | async-done | bytes 1048592 | tf_op jit(solution)/shard_map/reduce_scatter | solution.py:87
  1944.8 39.6 %all-reduce = (f32[]{:T(128)}, f32[2048]{0:T(1024)}, f32[2048]{0:T(1024)}) all-reduce(f32[]{:T(128)} %select_reduce_fusion.2, f32[2048]{0:T(1024)S(1)} %get-tuple-element.81, f32[2048]{0:T(1024)S(1)} %copy-done.57), channel_id=1, replica_groups=mesh['dp'=2,'context'=4,'expert'=4] {'dp','context','expert'}, use_global_device_ids=true, to_apply=%region_13.14 | all-reduce | flops 4097 | bytes 32776 | tf_op jit(solution)/shard_map/psum | solution.py:685
  1985.1 81.5 %all-reduce.9.cloned.1.call-done = f32[2048,16]{0,1:T(8,128)} async-done(((f32[2048,16]{0,1:T(8,128)}), f32[2048,16]{0,1:T(8,128)}) %all-reduce.9.cloned.1.call-update) | async-done | bytes 131088 | tf_op jit(solution)/shard_map/psum | solution.py:685
  (270 shorter events, 85.4 us)
Async XLA Ops:
  7.2 276.0 %copy-start = (bf16[512,2048]{1,0:T(8,128)(2,1)S(1)}, bf16[512,2048]{1,0:T(8,128)(2,1)}, u32[]{:S(2)}) copy-start(bf16[512,2048]{1,0:T(8,128)(2,1)} %param.26) | copy-start | bytes 6291460
  7.2 135.1 %all-gather.15.cloned.1.call-start = ((), (), s32[]{:S(2)}) async-start(), calls=%async_computation.7 | async-start | bytes 17825792 | tf_op jit(solution)/shard_map/all_gather | solution.py:83
  12.5 318.9 %reduce-scatter.5.cloned.1.call-start = ((), (), s32[]{:S(2)}) async-start(), calls=%async_computation.8 | async-start | bytes 5242880 | tf_op jit(solution)/shard_map/reduce_scatter | solution.py:293
  13.3 203.9 %copy-start.67 = (f32[128]{0:T(128)}, f32[128]{0:T(128)S(1)}, u32[]{:S(2)}) copy-start(f32[128]{0:T(128)S(1)} %dynamic_slice.40) | copy-start | bytes 1540
  14.1 203.2 %copy-start.69 = (f32[128]{0:T(128)}, f32[128]{0:T(128)S(1)}, u32[]{:S(2)}) copy-start(f32[128]{0:T(128)S(1)} %dynamic_slice.41) | copy-start | bytes 1540
  14.8 206.6 %copy-start.74 = (f32[64]{0:T(128)}, f32[64]{0:T(128)S(1)}, u32[]{:S(2)}) copy-start(f32[64]{0:T(128)S(1)} %negate_power_fusion) | copy-start | bytes 772
  14.8 206.6 %copy-start.45 = (f32[4096]{0:T(1024)}, f32[4096]{0:T(1024)S(1)}, u32[]{:S(2)}) copy-start(f32[4096]{0:T(1024)S(1)} %iota_convert_fusion) | copy-start | bytes 49156
  18.0 136.5 %copy-start.35 = (bf16[2048,128]{1,0:T(8,128)(2,1)}, bf16[2048,128]{1,0:T(8,128)(2,1)S(1)}, u32[]{:S(2)}) copy-start(bf16[2048,128]{1,0:T(8,128)(2,1)S(1)} %get-tuple-element.127) | copy-start | bytes 1572868
  18.0 136.5 %copy-start.36 = (bf16[2048,128]{1,0:T(8,128)(2,1)}, bf16[2048,128]{1,0:T(8,128)(2,1)S(1)}, u32[]{:S(2)}) copy-start(bf16[2048,128]{1,0:T(8,128)(2,1)S(1)} %get-tuple-element.128) | copy-start | bytes 1572868
  232.8 22.9 %copy-start.6 = (bf16[4096,128]{1,0:T(8,128)(2,1)}, bf16[4096,128]{1,0:T(8,128)(2,1)S(1)}, u32[]{:S(2)}) copy-start(bf16[4096,128]{1,0:T(8,128)(2,1)S(1)} %fusion.66.q_ref) | copy-start | bytes 3145732
  255.7 26.5 %copy-start.2 = (bf16[4096,128]{1,0:T(8,128)(2,1)}, bf16[4096,128]{1,0:T(8,128)(2,1)S(1)}, u32[]{:S(2)}) copy-start(bf16[4096,128]{1,0:T(8,128)(2,1)S(1)} %get-tuple-element.20) | copy-start | bytes 3145732
  287.6 43.8 %copy-start.10 = (bf16[256,2048]{1,0:T(8,128)(2,1)S(1)}, bf16[256,2048]{1,0:T(8,128)(2,1)}, u32[]{:S(2)}) copy-start(bf16[256,2048]{1,0:T(8,128)(2,1)} %param.16) | copy-start | bytes 3145732
  287.6 46.6 %copy-start.51 = (f32[2048]{0:T(1024)S(1)}, f32[2048]{0:T(1024)}, u32[]{:S(2)}) copy-start(f32[2048]{0:T(1024)} %param.27) | copy-start | bytes 24580
  287.7 176.8 %all-gather.17.cloned.1.call-start = ((), (), s32[]{:S(2)}) async-start(), calls=%async_computation.9 | async-start | bytes 17825792 | tf_op jit(solution)/shard_map/all_gather | solution.py:83
  335.8 185.1 %all-gather.25.cloned.1.call-start = ((), (), s32[]{:S(2)}) async-start(), calls=%async_computation.19 | async-start | bytes 6291456 | tf_op jit(solution)/shard_map/all_gather | solution.py:526
  336.4 22.9 %copy-start.41 = (bf16[2048,16]{0,1:T(8,128)(2,1)S(1)}, bf16[2048,16]{0,1:T(8,128)(2,1)}, u32[]{:S(2)}) copy-start(bf16[2048,16]{0,1:T(8,128)(2,1)} %param.28) | copy-start | bytes 196612
  336.4 242.8 %all-gather.27.cloned.1.call-start = ((), (), s32[]{:S(2)}) async-start(), calls=%async_computation.20 | async-start | bytes 6291456 | tf_op jit(solution)/shard_map/all_gather | solution.py:526
  337.0 300.4 %all-gather.29.cloned.1.call-start = ((), (), s32[]{:S(2)}) async-start(), calls=%async_computation.21 | async-start | bytes 6291456 | tf_op jit(solution)/shard_map/all_gather | solution.py:529
  337.6 509.4 %reduce-scatter.7.cloned.1.call-start = ((), (), s32[]{:S(2)}) async-start(), calls=%async_computation.10 | async-start | bytes 17825792 | tf_op jit(solution)/shard_map/reduce_scatter | solution.py:87
  337.6 139.9 %copy-start.47 = (pred[256,16]{0,1:T(8,128)(4,1)}, pred[256,16]{0,1:T(8,128)(4,1)S(1)}, u32[]{:S(2)}) copy-start(pred[256,16]{0,1:T(8,128)(4,1)S(1)} %fusion.68) | copy-start | bytes 12292
  361.6 19.7 copy-start.58
  668.1 308.7 %all-gather.19.cloned.1.call-start = ((), (), s32[]{:S(2)}) async-start(), calls=%async_computation.11 | async-start | bytes 17825792 | tf_op jit(solution)/shard_map/all_gather | solution.py:83
  850.8 406.6 %reduce-scatter.9.cloned.1.call-start = ((), (), s32[]{:S(2)}) async-start(), calls=%async_computation.12 | async-start | bytes 17825792 | tf_op jit(solution)/shard_map/reduce_scatter | solution.py:87
  1005.2 12.8 copy-start.78
  1080.5 9.6 copy-start.59
  1080.5 176.9 %copy-start.42 = (bf16[2048,16]{0,1:T(8,128)(2,1)S(1)}, bf16[2048,16]{0,1:T(8,128)(2,1)}, u32[]{:S(2)}) copy-start(bf16[2048,16]{0,1:T(8,128)(2,1)} %param.28) | copy-start | bytes 196612
  1080.5 176.9 %copy-start.52 = (f32[2048]{0:T(1024)S(1)}, f32[2048]{0:T(1024)}, u32[]{:S(2)}) copy-start(f32[2048]{0:T(1024)} %param.27) | copy-start | bytes 24580
  1080.5 176.9 %copy-start.64 = (f32[256]{0:T(256)S(1)}, f32[256]{0:T(256)}, u32[]{:S(2)}) copy-start(f32[256]{0:T(256)} %copy-done.63) | copy-start | bytes 3076
  1080.5 219.1 %all-gather.21.cloned.1.call-start = ((), (), s32[]{:S(2)}) async-start(), calls=%async_computation.13 | async-start | bytes 5242880 | tf_op jit(solution)/shard_map/all_gather | solution.py:79
  1090.1 172.7 %copy-start.43 = (f32[16,1,256]{2,1,0:T(1,128)}, f32[16,1,256]{2,1,0:T(1,128)S(1)}, u32[]{:S(2)}) copy-start(f32[16,1,256]{2,1,0:T(1,128)S(1)} %all_to_all.51) | copy-start | bytes 49156
  1090.1 172.7 %copy-start.65 = (f32[256]{0:T(256)}, f32[256]{0:T(256)S(1)}, u32[]{:S(2)}) copy-start(f32[256]{0:T(256)S(1)} %multiply_reduce_fusion.11) | copy-start | bytes 3076
  1090.1 172.7 %copy-start.72 = (f32[256]{0:T(256)S(1)}, f32[256]{0:T(256)}, u32[]{:S(2)}) copy-start(f32[256]{0:T(256)} %get-tuple-element.122) | copy-start | bytes 3076
  1305.1 33.2 %copy-start.3 = (bf16[4096,128]{1,0:T(8,128)(2,1)S(1)}, bf16[4096,128]{1,0:T(8,128)(2,1)}, u32[]{:S(2)}) copy-start(bf16[4096,128]{1,0:T(8,128)(2,1)} %copy-done.2) | copy-start | bytes 3145732
  1307.5 31.5 %copy-start.5 = (bf16[4096,128]{1,0:T(8,128)(2,1)S(1)}, bf16[4096,128]{1,0:T(8,128)(2,1)}, u32[]{:S(2)}) copy-start(bf16[4096,128]{1,0:T(8,128)(2,1)} %copy-done.4) | copy-start | bytes 3145732
  1307.5 30.9 %all-to-all-start.2 = ((bf16[1024,4,128]{2,0,1:T(8,128)(2,1)}), bf16[1024,4,128]{2,0,1:T(8,128)(2,1)S(1)}, u32[]{:S(2)}, u32[]{:S(2)}) async-start(bf16[1024,4,128]{2,0,1:T(8,128)(2,1)} %copy.64), calls=%async_computation.5 | async-start | bytes 2097152 | tf_op jit(solution)/shard_map/all_to_all | solution.py:287
  1312.2 212.8 %all-reduce.5.cloned.1.call-start = ((), (), s32[]{:S(2)}) async-start(), calls=%async_computation.15 | async-start | bytes 3145728 | tf_op jit(solution)/shard_map/psum | solution.py:93
  1339.9 37.4 %copy-start.46 = (f32[4096]{0:T(1024)S(1)}, f32[4096]{0:T(1024)}, u32[]{:S(2)}) copy-start(f32[4096]{0:T(1024)} %copy-done.45) | copy-start | bytes 49156
  1339.9 37.4 %copy-start.75 = (f32[64]{0:T(128)S(1)}, f32[64]{0:T(128)}, u32[]{:S(2)}) copy-start(f32[64]{0:T(128)} %copy-done.74) | copy-start | bytes 772
  1377.3 11.5 slice-start
  1377.3 11.5 slice-start.1
  1377.3 11.5 copy-start.68
  1377.4 11.5 copy-start.70
  1464.0 13.6 copy-start.27
  1477.5 258.0 %all-reduce.7.cloned.1.call-start = ((), (), s32[]{:S(2)}) async-start(), calls=%async_computation.17 | async-start | bytes 4194304 | tf_op jit(solution)/shard_map/psum | solution.py:93
  1483.9 41.1 %copy-start.29 = (bf16[4096,128]{1,0:T(8,128)(2,1)S(1)}, bf16[4096,128]{1,0:T(8,128)(2,1)}, u32[]{:S(2)}) copy-start(bf16[4096,128]{1,0:T(8,128)(2,1)} %copy-done.28) | copy-start | bytes 3145732
  1483.9 41.2 %copy-start.31 = (bf16[4096,128]{1,0:T(8,128)(2,1)S(1)}, bf16[4096,128]{1,0:T(8,128)(2,1)}, u32[]{:S(2)}) copy-start(bf16[4096,128]{1,0:T(8,128)(2,1)} %copy-done.30) | copy-start | bytes 3145732
  1483.9 274.3 %all-gather.23.cloned.1.call-start = ((), (), s32[]{:S(2)}) async-start(), calls=%async_computation.16 | async-start | bytes 7864320 | tf_op jit(solution)/shard_map/all_gather | solution.py:344
  1525.0 414.0 %reduce-scatter.11.cloned.1.call-start = ((), (), s32[]{:S(2)}) async-start(), calls=%async_computation.14 | async-start | bytes 17825792 | tf_op jit(solution)/shard_map/reduce_scatter | solution.py:87
  1538.2 23.2 %slice-start.4 = ((s8[5242880]{0:T(1024)(128)(4,1)}), s8[1048576]{0:T(1024)(128)(4,1)S(1)}, s32[]{:S(2)}) async-start(s8[5242880]{0:T(1024)(128)(4,1)} %bitcast.186), calls=%async_computation.26 | async-start | bytes 2097152
  1538.3 528.3 %all-reduce.9.cloned.1.call-start = ((), (), s32[]{:S(2)}) async-start(), calls=%async_computation.18 | async-start | bytes 262144 | tf_op jit(solution)/shard_map/psum | solution.py:685
  1538.3 23.2 %slice-start.5 = ((s8[5242880]{0:T(1024)(128)(4,1)}), s8[4194304]{0:T(1024)(128)(4,1)S(1)}, s32[]{:S(2)}) async-start(s8[5242880]{0:T(1024)(128)(4,1)} %bitcast.186), calls=%async_computation.27 | async-start | bytes 8388608
  1561.2 59.4 %collective-permute-start.2 = (bf16[512,2048]{1,0:T(8,128)(2,1)}, bf16[512,2048]{1,0:T(8,128)(2,1)}, u32[]{:S(2)}, u32[]{:S(2)}) collective-permute-start(bf16[512,2048]{1,0:T(8,128)(2,1)} %dynamic-slice_convert_fusion), channel_id=1, source_target_pairs={{0,16},{16,0},{1,17},{17,1},{2,18},{18,2},{3,19},{19,3},{4,20},{20... | collective-permute-start | bytes 6291464 | tf_op jit(solution)/shard_map/ppermute | solution.py:106
  1598.5 71.5 %collective-permute-start.1 = (bf16[2048,512]{1,0:T(8,128)(2,1)}, bf16[2048,512]{1,0:T(8,128)(2,1)}, u32[]{:S(2)}, u32[]{:S(2)}) collective-permute-start(bf16[2048,512]{1,0:T(8,128)(2,1)} %dynamic-slice_convert_fusion.1), channel_id=1, source_target_pairs={{0,16},{16,0},{1,17},{17,1},{2,18},{18,2},{3,19},{19,3},{4,20},{20... | collective-permute-start | bytes 6291464 | tf_op jit(solution)/shard_map/ppermute | solution.py:106
  1603.8 110.0 %collective-permute-start = (bf16[2048,512]{1,0:T(8,128)(2,1)}, bf16[2048,512]{1,0:T(8,128)(2,1)}, u32[]{:S(2)}, u32[]{:S(2)}) collective-permute-start(bf16[2048,512]{1,0:T(8,128)(2,1)} %dynamic-slice_convert_fusion.2), channel_id=1, source_target_pairs={{0,16},{16,0},{1,17},{17,1},{2,18},{18,2},{3,19},{19,3},{4,20},{20... | collective-permute-start | bytes 6291464 | tf_op jit(solution)/shard_map/ppermute | solution.py:106
  1620.6 93.1 %slice-start.2 = ((s8[8388608]{0:T(1024)(128)(4,1)}), s8[4194304]{0:T(1024)(128)(4,1)S(1)}, s32[]{:S(2)}) async-start(s8[8388608]{0:T(1024)(128)(4,1)} %bitcast.148), calls=%async_computation.24 | async-start | bytes 8388608
  1626.5 87.3 %slice-start.3 = ((s8[8388608]{0:T(1024)(128)(4,1)}), s8[4194304]{0:T(1024)(128)(4,1)S(1)}, s32[]{:S(2)}) async-start(s8[8388608]{0:T(1024)(128)(4,1)} %bitcast.148), calls=%async_computation.25 | async-start | bytes 8388608
  1675.5 42.7 %copy-start.73 = (f32[256]{0:T(256)S(1)}, f32[256]{0:T(256)}, u32[]{:S(2)}) copy-start(f32[256]{0:T(256)} %get-tuple-element.80) | copy-start | bytes 3076
  1675.5 43.4 %copy-start.76 = (f32[128]{0:T(128)S(1)}, f32[128]{0:T(128)}, u32[]{:S(2)}) copy-start(f32[128]{0:T(128)} %get-tuple-element.70) | copy-start | bytes 1540
  1675.5 43.4 %copy-start.77 = (f32[128]{0:T(128)S(1)}, f32[128]{0:T(128)}, u32[]{:S(2)}) copy-start(f32[128]{0:T(128)} %get-tuple-element.75) | copy-start | bytes 1540
  1793.1 145.9 %copy-start.11 = (bf16[256,2048]{1,0:T(8,128)(2,1)S(1)}, bf16[256,2048]{1,0:T(8,128)(2,1)}, u32[]{:S(2)}) copy-start(bf16[256,2048]{1,0:T(8,128)(2,1)} %param.16) | copy-start | bytes 3145732
  1793.1 145.9 %copy-start.50 = (f32[2048]{0:T(1024)S(1)}, f32[2048]{0:T(1024)}, u32[]{:S(2)}) copy-start(f32[2048]{0:T(1024)} %param.20) | copy-start | bytes 24580
  1793.1 145.9 %copy-start.62 = (f32[256]{0:T(256)S(1)}, f32[256]{0:T(256)}, u32[]{:S(2)}) copy-start(f32[256]{0:T(256)} %copy-done.61) | copy-start | bytes 3076
  1798.6 142.9 %copy-start.71 = (f32[256]{0:T(256)S(1)}, f32[256]{0:T(256)}, u32[]{:S(2)}) copy-start(f32[256]{0:T(256)} %get-tuple-element.120) | copy-start | bytes 3076
  1941.5 126.6 %copy-start.1 = (bf16[512,2048]{1,0:T(8,128)(2,1)S(1)}, bf16[512,2048]{1,0:T(8,128)(2,1)}, u32[]{:S(2)}) copy-start(bf16[512,2048]{1,0:T(8,128)(2,1)} %param.26) | copy-start | bytes 6291460
  (40 other events, 156.5 us)
Sparse Core Ops, SparseCore 0:
  12.6 129.5 all-gather.14
  287.8 43.5 reduce-scatter.4
  335.9 128.5 all-gather.16
  465.9 54.9 all-gather.24
  522.4 56.7 all-gather.26
  580.6 56.7 all-gather.28
  668.3 178.6 reduce-scatter.6
  850.9 125.8 all-gather.18
  1080.6 176.7 reduce-scatter.8
  1266.1 33.4 all-gather.20
  1477.6 47.3 all-reduce.4
  1529.0 113.4 all-reduce.6
  1644.1 114.0 all-gather.22
  1762.2 176.7 reduce-scatter.10
  1945.0 121.4 all-reduce.8

commit v2 on v1

--- a/solution.py
+++ b/solution.py
@@ -20,7 +20,7 @@
 SCORE_SCALE = HD ** (-0.5)
 TOKEN_AXES = ("context", "expert")
 ALL_AXES = ("dp", "context", "expert")
-VMEM_LIMIT = 48 * 2**20
+VMEM_LIMIT = 56 * 2**20
 
 
 def rms_scale(values):
@@ -75,38 +75,373 @@
     return values.astype(jnp.bfloat16)
 
 
+def steps_back(axis, size, stride=1):
+    group = size * stride
+    total = lax.axis_size(axis)
+    return tuple(
+        (i, i // group * group + (i + stride) % group) for i in range(total)
+    )
+
+
+def moved(values, axis, pairs):
+    return jax.tree.map(lambda v: lax.ppermute(v, axis, pairs), values)
+
+
+def next_on(axis, values):
+    return moved(values, axis, steps_back(axis, lax.axis_size(axis)))
+
+
+def next_chip(values):
+    return moved(values, "expert", steps_back("expert", chips_of_expert(), 2))
+
+
+def partner(values):
+    pairs = tuple((i, i ^ 1) for i in range(lax.axis_size("expert")))
+    return moved(values, "expert", pairs)
+
+
+def chips_of_expert():
+    return lax.axis_size("expert") // 2
+
+
+def together(*values):
+    return lax.optimization_barrier(values)
+
+
+def place_of(z, e):
+    return z, e // 2, e % 2
+
+
+def relative_to_absolute():
+    ring, chips = (lax.axis_size("context"), chips_of_expert())
+    z, x, c = place_of(lax.axis_index("context"), lax.axis_index("expert"))
+    r = jnp.arange(ring * chips * 2, dtype=jnp.int32)
+    s, dc, dx = (r // (2 * chips), r // chips % 2, r % chips)
+    return ((z + ring - s) % ring * chips + (x + chips - dx) % chips) * 2 + (c + dc) % 2
+
+
+def absolute_to_relative():
+    ring, chips = (lax.axis_size("context"), chips_of_expert())
+    z, x, c = place_of(lax.axis_index("context"), lax.axis_index("expert"))
+    b = jnp.arange(ring * chips * 2, dtype=jnp.int32)
+    bz, bx, bc = (b // (2 * chips), b // 2 % chips, b % 2)
+    return ((z + ring - bz) % ring * 2 + (c + bc) % 2) * chips + (x + chips - bx) % chips
+
+
+def reorder(blocks, order):
+    count = blocks.shape[0]
+    onehot = (order[:, None] == jnp.arange(count, dtype=jnp.int32)[None, :]).astype(jnp.float32)
+    moved = lax.dot_general(
+        onehot,
+        blocks.reshape(count, -1),
+        (((1,), (0,)), ((), ())),
+        precision=lax.Precision.HIGHEST,
+    )
+    return moved.reshape(blocks.shape)
+
+
+def gather_expert(rows):
+    parts = [rows]
+    for _ in range(chips_of_expert() - 1):
+        parts.append(next_chip(parts[-1]))
+    return parts + [partner(p) for p in parts]
+
+
+def gather_chunks(rows, work, beside=(), slack=0):
+    ring = lax.axis_size("context")
+    results, done = ([], [])
+    for s in range(ring):
+        following = next_on("context", rows) if s < ring - 1 else rows
+        parts = [rows]
+        for _ in range(chips_of_expert() - 1):
+            parts.append(next_chip(parts[-1]))
+        extra = beside[s] if s < len(beside) else ()
+        due = s - 1 - slack
+        result = results[due] if due >= 0 else None
+        following, parts[-1], result, extra = together(following, parts[-1], result, extra)
+        if due >= 0:
+            results[due] = result
+        done.append(extra)
+        results.append(work(s, parts + [partner(p) for p in parts]))
+        rows = following
+    return results, done
+
+
+def scatter_expert(kept, sent, waiting=None, beside=()):
+    terms = kept.astype(jnp.float32) + partner(low(sent)).astype(jnp.float32)
+    running = low(terms[1])
+    running, waiting, beside = together(running, waiting, beside)
+    if waiting is not None:
+        waiting = next_on("context", waiting)
+    for d in range(2, terms.shape[0]):
+        running = low(terms[d] + next_chip(running).astype(jnp.float32))
+    total = terms[0] + next_chip(running).astype(jnp.float32)
+    if waiting is not None:
+        total = total + waiting.astype(jnp.float32)
+    return total, beside
+
+
+def scatter_chunks(term, works):
+    ring = lax.axis_size("context")
+    total, result = (None, ())
+    for i, s in enumerate((*range(1, ring), 0)):
+        arrays, work = works[i]
+        kept, sent = term(s)
+        waiting = None if total is None else low(total)
+        total, (result, arrays) = scatter_expert(kept, sent, waiting, (result, arrays))
+        result = work(result, *arrays)
+    return total, result
+
+
+def ring_sum_begin(parts, axis):
+    running = parts[1]
+    for part in parts[2:]:
+        running = part + next_on(axis, low(running)).astype(jnp.float32)
+    return parts[0], next_on(axis, low(running))
+
+
+def ring_sum(parts, axis):
+    kept, received = ring_sum_begin(parts, axis)
+    return kept + received.astype(jnp.float32)
+
+
+def ring_parts(values, axis, dim):
+    size, me = (lax.axis_size(axis), lax.axis_index(axis))
+    share = values.shape[dim] // size
+    return [
+        lax.dynamic_slice_in_dim(values, ((me - d) % size) * share, share, dim)
+        for d in range(size)
+    ]
+
+
+def ring_gather(values, axis):
+    parts = [values]
+    for _ in range(lax.axis_size(axis) - 1):
+        parts.append(next_on(axis, parts[-1]))
+    return parts
+
+
+def small_sum(values, axes):
+    for axis in axes:
+        size = lax.axis_size(axis)
+        parts = [values] + [
+            lax.ppermute(values, axis, tuple((i, i ^ bits) for i in range(size)))
+            for bits in range(1, size)
+        ]
+        while len(parts) > 1:
+            parts = [left + right for left, right in zip(parts[::2], parts[1::2])]
+        values = parts[0]
+    return values
+
+
 def gather_block(rows):
     return lax.all_gather(rows, "expert", axis=0, tiled=True)
 
 
-def gather_sequence(rows):
-    return lax.all_gather(rows, TOKEN_AXES, axis=0, tiled=True)
-
-
-def scatter_sequence(rows):
-    return lax.psum_scatter(low(rows), TOKEN_AXES, scatter_dimension=0, tiled=True).astype(
-        jnp.float32
-    )
-
-
 def sum_low(values, axes):
     return lax.psum(low(values), axes).astype(jnp.float32)
 
 
-def sum_half_over_dp(values, axis):
-    size = lax.axis_size("dp")
-    if size != 2:
-        return lax.psum_scatter(low(values), "dp", scatter_dimension=axis, tiled=True).astype(
-            jnp.float32
-        )
-    mine = lax.axis_index("dp")
-    share = values.shape[axis] // 2
-    sent = lax.dynamic_slice_in_dim(values, (1 - mine) * share, share, axis)
-    kept = lax.dynamic_slice_in_dim(values, mine * share, share, axis)
-    return kept + lax.ppermute(low(sent), "dp", ((0, 1), (1, 0))).astype(jnp.float32)
-
-
-def flash_forward_kernel(length_ref, q_ref, k_ref, v_ref, out_ref, log_ref, *, block):
+def as_row(column):
+    return jnp.broadcast_to(column, (column.shape[0], HD)).T[0:1, :]
+
+
+def project_kernel(places_ref, *refs, count):
+    blocks, weight_ref = (refs[:count], refs[count])
+    raw_ref, copy_ref, square_ref, member_ref = refs[-4:]
+    width = weight_ref.shape[0]
+    for i, block_ref in enumerate(blocks):
+
+        @pl.when(pl.program_id(0) == i)
+        def _(block_ref=block_ref):
+            rows = block_ref[:, :width]
+            raw = contract(rows, weight_ref[...], 1, 0)
+            raw_ref[...] = raw
+            copy_ref[...] = rows
+            for j in range(2):
+                part = raw[:, j * HD : (j + 1) * HD]
+                square_ref[j : j + 1, :] = as_row(jnp.sum(part * part, axis=1, keepdims=True))
+            chosen = block_ref[:, width:].astype(jnp.float32)
+            lane = lax.broadcasted_iota(jnp.int32, chosen.shape, 1)
+            here = lane == places_ref[count]
+            member = jnp.sum(jnp.where(here, chosen, 0.0), axis=1, keepdims=True)
+            member_ref[0] = as_row(member)
+
+
+def project_chunk(blocks, weight, places, before, total_rows):
+    count = len(blocks)
+    tok_rows = blocks[0].shape[0]
+    width, columns = weight.shape
+    whole = fixed_spec(*blocks[0].shape)
+    outs = [
+        (
+            (total_rows, columns),
+            jnp.float32,
+            pl.BlockSpec((tok_rows, columns), lambda i, places: (places[i], 0)),
+        ),
+        (
+            (total_rows, width),
+            jnp.bfloat16,
+            pl.BlockSpec((tok_rows, width), lambda i, places: (places[i], 0)),
+        ),
+        (
+            (2, total_rows),
+            jnp.float32,
+            pl.BlockSpec((2, tok_rows), lambda i, places: (0, places[i])),
+        ),
+        (
+            (count, 1, tok_rows),
+            jnp.float32,
+            pl.BlockSpec((1, 1, tok_rows), lambda i, places: (i, 0, 0)),
+        ),
+    ]
+    return chunk_call(
+        functools.partial(project_kernel, count=count),
+        (*blocks, weight),
+        [whole] * count + [fixed_spec(width, columns)],
+        outs,
+        dict(enumerate(before)),
+        [],
+        count,
+        pl.CostEstimate(
+            flops=2 * count * tok_rows * width * columns,
+            bytes_accessed=4 * count * tok_rows * width + 2 * width * columns,
+            transcendentals=0,
+        ),
+        (places,),
+    )
+
+
+def inverse_norms(totals):
+    return lax.rsqrt(totals * (1.0 / (HEADS * HD)) + EPSILON).T
+
+
+def turn_kernel(raw_ref, total_ref, gain_ref, cos_ref, sin_ref, q_ref, k_ref, v_ref):
+    inverse = inverse_norms(total_ref[...])
+    cosine, sine_part = (cos_ref[...], sin_ref[...])
+    for i, (out_ref, factor) in enumerate(((q_ref, SCORE_SCALE * LOG2E), (k_ref, 1.0))):
+        values = raw_ref[:, i * HD : (i + 1) * HD] * inverse[:, i : i + 1] * gain_ref[i : i + 1, :]
+        turned = values * cosine + pltpu.roll(values, HD // 2, 1) * sine_part
+        out_ref[...] = low(turned * factor)
+    v_ref[...] = low(raw_ref[:, 2 * HD :])
+
+
+def turned_back(grad, cosine, sine_part):
+    return grad * cosine - pltpu.roll(grad, HD // 2, 1) * sine_part
+
+
+def turn_grad_kernel(
+    raw_ref, total_ref, gain_ref, cos_ref, sin_ref, dq_ref, dk_ref, dots_ref, gains_ref
+):
+    @pl.when(pl.program_id(0) == 0)
+    def _():
+        gains_ref[...] = jnp.zeros_like(gains_ref)
+
+    inverse = inverse_norms(total_ref[...])
+    for i, grad_ref in enumerate((dq_ref, dk_ref)):
+        back = turned_back(grad_ref[...], cos_ref[...], sin_ref[...])
+        scaled = raw_ref[:, i * HD : (i + 1) * HD] * back
+        dots = jnp.sum(scaled * gain_ref[i : i + 1, :], axis=1, keepdims=True)
+        dots_ref[i : i + 1, :] = as_row(dots)
+        gains_ref[i : i + 1, :] += jnp.sum(scaled * inverse[:, i : i + 1], axis=0, keepdims=True)
+
+
+def norm_grad_kernel(
+    places_ref,
+    raw_ref,
+    total_ref,
+    gain_ref,
+    cos_ref,
+    sin_ref,
+    dq_ref,
+    dk_ref,
+    dv_ref,
+    dots_ref,
+    out_ref,
+    relative_ref,
+    *,
+    share,
+):
+    inverse = inverse_norms(total_ref[...])
+    dots = dots_ref[...].T
+    for i, grad_ref in enumerate((dq_ref, dk_ref)):
+        back = turned_back(grad_ref[...], cos_ref[...], sin_ref[...])
+        raw = raw_ref[:, i * HD : (i + 1) * HD]
+        inv = inverse[:, i : i + 1]
+        shared = inv * inv * inv * dots[:, i : i + 1] * (1.0 / (HEADS * HD))
+        out_ref[:, i * HD : (i + 1) * HD] = low(
+            back * gain_ref[i : i + 1, :] * inv - raw * shared
+        )
+    out_ref[:, 2 * HD :] = low(dv_ref[...])
+    spread_relative(places_ref, out_ref, relative_ref, share)
+
+
+def spread_relative(places_ref, from_ref, to_ref, share):
+    ring = places_ref.shape[0] - share
+    rows = from_ref.shape[0] // share
+    for b in range(share):
+        place = pl.multiple_of(places_ref[ring + b] * rows, rows)
+        to_ref[pl.ds(place, rows), :] = from_ref[b * rows : (b + 1) * rows, :]
+
+
+def context_grad_kernel(places_ref, grad_ref, context_ref, out_ref, delta_ref, *, share):
+    ring = places_ref.shape[0] - share
+    rows = out_ref.shape[0] // share
+    for b in range(share):
+        place = pl.multiple_of(places_ref[ring + b] * rows, rows)
+        here = pl.ds(b * rows, rows)
+        grads = grad_ref[pl.ds(place, rows), :]
+        out_ref[here, :] = grads
+        product = grads.astype(jnp.float32) * context_ref[here, :].astype(jnp.float32)
+        delta_ref[0:1, here] = as_row(jnp.sum(product, axis=1, keepdims=True))
+
+
+def sequence_places():
+    ring, chips = (lax.axis_size("context"), chips_of_expert())
+    z, x, c = place_of(lax.axis_index("context"), lax.axis_index("expert"))
+    distances = (z + ring - jnp.arange(ring, dtype=jnp.int32)) % ring
+    b = jnp.arange(2 * chips, dtype=jnp.int32)
+    places = (c + b % 2) % 2 * chips + (x + chips - b // 2) % chips
+    return jnp.concatenate([distances, places])
+
+
+def block_call(kernel, arrays, in_specs, out_specs, out_shape, count, places=None):
+    prefetch = [] if places is None else [places]
+    return pl.pallas_call(
+        kernel,
+        grid_spec=pltpu.PrefetchScalarGridSpec(
+            num_scalar_prefetch=len(prefetch),
+            grid=(count,),
+            in_specs=in_specs,
+            out_specs=out_specs,
+        ),
+        out_shape=out_shape,
+        compiler_params=pltpu.CompilerParams(vmem_limit_bytes=VMEM_LIMIT),
+        cost_estimate=pl.CostEstimate(
+            flops=2**22, bytes_accessed=2**23, transcendentals=0
+        ),
+    )(*prefetch, *arrays)
+
+
+def rows_spec(rows, width):
+    return pl.BlockSpec((rows, width), lambda b, *_: (b, 0))
+
+
+def distance_spec(rows, width):
+    return pl.BlockSpec((rows, width), lambda b, places: (places[b], 0))
+
+
+def scalars_spec(rows, count=8):
+    return pl.BlockSpec((count, rows), lambda b, *_: (0, b))
+
+
+def fixed_spec(*shape):
+    return pl.BlockSpec(shape, lambda *_: (0,) * len(shape))
+
+
+def flash_forward_kernel(
+    length_ref, places_ref, q_ref, k_ref, v_ref, out_ref, log_ref, relative_ref, *, block, share
+):
     row_block = pl.program_id(0)
     length = length_ref[0]
     queries = q_ref[...]
@@ -138,23 +473,29 @@
     highest, total, acc = lax.fori_loop(full, end, lambda j, c: step(j, c, True), carry)
     out_ref[...] = low(acc / total)
     log_ref[...] = jnp.broadcast_to(highest + jnp.log2(total), (block, HD)).T[:8, :]
-
-
-def flash_forward(queries, keys, values, length, block):
+    spread_relative(places_ref, out_ref, relative_ref, share)
+
+
+def flash_forward(queries, keys, values, length, places, block, share):
     rows = queries.shape[0]
-    whole = pl.BlockSpec((rows, HD), lambda i, _: (0, 0))
-    part = pl.BlockSpec((block, HD), lambda i, _: (i, 0))
+    whole = pl.BlockSpec((rows, HD), lambda i, *_: (0, 0))
+    part = pl.BlockSpec((block, HD), lambda i, *_: (i, 0))
     return pl.pallas_call(
-        functools.partial(flash_forward_kernel, block=block),
+        functools.partial(flash_forward_kernel, block=block, share=share),
         grid_spec=pltpu.PrefetchScalarGridSpec(
-            num_scalar_prefetch=1,
+            num_scalar_prefetch=2,
             grid=(rows // block,),
             in_specs=[part, whole, whole],
-            out_specs=[part, pl.BlockSpec((8, block), lambda i, _: (0, i))],
+            out_specs=[
+                part,
+                pl.BlockSpec((8, block), lambda i, *_: (0, i)),
+                pl.BlockSpec((block, HD), lambda i, _, places: (places[i], 0)),
+            ],
         ),
         out_shape=[
             jax.ShapeDtypeStruct((rows, HD), jnp.bfloat16),
             jax.ShapeDtypeStruct((8, rows), jnp.float32),
+            jax.ShapeDtypeStruct((rows, HD), jnp.bfloat16),
         ],
         compiler_params=pltpu.CompilerParams(vmem_limit_bytes=VMEM_LIMIT),
         cost_estimate=pl.CostEstimate(
@@ -162,7 +503,7 @@
             bytes_accessed=8 * rows * HD,
             transcendentals=rows * rows // 2,
         ),
-    )(length, queries, keys, values)
+    )(length, places, queries, keys, values)
 
 
 def flash_backward_kernel(
@@ -227,7 +568,7 @@
                 whole,
                 whole,
                 pl.BlockSpec((8, rows), lambda j, _: (0, 0)),
-                pl.BlockSpec((1, rows), lambda j, _: (0, 0)),
+                pl.BlockSpec((8, rows), lambda j, _: (0, 0)),
                 part,
                 part,
             ],
@@ -243,10 +584,22 @@
     )(length, queries, grads, logs, delta, keys, values)
 
 
+def finish(pending):
+    return [(kept + received.astype(jnp.float32))[None] for kept, received in pending]
+
+
+def permute_by(axis, values, distance):
+    size = lax.axis_size(axis)
+    return lax.ppermute(values, axis, tuple((i, (i + distance) % size) for i in range(size)))
+
+
 class HeadAttention:
-    def __init__(self, normed, length, weights, gains, output_weight):
-        self.tok_rows = normed.shape[0]
-        self.output_weight = output_weight
+    def __init__(self, normed, length, weights, gains, output_weight, experts, count):
+        self.ring = ring = lax.axis_size("context")
+        self.share = share = 2 * chips_of_expert()
+        self.tok_rows = tok_rows = normed.shape[0]
+        self.block = block = share * tok_rows
+        self.rows = rows = ring * block
         self.length = length.reshape(1)
         head = lax.axis_index("context")
 
@@ -254,55 +607,111 @@
             return lax.dynamic_slice_in_dim(array, head * HD, HD, array.ndim - 1)
 
         self.weight = jnp.concatenate([mine(w) for w in weights], axis=1)
-        self.query_gain, self.key_gain = (mine(g) for g in gains)
-        self.normed = gather_sequence(normed)
-        rows = self.normed.shape[0]
-        self.block = math.gcd(1024, rows)
-        self.tables = rope_tables(jnp.arange(rows, dtype=jnp.int32))
-        projected = jnp.dot(self.normed, self.weight, preferred_element_type=jnp.float32)
-        self.query_raw = projected[:, :HD]
-        self.key_raw = projected[:, HD : 2 * HD]
-        self.values = low(projected[:, 2 * HD :])
-        totals = lax.psum(
-            jnp.stack([jnp.sum(self.query_raw**2, axis=-1), jnp.sum(self.key_raw**2, axis=-1)]),
-            TOKEN_AXES,
-        )
-        inverse = lax.rsqrt(totals / (HEADS * HD) + EPSILON)
-        self.query_inv, self.key_inv = (inverse[0][:, None], inverse[1][:, None])
-        turned = self.turn(self.query_raw * self.query_inv * self.query_gain, rotate)
-        self.queries = low(turned * (SCORE_SCALE * LOG2E))
-        self.keys = low(self.turn(self.key_raw * self.key_inv * self.key_gain, rotate))
-        self.context, self.logs = flash_forward(
-            self.queries, self.keys, self.values, self.length, self.block
-        )
-        self.context_block = self.to_block(self.context)
-
-    def turn(self, values, how):
-        return how(values[:, None, :], *self.tables)[:, 0, :]
-
-    def to_block(self, rows):
-        return lax.all_to_all(rows, "context", split_axis=0, concat_axis=1, tiled=True)
-
-    def to_heads(self, rows):
-        return lax.all_to_all(rows, "context", split_axis=1, concat_axis=0, tiled=True)
+        self.gains = jnp.pad(jnp.stack([mine(g) for g in gains]), ((0, 6), (0, 0)))
+        self.output_weight = jnp.concatenate(
+            [
+                lax.dynamic_slice_in_dim(output_weight, (head + d) % ring * HD, HD, 0)
+                for d in range(ring)
+            ]
+        )
+        self.places = sequence_places()
+        absolute = relative_to_absolute()
+        cosine, sine_part = rope_tables(jnp.arange(rows, dtype=jnp.int32))
+        tables = (
+            jnp.concatenate([cosine, cosine], axis=1),
+            jnp.concatenate([-sine_part, sine_part], axis=1),
+        )
+        made = [()]
+
+        def project(s, blocks):
+            places = absolute[s * share : (s + 1) * share]
+            places = jnp.concatenate([places, experts.expert.reshape(1).astype(jnp.int32)])
+            results = project_chunk(blocks, self.weight, places, made[0], rows)
+            made[0] = results[:3]
+            experts.pick(results[3][:, 0, :])
+            return results[3]
+
+        gates, ups, downs = experts.weights
+        _, done = gather_chunks(
+            jnp.concatenate([normed, experts.chosen], axis=1),
+            project,
+            [(), (tables, gates), (), ups],
+            1,
+        )
+        tables, gates = done[1]
+        self.count_total = count
+        self.raw, self.normed, squares = made[0]
+        squares, downs = together(squares, downs)
+        experts.weights = (gates, done[3], downs)
+        totals = small_sum(squares, TOKEN_AXES)
+        self.common = (self.raw, totals, self.gains, *tables)
+        self.common_specs = [
+            rows_spec(block, 3 * HD),
+            scalars_spec(block, 2),
+            fixed_spec(8, HD),
+            rows_spec(block, HD),
+            rows_spec(block, HD),
+        ]
+        self.queries, self.keys, self.values = block_call(
+            turn_kernel,
+            self.common,
+            self.common_specs,
+            [rows_spec(block, HD)] * 3,
+            [jax.ShapeDtypeStruct((rows, HD), jnp.bfloat16)] * 3,
+            ring,
+        )
+        self.context, self.logs, pieces = flash_forward(
+            self.queries, self.keys, self.values, self.length, self.places, block, share
+        )
+        pieces = jnp.split(pieces, ring)
+        self.context_block = jnp.concatenate(
+            [pieces[0]] + [permute_by("context", pieces[d], -d) for d in range(1, ring)], axis=1
+        )
 
     def output(self):
-        term = jnp.dot(
-            self.context_block, self.output_weight, preferred_element_type=jnp.float32
-        )
-        return lax.psum_scatter(low(term), "expert", scatter_dimension=0, tiled=True).astype(
-            jnp.float32
-        )
-
-    def backward(self, grad_attn):
-        block_grad = gather_block(grad_attn)
-        grad_context = self.to_heads(low(contract_last(block_grad, self.output_weight)))
-        output_total = sum_low(
-            contract_rows(self.context_block, block_grad), ("dp", "context")
-        )
-        delta = jnp.sum(
-            grad_context.astype(jnp.float32) * self.context.astype(jnp.float32), axis=-1
-        )[None]
+        shape = (self.share // 2, self.tok_rows, self.output_weight.shape[1])
+        half = self.block // 2
+        kept, sent = (
+            contract(part, self.output_weight, 1, 0).reshape(shape)
+            for part in (self.context_block[:half], self.context_block[half:])
+        )
+        return scatter_expert(kept, sent)[0]
+
+    def backward(self, grad_attn, sums, pending):
+        tok_rows, ring, block, rows = (self.tok_rows, self.ring, self.block, self.rows)
+        block_grad = gather_expert(grad_attn)
+        sums, block_grad[-1] = together(small_sum(sums, ("context",)), block_grad[-1])
+        block_grad = jnp.concatenate(block_grad)
+        grad_context = low(contract_last(block_grad, self.output_weight))
+        sums, grad_context = together(sums, grad_context)
+        sums = small_sum(sums, ("expert",))
+        pieces = jnp.split(grad_context, ring, axis=1)
+        pieces = jnp.concatenate(
+            [pieces[0]] + [permute_by("context", pieces[d], d) for d in range(1, ring)]
+        )
+        grad_context, delta = block_call(
+            functools.partial(context_grad_kernel, share=self.share),
+            (pieces, self.context),
+            [distance_spec(block, HD), rows_spec(block, HD)],
+            [rows_spec(block, HD), scalars_spec(block)],
+            [
+                jax.ShapeDtypeStruct((rows, HD), jnp.bfloat16),
+                jax.ShapeDtypeStruct((8, rows), jnp.float32),
+            ],
+            ring,
+            self.places,
+        )
+        sums, delta = together(sums, delta)
+        sums = small_sum(sums, ("dp",))
+        output_grad = contract_rows(self.context_block, block_grad)
+        head = lax.axis_index("context")
+        output_grad = jnp.concatenate(
+            [
+                lax.dynamic_slice_in_dim(output_grad, (h + ring - head) % ring * HD, HD, 0)
+                for h in range(ring)
+            ]
+        )
+        output_total = lax.psum(low(output_grad), ("dp", "context"))
         query_grad, key_grad, value_grad = flash_backward(
             self.queries,
             self.keys,
@@ -311,55 +720,124 @@
             self.logs,
             delta,
             self.length,
-            self.block,
-        )
-        grad_query_normed = self.turn(query_grad, rotate_back)
-        grad_key_normed = self.turn(key_grad, rotate_back)
-        gain_grads = jnp.concatenate(
+            block,
+        )
+        kept, received = zip(*pending)
+        query_grad, kept = together(query_grad, kept)
+        self.finished = finish(zip(kept, received))
+        dots, gain_grads = block_call(
+            turn_grad_kernel,
+            (*self.common, query_grad, key_grad),
+            self.common_specs + [rows_spec(block, HD)] * 2,
+            [scalars_spec(block, 2), fixed_spec(8, HD)],
             [
-                jnp.sum(self.query_raw * self.query_inv * grad_query_normed, axis=0),
-                jnp.sum(self.key_raw * self.key_inv * grad_key_normed, axis=0),
-            ]
-        )
-        dots = lax.psum(
-            jnp.stack(
-                [
-                    jnp.sum(self.query_raw * self.query_gain * grad_query_normed, axis=-1),
-                    jnp.sum(self.key_raw * self.key_gain * grad_key_normed, axis=-1),
-                ]
+                jax.ShapeDtypeStruct((2, rows), jnp.float32),
+                jax.ShapeDtypeStruct((8, HD), jnp.float32),
+            ],
+            ring,
+        )
+        dots = small_sum(dots, TOKEN_AXES)
+        grad_joint, relative = block_call(
+            functools.partial(norm_grad_kernel, share=self.share),
+            (*self.common, query_grad, key_grad, value_grad, dots),
+            self.common_specs + [rows_spec(block, HD)] * 3 + [scalars_spec(block, 2)],
+            [rows_spec(block, 3 * HD), distance_spec(block, 3 * HD)],
+            [jax.ShapeDtypeStruct((rows, 3 * HD), jnp.bfloat16)] * 2,
+            ring,
+            self.places,
+        )
+        half = block // 2
+
+        def term(s):
+            return tuple(
+                contract_last(relative[start : start + half], self.weight).reshape(
+                    -1, tok_rows, self.weight.shape[0]
+                )
+                for start in (s * block, s * block + half)
+            )
+
+        joint = JointTotal(ring, self.weight.shape[0] // lax.axis_size("dp"))
+
+        def first(_, rows, right, gain_grads):
+            joint_grad = contract_rows(rows, right)
+            product = jnp.sum(joint_grad * self.weight.astype(jnp.float32), axis=1)
+            here = (lax.axis_index("expert") * ring + head) * HD
+            gains = lax.dynamic_update_slice(
+                jnp.zeros((2, product.shape[0]), jnp.float32), gain_grads[:2], (0, here)
+            )
+            share = ring_sum(ring_parts(joint_grad, "dp", 0), "dp")
+            return (low(share), jnp.concatenate([product[None], gains]), ())
+
+        def later(i):
+            def work(result):
+                piece, gains, outs = result
+                joint.outs = outs
+                joint.add(piece, i)
+                axes = ("expert", "context", "dp")
+                gains = small_sum(gains, axes[i : i + 1])
+                return (next_on("context", piece), gains, joint.outs)
+
+            return work
+
+        works = [((self.normed, grad_joint, gain_grads), first)]
+        works += [((), later(i)) for i in range(ring - 1)]
+        total, (piece, gains, joint.outs) = scatter_chunks(term, works)
+        if ring < 4:
+            gains = small_sum(gains, ("expert", "context", "dp")[ring - 1 :])
+        joint.add(piece, ring - 1)
+        output_total, total = together(output_total, total)
+        return (
+            total,
+            sums,
+            gains[0],
+            *joint.outs,
+            *lax.dynamic_slice_in_dim(
+                gains[1:], lax.axis_index("expert") * ring * HD, ring * HD, 1
             ),
-            TOKEN_AXES,
-        ) / (HEADS * HD)
-        grad_query = (
-            self.query_inv * self.query_gain * grad_query_normed
-            - self.query_raw * self.query_inv**3 * dots[0][:, None]
-        )
-        grad_key = (
-            self.key_inv * self.key_gain * grad_key_normed
-            - self.key_raw * self.key_inv**3 * dots[1][:, None]
-        )
-        grad_joint = low(jnp.concatenate([grad_query, grad_key, value_grad], axis=1))
-        grad_normed = scatter_sequence(contract_last(grad_joint, self.weight))
-        joint_grad = contract_rows(self.normed, grad_joint)
-        joint_total = lax.all_gather(low(sum_low(joint_grad, "dp")), "context", axis=0)
-        gains_total = lax.all_gather(lax.psum(gain_grads, "dp"), "context", axis=0)
-
-        def spread(part):
-            part = part.astype(jnp.float32)
-            return jnp.moveaxis(part, 0, -2).reshape(part.shape[1:-1] + (-1,))
-
-        return (
-            grad_normed,
-            *(spread(joint_total[..., i * HD : (i + 1) * HD]) for i in range(3)),
-            *(spread(gains_total[..., i * HD : (i + 1) * HD]) for i in range(2)),
-            output_total,
-        )
+            output_total.astype(jnp.float32),
+        )
+
+
+def spread_kernel(place_ref, in_ref, *refs):
+    for i, out_ref in enumerate(refs[-3:]):
+        out_ref[...] = in_ref[:, i * HD : (i + 1) * HD].astype(jnp.float32)
+
+
+class JointTotal:
+    def __init__(self, ring, rows):
+        self.ring, self.rows = (ring, rows)
+        self.outs = ()
+
+    def add(self, piece, distance):
+        ring, rows, size = (self.ring, self.rows, lax.axis_size("dp"))
+        head = (lax.axis_index("context") + ring - distance) % ring
+        for j, part in enumerate(ring_gather(piece, "dp")):
+            half = (lax.axis_index("dp") + size - j) % size
+            self.outs = pl.pallas_call(
+                spread_kernel,
+                grid_spec=pltpu.PrefetchScalarGridSpec(
+                    num_scalar_prefetch=1,
+                    grid=(1,),
+                    in_specs=[fixed_spec(rows, 3 * HD)]
+                    + [pl.BlockSpec(memory_space=pl.ANY)] * len(self.outs),
+                    out_specs=[pl.BlockSpec((rows, HD), lambda i, place: (place[0], place[1]))]
+                    * 3,
+                ),
+                out_shape=[jax.ShapeDtypeStruct((rows * size, ring * HD), jnp.float32)] * 3,
+                input_output_aliases={2 + i: i for i in range(len(self.outs))},
+                compiler_params=pltpu.CompilerParams(vmem_limit_bytes=VMEM_LIMIT),
+                cost_estimate=pl.CostEstimate(
+                    flops=0, bytes_accessed=18 * rows * HD, transcendentals=0
+                ),
+            )(jnp.stack([half, head]).astype(jnp.int32), part, *self.outs)
 
 
 class BlockAttention:
-    def __init__(self, normed, length, weights, gains, output_weight):
+    def __init__(self, normed, length, weights, gains, output_weight, experts, count):
         self.tok_rows = normed.shape[0]
         self.output_weight = output_weight
+        self.count_total = count
+        gather_chunks(experts.chosen, lambda s, blocks: experts.pick(experts.here(blocks)))
         self.length = length
         self.query_gain, self.key_gain = gains
         self.head_width = head_width = weights[0].shape[1]
@@ -430,7 +908,9 @@
             jnp.float32
         )
 
-    def backward(self, grad_attn):
+    def backward(self, grad_attn, sums, pending):
+        self.finished = finish(pending)
+        sums = small_sum(sums, ALL_AXES)
         rows, heads = (self.rows, self.heads)
         block_grad = gather_block(grad_attn)
         output_total = sum_low(contract_rows(self.context, block_grad), ("dp", "context"))
@@ -505,84 +985,437 @@
             ),
             ("dp", "context"),
         )
-        return (grad_normed, *jnp.split(joint_total, 3, axis=1), *gains_total, output_total)
+        gain_product = jnp.sum(joint_total * self.weight.astype(jnp.float32), axis=1)
+        gain_product = lax.psum(gain_product, "expert")
+        return (
+            grad_normed,
+            sums,
+            gain_product,
+            *jnp.split(joint_total, 3, axis=1),
+            *gains_total,
+            output_total,
+        )
+
+
+UNIT_TILE = 256
+WIDTH_TILE = 512
+
+
+def expert_forward_kernel(expert_ref, *refs, count, experts_all, unit_tiles):
+    blocks = refs[:count]
+    pick_ref, router_ref, gate_weight_ref, up_weight_ref, down_weight_ref = refs[
+        count : count + 5
+    ]
+    (
+        rows_ref,
+        gate_ref,
+        up_ref,
+        hidden_ref,
+        out_ref,
+        row_gate_ref,
+        kept_ref,
+        sent_ref,
+        scaled_ref,
+        units_ref,
+    ) = refs[-10:]
+    step = pl.program_id(0)
+    capacity = pick_ref.shape[1]
+
+    @pl.when(step == 0)
+    def _():
+        for i, block_ref in enumerate(blocks):
+            here = pl.ds(i * capacity, capacity)
+            tokens = block_ref[...]
+            pick = pick_ref[i]
+            rows_ref[here, :] = low(contract(pick, tokens, 1, 0))
+            logits = contract(tokens, router_ref[...], 1, 0)
+            lane = lax.broadcasted_iota(jnp.int32, logits.shape, 1)
+            logits = jnp.where(lane < experts_all, logits, NEGATIVE)
+            weights = jnp.exp(logits - jnp.max(logits, axis=1, keepdims=True))
+            chosen = jnp.sum(
+                jnp.where(lane == expert_ref[0], weights, 0.0), axis=1, keepdims=True
+            )
+            gates = as_row(chosen / jnp.sum(weights, axis=1, keepdims=True))
+            scaled = pick.astype(jnp.float32) * gates
+            scaled_ref[i] = low(scaled)
+            row_gates = jnp.sum(scaled, axis=1, keepdims=True)
+            row_gate_ref[here, :] = jnp.broadcast_to(row_gates, (capacity, HD))
+
+    @pl.when(step < unit_tiles)
+    def _():
+        rows = rows_ref[...]
+        gate_part = contract(rows, gate_weight_ref[...], 1, 0)
+        up_part = contract(rows, up_weight_ref[...], 1, 0)
+        hidden = low(silu_parts(gate_part)[0] * up_part)
+        gate_ref[...] = low(gate_part)
+        up_ref[...] = low(up_part)
+        hidden_ref[...] = hidden
+        for j in range(unit_tiles):
+
+            @pl.when(step == j)
+            def _(j=j):
+                units_ref[:, j * UNIT_TILE : (j + 1) * UNIT_TILE] = hidden
+
+    @pl.when(step >= unit_tiles)
+    def _():
+        out_ref[...] = low(contract(units_ref[...], down_weight_ref[...], 1, 0))
+        spread_tokens(scaled_ref, out_ref, kept_ref, sent_ref)
+
+
+def spread_tokens(pick_ref, rows_ref, kept_ref, sent_ref):
+    count, capacity, tok_rows = pick_ref.shape
+    half = count // 2
+    for i in range(count):
+        terms = contract_rows(pick_ref[i], rows_ref[pl.ds(i * capacity, capacity), :])
+        if i < half:
+            kept_ref[i] = low(terms)
+        else:
+            sent_ref[i - half] = low(terms)
+
+
+def expert_backward_kernel(*refs, count, unit_tiles):
+    blocks = refs[:count]
+    (
+        pick_ref,
+        row_gate_ref,
+        gate_ref,
+        up_ref,
+        out_ref,
+        down_weight_ref,
+        gate_weight_ref,
+        up_weight_ref,
+    ) = refs[count : count + 8]
+    (
+        gate_grad_ref,
+        grad_out_ref,
+        grad_gate_ref,
+        grad_up_ref,
+        kept_ref,
+        sent_ref,
+        gates_ref,
+        ups_ref,
+        rows_ref,
+    ) = refs[-9:]
+    step = pl.program_id(0)
+    capacity = pick_ref.shape[1]
+
+    @pl.when(step == 0)
+    def _():
+        for i, block_ref in enumerate(blocks):
+            here = pl.ds(i * capacity, capacity)
+            pick = pick_ref[i]
+            grads = contract(pick, block_ref[...], 1, 0)
+            dots = jnp.sum(grads * out_ref[here, :].astype(jnp.float32), axis=1, keepdims=True)
+            gate_grad_ref[i : i + 1, :] = jnp.sum(
+                pick.astype(jnp.float32) * dots, axis=0, keepdims=True
+            )
+            grad_out_ref[here, :] = low(grads * row_gate_ref[here, 0:1])
+
+    @pl.when(step < unit_tiles)
+    def _():
+        grad_hidden = contract_last(grad_out_ref[...], down_weight_ref[...])
+        silu_value, silu_slope = silu_parts(gate_ref[...].astype(jnp.float32))
+        grad_gate = low(grad_hidden * up_ref[...].astype(jnp.float32) * silu_slope)
+        grad_up = low(grad_hidden * silu_value)
+        grad_gate_ref[...] = grad_gate
+        grad_up_ref[...] = grad_up
+        for j in range(unit_tiles):
+
+            @pl.when(step == j)
+            def _(j=j):
+                gates_ref[:, j * UNIT_TILE : (j + 1) * UNIT_TILE] = grad_gate
+                ups_ref[:, j * UNIT_TILE : (j + 1) * UNIT_TILE] = grad_up
+
+    @pl.when(step >= unit_tiles)
+    def _():
+        rows_ref[...] = low(
+            contract_last(gates_ref[...], gate_weight_ref[...])
+            + contract_last(ups_ref[...], up_weight_ref[...])
+        )
+        spread_tokens(pick_ref, rows_ref, kept_ref, sent_ref)
+
+
+def chunk_call(kernel, arrays, in_specs, outs, before, scratch, steps, cost, prefetch=()):
+    first = len(prefetch) + len(arrays)
+    return pl.pallas_call(
+        kernel,
+        grid_spec=pltpu.PrefetchScalarGridSpec(
+            num_scalar_prefetch=len(prefetch),
+            grid=(steps,),
+            in_specs=in_specs + [pl.BlockSpec(memory_space=pl.ANY)] * len(before),
+            out_specs=[out[2] for out in outs],
+            scratch_shapes=scratch,
+        ),
+        out_shape=[jax.ShapeDtypeStruct(out[0], out[1]) for out in outs],
+        input_output_aliases={first + i: j for i, j in enumerate(before)},
+        compiler_params=pltpu.CompilerParams(vmem_limit_bytes=VMEM_LIMIT),
+        cost_estimate=cost,
+    )(*prefetch, *arrays, *before.values())
 
 
 class Experts:
-    def __init__(self, routes, capacity, gate_weight, up_weight, down_weight):
-        tok_rows = routes.shape[0]
-        expert = lax.axis_index("context") * lax.axis_size("expert") + lax.axis_index("expert")
-        self.expert = expert
-        everyone = lax.all_gather(routes.T, TOKEN_AXES, axis=0)
-        member = jnp.any(everyone == expert, axis=1)
+    def __init__(self, routes, capacity, router_weight, gate_weight, up_weight, down_weight):
+        self.capacity = -(-capacity // 16) * 16
+        self.experts_all = router_weight.shape[1]
+        self.expert = lax.axis_index("context") * lax.axis_size("expert") + lax.axis_index(
+            "expert"
+        )
+        self.router_weight = jnp.pad(router_weight, ((0, 0), (0, HD - self.experts_all)))
+        expert_ids = jnp.arange(HD, dtype=jnp.int32)
+        self.chosen = low(jnp.any(routes[:, :, None] == expert_ids, axis=1))
+        gates = ring_gather(gate_weight[0], "dp")
+        _, up_first = together(gates[-1], up_weight[0])
+        ups = ring_gather(up_first, "dp")
+        _, down_first = together(ups[-1], down_weight[0])
+        self.weights = (gates, ups, ring_gather(down_first, "dp"))
+        self.picks = []
+
+    def here(self, blocks):
+        lane = jnp.arange(HD, dtype=jnp.int32) == self.expert
+        return jnp.sum(jnp.where(lane, jnp.stack(blocks).astype(jnp.float32), 0.0), axis=-1)
+
+    def pick(self, here):
+        member = here > 0
+        tok_rows = member.shape[1]
         token = jnp.arange(tok_rows, dtype=jnp.int32)
         before = low(token[:, None] < token[None, :])
-        slots = jnp.dot(low(member), before, preferred_element_type=jnp.float32)
-        slot_index = jnp.arange(capacity, dtype=jnp.int32)
-        matches = slots.astype(jnp.int32)[:, None, :] == slot_index[None, :, None]
-        self.picks = (matches & member[:, None, :]).astype(jnp.float32)
-        self.pick = low(self.picks)
-        gate_all, up_all = (
-            lax.all_gather(w[0], "dp", axis=1, tiled=True) for w in (gate_weight, up_weight)
-        )
-        self.joint = jnp.concatenate([gate_all, up_all], axis=1)
-        self.down = lax.all_gather(down_weight[0], "dp", axis=0, tiled=True)
-
-    def rows_of(self, tokens):
-        blocks = tokens.reshape(self.pick.shape[0], self.pick.shape[2], -1)
-        rows = jnp.einsum("bst,btd->bsd", self.pick, blocks, preferred_element_type=jnp.float32)
-        return rows.reshape(-1, blocks.shape[2])
-
-    def tokens_of(self, pick, rows):
-        blocks = low(rows).reshape(pick.shape[0], pick.shape[1], -1)
-        tokens = jnp.einsum("bst,bsd->btd", pick, blocks, preferred_element_type=jnp.float32)
-        return tokens.reshape(-1, blocks.shape[2])
-
-    def forward(self, ffn_in, gates):
-        everyone = lax.all_gather(gates.T, TOKEN_AXES, axis=0)
-        gates_here = lax.dynamic_index_in_dim(everyone, self.expert, 1, keepdims=False)
-        scaled_picks = self.picks * gates_here[:, None, :]
-        self.row_gates = jnp.sum(scaled_picks, axis=-1).reshape(-1, 1)
-        self.rows = low(self.rows_of(gather_sequence(ffn_in)))
-        joint = low(jnp.dot(self.rows, self.joint, preferred_element_type=jnp.float32))
-        self.gate_part, self.up_part = jnp.split(joint, 2, axis=1)
-        silu_value, _ = silu_parts(self.gate_part.astype(jnp.float32))
-        self.hidden = low(silu_value * self.up_part.astype(jnp.float32))
-        self.out = low(jnp.dot(self.hidden, self.down, preferred_element_type=jnp.float32))
-        return scatter_sequence(self.tokens_of(low(scaled_picks), self.out))
+        slots = contract(low(member), before, 1, 0).astype(jnp.int32)
+        slot_index = jnp.arange(self.capacity, dtype=jnp.int32)
+        matches = slots[:, None, :] == slot_index[None, :, None]
+        self.picks.append(low(matches & member[:, None, :]))
+
+    def begin(self):
+        self.gate_weight, self.up_weight = (
+            jnp.concatenate(parts, axis=1) for parts in self.weights[:2]
+        )
+        self.down_weight = jnp.concatenate(self.weights[2], axis=0)
+        self.units = self.gate_weight.shape[1]
+        self.picks = jnp.stack(self.picks)
+        self.chained, self.chained_back = ((), ())
+        self.terms, self.terms_back = ({}, {})
+
+    def shapes(self):
+        ring, count, capacity, tok_rows = self.picks.shape
+        width = self.gate_weight.shape[0]
+        return ring, count, count * capacity, tok_rows, width
+
+    def plan(self, s):
+        ring, count, rows, tok_rows, width = self.shapes()
+        tiles = self.units // UNIT_TILE
+        tile = math.gcd(WIDTH_TILE, width)
+
+        def unit(j):
+            return jnp.minimum(j, tiles - 1)
+
+        def column(j):
+            return jnp.maximum(j - tiles, 0)
+
+        half = count // 2
+        all_rows = ring * rows
+        term = (
+            (half, tok_rows, width),
+            jnp.bfloat16,
+            pl.BlockSpec((half, tok_rows, tile), lambda j, *_: (0, 0, column(j))),
+        )
+        unit_spec = pl.BlockSpec((rows, UNIT_TILE), lambda j, *_: (s, unit(j)))
+        whole_spec = pl.BlockSpec((rows, width), lambda j, *_: (s, 0))
+        scalar_spec = pl.BlockSpec((rows, HD), lambda j, *_: (s, 0))
+        column_spec = pl.BlockSpec((rows, tile), lambda j, *_: (s, column(j)))
+        block_specs = [pl.BlockSpec((tok_rows, width), lambda j, *_: (0, 0))] * count
+        pick_spec = pl.BlockSpec((None, *self.picks.shape[1:]), lambda j, *_: (s, 0, 0, 0))
+        narrow = ((all_rows, self.units), jnp.bfloat16, unit_spec)
+        wide = ((all_rows, width), jnp.bfloat16, whole_spec)
+        cost = pl.CostEstimate(
+            flops=6 * rows * width * self.units,
+            bytes_accessed=6 * self.units * width + 12 * rows * width,
+            transcendentals=rows * self.units,
+        )
+        return (
+            unit,
+            column,
+            tiles,
+            tile,
+            term,
+            unit_spec,
+            whole_spec,
+            scalar_spec,
+            column_spec,
+            block_specs,
+            pick_spec,
+            narrow,
+            wide,
+            cost,
+        )
+
+    def forward_chunk(self, s, blocks):
+        ring, count, rows, tok_rows, width = self.shapes()
+        (
+            unit,
+            column,
+            tiles,
+            tile,
+            term,
+            unit_spec,
+            whole_spec,
+            scalar_spec,
+            column_spec,
+            block_specs,
+            pick_spec,
+            narrow,
+            wide,
+            cost,
+        ) = self.plan(s)
+        results = chunk_call(
+            functools.partial(
+                expert_forward_kernel,
+                count=count,
+                experts_all=self.experts_all,
+                unit_tiles=tiles,
+            ),
+            (
+                *blocks,
+                self.picks,
+                self.router_weight,
+                self.gate_weight,
+                self.up_weight,
+                self.down_weight,
+            ),
+            [
+                *block_specs,
+                pick_spec,
+                fixed_spec(width, HD),
+                pl.BlockSpec((width, UNIT_TILE), lambda j, *_: (0, unit(j))),
+                pl.BlockSpec((width, UNIT_TILE), lambda j, *_: (0, unit(j))),
+                pl.BlockSpec((self.units, tile), lambda j, *_: (0, column(j))),
+            ],
+            [
+                wide,
+                narrow,
+                narrow,
+                narrow,
+                (wide[0], wide[1], column_spec),
+                ((ring * rows, HD), jnp.float32, scalar_spec),
+                term,
+                term,
+            ],
+            dict(enumerate(self.chained)),
+            [
+                pltpu.VMEM(self.picks.shape[1:], jnp.bfloat16),
+                pltpu.VMEM((rows, self.units), jnp.bfloat16),
+            ],
+            tiles + width // tile,
+            cost,
+            (self.expert.reshape(1).astype(jnp.int32),),
+        )
+        self.chained = results[:6]
+        self.terms[s] = results[6:]
+        return results[7]
+
+    def forward(self, ffn_in):
+        last = lax.axis_size("context") - 1
+        done, _ = gather_chunks(ffn_in, self.forward_chunk, slack=1)
+        idle = ((), lambda result: result)
+        works = [((), lambda result: done[last])] + [idle] * last
+        mixture, _ = scatter_chunks(lambda s: self.terms[s], works)
+        return mixture
+
+    def backward_chunk(self, s, blocks):
+        ring, count, rows, tok_rows, width = self.shapes()
+        (
+            unit,
+            column,
+            tiles,
+            tile,
+            term,
+            unit_spec,
+            whole_spec,
+            scalar_spec,
+            column_spec,
+            block_specs,
+            pick_spec,
+            narrow,
+            wide,
+            cost,
+        ) = self.plan(s)
+        chunk_rows, gate_part, up_part, hidden, out, row_gates = self.chained
+        results = chunk_call(
+            functools.partial(expert_backward_kernel, count=count, unit_tiles=tiles),
+            (
+                *blocks,
+                self.picks,
+                row_gates,
+                gate_part,
+                up_part,
+                out,
+                self.down_weight,
+                self.gate_weight,
+                self.up_weight,
+            ),
+            [
+                *block_specs,
+                pick_spec,
+                scalar_spec,
+                unit_spec,
+                unit_spec,
+                whole_spec,
+                pl.BlockSpec((UNIT_TILE, width), lambda j, *_: (unit(j), 0)),
+                pl.BlockSpec((tile, self.units), lambda j, *_: (column(j), 0)),
+                pl.BlockSpec((tile, self.units), lambda j, *_: (column(j), 0)),
+            ],
+            [
+                ((count, tok_rows), jnp.float32, fixed_spec(count, tok_rows)),
+                wide,
+                narrow,
+                narrow,
+                term,
+                term,
+            ],
+            {j + 1: array for j, array in enumerate(self.chained_back)},
+            [
+                pltpu.VMEM((rows, self.units), jnp.bfloat16),
+                pltpu.VMEM((rows, self.units), jnp.bfloat16),
+                pltpu.VMEM((rows, tile), jnp.bfloat16),
+            ],
+            tiles + width // tile,
+            cost,
+        )
+        self.chained_back = results[1:4]
+        self.terms_back[s] = results[4:]
+        return results[0]
 
     def backward(self, grad_out):
-        grads = self.rows_of(gather_sequence(low(grad_out)))
-        gate_grads = jnp.sum(grads * self.out.astype(jnp.float32), axis=-1)
-        tok_rows = self.picks.shape[2]
-        gate_grads = jnp.sum(
-            self.picks * gate_grads.reshape(self.picks.shape[:2])[:, :, None], axis=1
-        )
-        grad_gates = lax.all_to_all(
-            gate_grads, TOKEN_AXES, split_axis=0, concat_axis=0, tiled=True
-        ).T
-        grad_rows_out = low(grads * self.row_gates)
-        grad_hidden = contract_last(grad_rows_out, self.down)
-        silu_value, silu_slope = silu_parts(self.gate_part.astype(jnp.float32))
-        grad_joint = low(
-            jnp.concatenate(
-                [
-                    grad_hidden * self.up_part.astype(jnp.float32) * silu_slope,
-                    grad_hidden * silu_value,
-                ],
-                axis=1,
-            )
-        )
-        grad_rows = contract_last(grad_joint, self.joint)
-        grad_ffn = scatter_sequence(self.tokens_of(self.pick, grad_rows))
-        joint_grad = contract_rows(self.rows, grad_joint)
-        gate_grad, up_grad = jnp.split(joint_grad, 2, axis=1)
-        down_grad = contract_rows(self.hidden, grad_rows_out)
-        weight_grads = tuple(
-            sum_half_over_dp(g, axis)[None]
-            for g, axis in ((gate_grad, 1), (up_grad, 1), (down_grad, 0))
-        )
-        return grad_ffn, grad_gates, weight_grads
+        last = lax.axis_size("context") - 1
+        gate_grads, _ = gather_chunks(low(grad_out), self.backward_chunk, slack=1)
+        grad_rows_out, grad_gate, grad_up = self.chained_back
+        chunk_rows, hidden = (self.chained[0], self.chained[3])
+        size = lax.axis_size("dp")
+
+        def parts(left, right, axis):
+            return jnp.split(contract_rows(left, right), size, axis=axis)
+
+        def first(_):
+            return gate_grads[last]
+
+        def second(_, grad, rows, right):
+            grad_gates = lax.all_to_all(
+                reorder(grad, absolute_to_relative()),
+                TOKEN_AXES,
+                split_axis=0,
+                concat_axis=0,
+                tiled=True,
+            ).T
+            return grad_gates, parts(rows, right, 1)
+
+        def third(result, rows, right):
+            return *result, parts(rows, right, 1)
+
+        works = [((), first)] + [((), lambda result: result)] * last
+        works[1] = ((jnp.concatenate(gate_grads), chunk_rows, grad_gate), second)
+        works[2] = ((chunk_rows, grad_up), third)
+        grad_ffn, (grad_gates, *grads) = scatter_chunks(lambda s: self.terms_back[s], works)
+        grads.append(parts(hidden, grad_rows_out, 0))
+        pending = [ring_sum_begin(part, "dp") for part in grads]
+        return grad_ffn, grad_gates, pending
 
 
 def per_device(
@@ -617,6 +1450,11 @@
     inverse_one = rms_scale(tokens)
     normed = low(tokens * inverse_one * attn_gain)
     heads_here = query_weight.shape[1] // HD
+    count_total = small_sum(jnp.full((8, 128), length, jnp.int32), ("dp",))
+    count_total, gate_weight = together(count_total, gate_weight)
+    experts = Experts(
+        expert_routes, capacity, router_weight, gate_weight, up_weight, down_weight
+    )
     attention_kind = HeadAttention if heads_here == context_size else BlockAttention
     attention = attention_kind(
         normed,
@@ -624,8 +1462,11 @@
         (query_weight, key_weight, value_weight),
         (query_gain, key_gain),
         output_weight,
-    )
-    experts = Experts(expert_routes, capacity, gate_weight, up_weight, down_weight)
+        experts,
+        count_total,
+    )
+    experts.begin()
+    count_total = attention.count_total[0, 0].astype(jnp.float32)
     residual = tokens + attention.output()
     inverse_two = rms_scale(residual)
     ffn_in = low(residual * inverse_two * ffn_gain)
@@ -634,22 +1475,21 @@
     router_probs = weights_router / jnp.sum(weights_router, axis=-1, keepdims=True)
     expert_ids = jnp.arange(experts_all, dtype=jnp.int32)
     chosen = jnp.any(expert_routes[:, :, None] == expert_ids, axis=1)
-    mixture = experts.forward(ffn_in, jnp.where(chosen, router_probs, 0.0))
+    mixture = experts.forward(ffn_in)
     output_full = residual + mixture
     own_pos = own_start + jnp.arange(tok_rows, dtype=jnp.int32)
     valid = (own_pos < length).astype(jnp.float32)
     difference = output_full - teacher_states
     local_loss = jnp.sum(jnp.sum(difference * difference, axis=-1) * valid)
-    count_total = lax.psum(length, "dp").astype(jnp.float32)
     grad_out = difference * (valid * (token_count_all / count_total))[:, None]
-    grad_ffn_experts, grad_gates, expert_grads = experts.backward(grad_out)
+    grad_ffn_experts, grad_gates, pending = experts.backward(grad_out)
     grad_router_probs = jnp.where(chosen, grad_gates, 0.0)
     grad_logits = router_probs * (
         grad_router_probs - jnp.sum(router_probs * grad_router_probs, axis=-1, keepdims=True)
     )
     router_grad = lax.dot_general(
+        grad_logits,
         ffn_in.astype(jnp.float32),
-        grad_logits,
         (((0,), (0,)), ((), ())),
         precision=lax.Precision.HIGHEST,
     )
@@ -666,31 +1506,37 @@
         + inverse_two * weighted_two
         - residual * inverse_two**3 * jnp.mean(residual * weighted_two, axis=-1, keepdims=True)
     )
+    sums = jnp.concatenate(
+        [
+            router_grad,
+            ffn_gain_grad[None],
+            jnp.broadcast_to(local_loss, ffn_gain_grad.shape)[None],
+        ]
+    )
     (
         grad_normed,
+        sums,
+        attn_gain_product,
         query_total,
         key_total,
         value_total,
         query_gain_total,
         key_gain_total,
         output_total,
-    ) = attention.backward(low(grad_residual))
-    attn_gain_grad = jnp.sum(tokens * inverse_one * grad_normed, axis=0)
+    ) = attention.backward(low(grad_residual), sums, pending)
     weighted_one = grad_normed * attn_gain
     input_grad = (
         grad_residual
         + inverse_one * weighted_one
         - tokens * inverse_one**3 * jnp.mean(tokens * weighted_one, axis=-1, keepdims=True)
     )
-    loss_total, ffn_total, router_total = lax.psum(
-        (local_loss, ffn_gain_grad, router_grad), ALL_AXES
-    )
-    attn_total = lax.psum(attn_gain_grad, ALL_AXES)
+    router_total, ffn_total = (sums[:experts_all].T, sums[experts_all])
+    loss_total = sums[experts_all + 1, 0]
     return (
         low(output_full),
         loss_total / count_total,
         input_grad,
-        attn_total,
+        attn_gain_product / attn_gain,
         query_total,
         key_total,
         value_total,
@@ -699,7 +1545,7 @@
         output_total,
         ffn_total,
         router_total,
-        *expert_grads,
+        *attention.finished,
     )
 
 

time: 2080 us -> 1230 us (0.59)
  waiting for transfers between devices: 1290 us -> 462 us
  Pallas kernels: 60.3 us -> 326 us
  blocking collectives: 253 us -> 0 us
  matrix products: 261 us -> 98.3 us
  starting transfers between devices: 9.31 us -> 134 us
    reduce_scatter x4 -> x0, waiting for transfers between devices: 524 us -> none  [the longest x3 481 us: scatter_sequence(): lax.psum_scatter(low(rows), TOKEN_AXES, scatter_dimension=0, tiled=True)]
    all_gather x8 -> x0, waiting for transfers between devices: 516 us -> none  [the longest x3 333 us: gather_sequence(): return lax.all_gather(rows, TOKEN_AXES, axis=0, tiled=True)]
    ppermute x3 -> x130, waiting for transfers between devices: 95.6 us -> 462 us  [the longest x97 383 us: moved(): return jax.tree.map(lambda v: lax.ppermute(v, axis, pairs), values)]
    pallas_call x1 -> x25, Pallas kernels: 22.9 us -> 288 us  [the longest x12 203 us: chunk_call(): pl.pallas_call(kernel, grid_spec=pltpu.PrefetchScalarGridSpec(num_scalar_...]
    psum x5 -> x0, blocking collectives: 166 us -> none  [the longest x1 58.9 us: __init__(): lax.psum(jnp.stack([jnp.sum(self.query_raw ** 2, axis=-1), jnp.sum(self.k...]
    ppermute x3 -> x130, starting transfers between devices: 3.8 us -> 130 us  [the longest x97 83.8 us: moved(): return jax.tree.map(lambda v: lax.ppermute(v, axis, pairs), values)]
    psum x3 -> x1, waiting for transfers between devices: 122 us -> 0.01 us  [backward(): output_total = lax.psum(low(output_grad), ('dp', 'context'))]
    dot_general x10 -> x2, matrix products: 119 us -> 0.71 us  [the longest x1 0.52 us: per_device(): lax.dot_general(grad_logits, ffn_in.astype(jnp.float32), (((0,), (0,)), (...]
  transfers between devices with their start and end apart: 19 -> 132, of which waited for: 18 -> 49; matrix products, arithmetic and copies ran while one was open for 9% -> 19% of each run, Pallas kernels for 0% -> 24%
where the time goes in v2:
time: 1230 us; the launch traced here: 1220 us
  waiting for transfers between devices  462 us (38%)
  Pallas kernels  326 us (27%)
  starting transfers between devices  134 us (11%)
  other arithmetic  119 us (10%)
  matrix products  98.3 us (8%)
  local copies, waits for them, and re-layouts  61.1 us (5%)
  between operations  19.4 us (2%)
    ppermute x97, waiting for transfers between devices, moved(): return jax.tree.map(lambda v: lax.ppermute(v, axis, pairs), values)  383 us
    pallas_call x12, Pallas kernels, chunk_call(): pl.pallas_call(kernel, grid_spec=pltpu.PrefetchScalarGridSpec(num_scalar_...  203 us
    dot_general x20, matrix products, contract(): lax.dot_general(left, right, (((left_dim,), (right_dim,)), ((), ())), pre...  93.1 us
    ppermute x97, starting transfers between devices, moved(): return jax.tree.map(lambda v: lax.ppermute(v, axis, pairs), values)  83.8 us
    ppermute x6, waiting for transfers between devices, permute_by(): lax.ppermute(values, axis, tuple(((i, (i + distance) % size) for i in ran...  50.9 us
    ppermute x27, starting transfers between devices, small_sum(): lax.ppermute(values, axis, tuple(((i, i ^ bits) for i in range(size))))  42.9 us
    pallas_call x1, Pallas kernels, flash_backward(): pl.pallas_call(functools.partial(flash_backward_kernel, block=block), gri...  38.7 us
    pallas_call x4, Pallas kernels, block_call(): pl.pallas_call(kernel, grid_spec=pltpu.PrefetchScalarGridSpec(num_scalar_...  34.5 us
  transfers between devices with their start and end apart: 132, of which 49 were waited for; matrix products, arithmetic and copies ran while one was open for 19% of the time, Pallas kernels for 24%

profile of v2, /device:TPU:0, one launch (start us, length us, event | category | flops | bytes accessed | tf_op | source)
XLA Modules:
  0.0 1219.1 jit_solution(745391480319242860)
XLA Ops:
  20.2 24.6 %collective-permute-done.refs_0_ = bf16[256,2176]{1,0:T(8,128)(2,1)} collective-permute-done((bf16[256,2176]{1,0:T(8,128)(2,1)}, bf16[256,2176]{1,0:T(8,128)(2,1)}, u32[]{:S(2)}, u32[]{:S(2)}) %collective-permute-start) | collective-permute-done | bytes 1114144 | tf_op jit(solution)/shard_map/ppermute | solution.py:87
  47.3 9.7 fusion.54
  57.0 9.5 collective-permute-done.5
  67.0 6.6 pad_maximum_fusion.1
  81.6 8.6 shard_map.271
  90.2 13.3 %collective-permute-done.6.refs_0_ = bf16[256,2176]{1,0:T(8,128)(2,1)} collective-permute-done((bf16[256,2176]{1,0:T(8,128)(2,1)}, bf16[256,2176]{1,0:T(8,128)(2,1)}, u32[]{:S(2)}, u32[]{:S(2)}) %collective-permute-start.6) | collective-permute-done | bytes 1114144 | tf_op jit(solution)/shard_map/ppermute | solution.py:87
  104.0 8.4 collective-permute-done.13
  114.2 8.4 shard_map.272
  122.6 7.3 collective-permute-done.10.refs_1_
  132.5 8.5 shard_map.273
  142.1 8.9 shard_map.274
  151.0 6.2 collective-permute-done.18
  173.2 7.5 shard_map.275
  180.7 26.2 %shard_map.276 = (bf16[4096,128]{1,0:T(8,128)(2,1)}, f32[8,4096]{1,0:T(8,128)}, bf16[4096,128]{1,0:T(8,128)(2,1)}) custom-call(s32[1]{0:T(128)} %copy.191.length_ref, s32[8]{0:T(128)} %pad_add_fusion.places_ref, bf16[4096,128]{1,0:T(8,128)(2,1)} %get-tuple-element.247.q_ref, bf16[4096,128]{1,0:T(8,128)(2,1)} %get-tuple-element.248.k_ref, ...), custom_call_target="tpu_custom_call" | custom-call | flops 8589934592 | bytes 4194304 | tf_op jit(solution)/shard_map/pallas_call | solution.py:483
  211.3 6.1 collective-permute-done.25
  217.4 15.5 %collective-permute-done.26 = bf16[1024,128]{1,0:T(8,128)(2,1)S(1)} collective-permute-done((bf16[1024,128]{1,0:T(8,128)(2,1)S(1)}, bf16[1024,128]{1,0:T(8,128)(2,1)S(1)}, u32[]{:S(2)}, u32[]{:S(2)}) %collective-permute-start.26) | collective-permute-done | bytes 262176 | tf_op jit(solution)/shard_map/ppermute | solution.py:593
  248.9 20.4 %collective-permute-done.29 = bf16[256,2048]{1,0:T(8,128)(2,1)S(1)} collective-permute-done((bf16[256,2048]{1,0:T(8,128)(2,1)S(1)}, bf16[256,2048]{1,0:T(8,128)(2,1)S(1)}, u32[]{:S(2)}, u32[]{:S(2)}) %collective-permute-start.29) | collective-permute-done | bytes 1048608 | tf_op jit(solution)/shard_map/ppermute | solution.py:87
  274.7 22.7 %collective-permute-done.30.refs_0_ = bf16[256,2048]{1,0:T(8,128)(2,1)S(1)} collective-permute-done((bf16[256,2048]{1,0:T(8,128)(2,1)S(1)}, bf16[256,2048]{1,0:T(8,128)(2,1)S(1)}, u32[]{:S(2)}, u32[]{:S(2)}) %collective-permute-start.30) | collective-permute-done | bytes 1048608 | tf_op jit(solution)/shard_map/ppermute | solution.py:87
  301.7 21.5 %collective-permute-done.35.refs_0_ = bf16[256,2048]{1,0:T(8,128)(2,1)S(1)} collective-permute-done((bf16[256,2048]{1,0:T(8,128)(2,1)S(1)}, bf16[256,2048]{1,0:T(8,128)(2,1)S(1)}, u32[]{:S(2)}, u32[]{:S(2)}) %collective-permute-start.35) | collective-permute-done | bytes 1048608 | tf_op jit(solution)/shard_map/ppermute | solution.py:87
  328.1 20.7 %shard_map.277 = (bf16[2560,2048]{1,0:T(8,128)(2,1)}, bf16[2560,1024]{1,0:T(8,128)(2,1)}, bf16[2560,1024]{1,0:T(8,128)(2,1)}, bf16[2560,1024]{1,0:T(8,128)(2,1)}...) custom-call(s32[1]{0:T(128)} %bitcast.expert_ref, ...), custom_call_target="tpu_custom_call" | custom-call | flops 8053063680 | bytes 28311552 | tf_op jit(solution)/shard_map/pallas_call | solution.py:1140
  348.8 21.2 %shard_map.278 = (bf16[2560,2048]{1,0:T(8,128)(2,1)}, bf16[2560,1024]{1,0:T(8,128)(2,1)}, bf16[2560,1024]{1,0:T(8,128)(2,1)}, bf16[2560,1024]{1,0:T(8,128)(2,1)}...) custom-call(s32[1]{0:T(128)} %bitcast.expert_ref, ...), custom_call_target="tpu_custom_call", output_to_operand_aliasing={{0}: (10, {}), {1}: (11, {}), {2}: (12, {}), {3}: (13, {}),... | custom-call | flops 8053063680 | bytes 28311552 | tf_op jit(solution)/shard_map/pallas_call | solution.py:1140
  371.8 6.8 collective-permute-done.44.refs_2_
  379.5 21.4 %shard_map.279 = (bf16[2560,2048]{1,0:T(8,128)(2,1)}, bf16[2560,1024]{1,0:T(8,128)(2,1)}, bf16[2560,1024]{1,0:T(8,128)(2,1)}, bf16[2560,1024]{1,0:T(8,128)(2,1)}...) custom-call(s32[1]{0:T(128)} %bitcast.expert_ref, ...), custom_call_target="tpu_custom_call", output_to_operand_aliasing={{0}: (10, {}), {1}: (11, {}), {2}: (12, {}), {3}: (13, {}),... | custom-call | flops 8053063680 | bytes 28311552 | tf_op jit(solution)/shard_map/pallas_call | solution.py:1140
  408.1 21.0 %shard_map.280 = (bf16[2560,2048]{1,0:T(8,128)(2,1)}, bf16[2560,1024]{1,0:T(8,128)(2,1)}, bf16[2560,1024]{1,0:T(8,128)(2,1)}, bf16[2560,1024]{1,0:T(8,128)(2,1)}...) custom-call(s32[1]{0:T(128)} %bitcast.expert_ref, ...), custom_call_target="tpu_custom_call", output_to_operand_aliasing={{0}: (10, {}), {1}: (11, {}), {2}: (12, {}), {3}: (13, {}),... | custom-call | flops 8053063680 | bytes 28311552 | tf_op jit(solution)/shard_map/pallas_call | solution.py:1140
  439.4 22.3 %collective-permute-done.50 = bf16[256,2048]{1,0:T(8,128)(2,1)S(1)} collective-permute-done((bf16[256,2048]{1,0:T(8,128)(2,1)S(1)}, bf16[256,2048]{1,0:T(8,128)(2,1)S(1)}, u32[]{:S(2)}, u32[]{:S(2)}) %collective-permute-start.50) | collective-permute-done | bytes 1048608 | tf_op jit(solution)/shard_map/ppermute | solution.py:87
  468.4 19.9 %collective-permute-done.52 = bf16[256,2048]{1,0:T(8,128)(2,1)S(1)} collective-permute-done((bf16[256,2048]{1,0:T(8,128)(2,1)S(1)}, bf16[256,2048]{1,0:T(8,128)(2,1)S(1)}, u32[]{:S(2)}, u32[]{:S(2)}) %collective-permute-start.52) | collective-permute-done | bytes 1048608 | tf_op jit(solution)/shard_map/ppermute | solution.py:87
  494.0 20.5 %collective-permute-done.54 = bf16[256,2048]{1,0:T(8,128)(2,1)} collective-permute-done((bf16[256,2048]{1,0:T(8,128)(2,1)}, bf16[256,2048]{1,0:T(8,128)(2,1)}, u32[]{:S(2)}, u32[]{:S(2)}) %collective-permute-start.54) | collective-permute-done | bytes 1048608 | tf_op jit(solution)/shard_map/ppermute | solution.py:87
  522.7 21.8 %collective-permute-done.56.refs_0_ = bf16[256,2048]{1,0:T(8,128)(2,1)} collective-permute-done((bf16[256,2048]{1,0:T(8,128)(2,1)S(1)}, bf16[256,2048]{1,0:T(8,128)(2,1)}, u32[]{:S(2)}, u32[]{:S(2)}) %collective-permute-start.56) | collective-permute-done | bytes 1048608 | tf_op jit(solution)/shard_map/ppermute | solution.py:87
  548.1 20.6 %shard_map.281 = (f32[4,256]{1,0:T(4,128)}, bf16[2560,2048]{1,0:T(8,128)(2,1)}, bf16[2560,1024]{1,0:T(8,128)(2,1)}, bf16[2560,1024]{1,0:T(8,128)(2,1)}, bf16[2,2...) custom-call(bf16[256,2048]{1,0:T(8,128)(2,1)} %copy-done.27, bf16[256,2048]{1,0:T(8,128)(2,1)} %copy-done.54, ...), custom_call_target="tpu_custom_call" | custom-call | flops 8053063680 | bytes 28311552 | tf_op jit(solution)/shard_map/pallas_call | solution.py:1140
  574.0 24.8 %collective-permute-done.63.refs_0_ = bf16[256,2048]{1,0:T(8,128)(2,1)} collective-permute-done((bf16[256,2048]{1,0:T(8,128)(2,1)S(1)}, bf16[256,2048]{1,0:T(8,128)(2,1)}, u32[]{:S(2)}, u32[]{:S(2)}) %collective-permute-start.63) | collective-permute-done | bytes 1048608 | tf_op jit(solution)/shard_map/ppermute | solution.py:87
  600.7 20.6 %shard_map.282 = (f32[4,256]{1,0:T(4,128)}, bf16[2560,2048]{1,0:T(8,128)(2,1)}, bf16[2560,1024]{1,0:T(8,128)(2,1)}, bf16[2560,1024]{1,0:T(8,128)(2,1)}, bf16[2,2...) custom-call(bf16[256,2048]{1,0:T(8,128)(2,1)} %collective-permute-do, ...), custom_call_target="tpu_custom_call", output_to_operand_aliasing={{1}: (12, {}), {2}: (13, {}), {3}: (14, {})} | custom-call | flops 8053063680 | bytes 28311552 | tf_op jit(solution)/shard_map/pallas_call | solution.py:1140
  626.0 22.1 %shard_map.283 = (f32[4,256]{1,0:T(4,128)}, bf16[2560,2048]{1,0:T(8,128)(2,1)}, bf16[2560,1024]{1,0:T(8,128)(2,1)}, bf16[2560,1024]{1,0:T(8,128)(2,1)}, bf16[2,2...) custom-call(bf16[256,2048]{1,0:T(8,128)(2,1)} %copy-done.60, ...), custom_call_target="tpu_custom_call", output_to_operand_aliasing={{1}: (12, {}), {2}: (13, {}), {3}: (14, {})} | custom-call | flops 8053063680 | bytes 28311552 | tf_op jit(solution)/shard_map/pallas_call | solution.py:1140
  654.1 20.9 %shard_map.284 = (f32[4,256]{1,0:T(4,128)}, bf16[2560,2048]{1,0:T(8,128)(2,1)}, bf16[2560,1024]{1,0:T(8,128)(2,1)}, bf16[2560,1024]{1,0:T(8,128)(2,1)}, bf16[2,2...) custom-call(bf16[256,2048]{1,0:T(8,128)(2,1)} %collective-permute-do, ...), custom_call_target="tpu_custom_call", output_to_operand_aliasing={{1}: (12, {}), {2}: (13, {}), {3}: (14, {})} | custom-call | flops 8053063680 | bytes 28311552 | tf_op jit(solution)/shard_map/pallas_call | solution.py:1140
  687.8 15.9 %fusion.109 = f32[2048,1024]{1,0:T(8,128)S(1)} fusion(bf16[2560,2048]{1,0:T(8,128)(2,1)} %get-tuple-element.346, bf16[2560,1024]{1,0:T(8,128)(2,1)} %get-tuple-element.339), kind=kOutput, calls=%fused_computation.307 | convolution fusion | flops 10737418240 | bytes 24117248 | tf_op jit(solution)/shard_map/dot_general | solution.py:58
  715.7 18.6 %collective-permute-done.76 = bf16[256,2048]{1,0:T(8,128)(2,1)} collective-permute-done((bf16[256,2048]{1,0:T(8,128)(2,1)}, bf16[256,2048]{1,0:T(8,128)(2,1)}, u32[]{:S(2)}, u32[]{:S(2)}) %collective-permute-start.76) | collective-permute-done | bytes 1048608 | tf_op jit(solution)/shard_map/ppermute | solution.py:87
  740.4 14.4 %fusion.110 = f32[2048,1024]{1,0:T(8,128)S(1)} fusion(bf16[2560,2048]{1,0:T(8,128)(2,1)} %get-tuple-element.346, bf16[2560,1024]{1,0:T(8,128)(2,1)S(1)} %bitcast.207), kind=kOutput, calls=%fused_computation.308 | convolution fusion | flops 10737418240 | bytes 24117248 | tf_op jit(solution)/shard_map/dot_general | solution.py:58
  759.7 4.4 collective-permute-done.78
  772.6 18.3 %collective-permute-done.80 = bf16[256,2048]{1,0:T(8,128)(2,1)} collective-permute-done((bf16[256,2048]{1,0:T(8,128)(2,1)}, bf16[256,2048]{1,0:T(8,128)(2,1)}, u32[]{:S(2)}, u32[]{:S(2)}) %collective-permute-start.80) | collective-permute-done | bytes 1048608 | tf_op jit(solution)/shard_map/ppermute | solution.py:87
  793.8 4.0 multiply_reduce_fusion.1
  804.7 4.3 collective-permute-start.84
  809.0 13.7 %collective-permute-done.85 = bf16[256,2048]{1,0:T(8,128)(2,1)} collective-permute-done((bf16[256,2048]{1,0:T(8,128)(2,1)}, bf16[256,2048]{1,0:T(8,128)(2,1)}, u32[]{:S(2)}, u32[]{:S(2)}) %collective-permute-start.85) | collective-permute-done | bytes 1048608 | tf_op jit(solution)/shard_map/ppermute | solution.py:87
  822.6 16.1 %fusion.111 = f32[1024,2048]{1,0:T(8,128)S(1)} fusion(bf16[2560,1024]{1,0:T(8,128)(2,1)} %get-tuple-element.364, bf16[2560,2048]{1,0:T(8,128)(2,1)} %get-tuple-element.365), kind=kOutput, calls=%fused_computation.309 | convolution fusion | flops 10737418240 | bytes 24117248 | tf_op jit(solution)/shard_map/dot_general | solution.py:58
  845.2 4.0 convolution_convert_fusion.5
  851.1 4.0 fusion.53
  862.1 11.2 collective-permute-done.91
  873.3 18.0 %collective-permute-done.92 = bf16[1024,128]{1,0:T(8,128)(2,1)S(1)} collective-permute-done((bf16[1024,128]{1,0:T(8,128)(2,1)S(1)}, bf16[1024,128]{1,0:T(8,128)(2,1)S(1)}, u32[]{:S(2)}, u32[]{:S(2)}) %collective-permute-start.92) | collective-permute-done | bytes 262176 | tf_op jit(solution)/shard_map/ppermute | solution.py:593
  892.4 4.9 shard_map.285
  897.3 38.7 %shard_map.286 = (f32[4096,128]{1,0:T(8,128)}, f32[4096,128]{1,0:T(8,128)}, f32[4096,128]{1,0:T(8,128)}) custom-call(s32[1]{0:T(128)} %copy.191.length_ref, bf16[4096,128]{1,0:T(8,128)(2,1)} %get-tuple-element.247.q_ref, bf16[4096,128]{1,0:T(8,128)(2,1)} %get-tuple-element.358.do_ref, f32[8,4096]{1,0:T(8,128)} %get-tuple-element.359.log_ref, ...), custom_call_target="tpu_custom_call" | custom-call | flops 21474836480 | bytes 10485760 | tf_op jit(solution)/shard_map/pallas_call | solution.py:562
  935.9 10.0 shard_map.287
  946.0 15.5 %collective-permute-start.95 = (f32[2,4096]{1,0:T(2,128)}, f32[2,4096]{1,0:T(2,128)S(1)}, u32[]{:S(2)}, u32[]{:S(2)}) collective-permute-start(f32[2,4096]{1,0:T(2,128)} %get-tuple-element.369), channel_id=1, source_target_pairs={{0,4},{4,0},{8,12},{12,8},{1,5},{5,1},{9,13},{13,9},{2,6},{6,2},{1... | collective-permute-start | bytes 98312 | tf_op jit(solution)/shard_map/ppermute | solution.py:228
  963.9 4.6 add_bitcast_fusion
  975.3 12.1 shard_map.288
  1013.6 11.1 multiply_reduce_fusion
  1028.0 3.7 convert_add_fusion.1
  1034.3 10.2 collective-permute-done.106
  1045.5 4.8 collective-permute-done.105
  1064.9 13.6 %collective-permute-done.112 = f32[3,2048]{1,0:T(4,128)} collective-permute-done((f32[3,2048]{1,0:T(4,128)}, f32[3,2048]{1,0:T(4,128)}, u32[]{:S(2)}, u32[]{:S(2)}) %collective-permute-start.112) | collective-permute-done | bytes 24608 | tf_op jit(solution)/shard_map/ppermute | solution.py:228
  1090.6 10.2 collective-permute-done.109.in_ref
  1107.1 24.1 %collective-permute-start.120 = (bf16[1024,384]{1,0:T(8,128)(2,1)}, bf16[1024,384]{1,0:T(8,128)(2,1)S(1)}, u32[]{:S(2)}, u32[]{:S(2)}) collective-permute-start(bf16[1024,384]{1,0:T(8,128)(2,1)} %collective-permute-done.109.in_ref), channel_id=1, source_target_pairs={{0,16},{16,0},{1,17},{17,1},{2,18},{18,2},{3,19},{19,3},{4,20},{20... | collective-permute-start | bytes 2359304 | tf_op jit(solution)/shard_map/ppermute | solution.py:87
  1135.0 12.4 %collective-permute-done.120.in_ref = bf16[1024,384]{1,0:T(8,128)(2,1)S(1)} collective-permute-done((bf16[1024,384]{1,0:T(8,128)(2,1)}, bf16[1024,384]{1,0:T(8,128)(2,1)S(1)}, u32[]{:S(2)}, u32[]{:S(2)}) %collective-permute-start.120) | collective-permute-done | bytes 786464 | tf_op jit(solution)/shard_map/ppermute | solution.py:87
  1157.1 4.4 add_bitcast_fusion.2
  1174.3 4.0 collective-permute-done.124.in_ref
  1185.4 11.5 collective-permute-done.122
  1199.9 4.3 convert_element_type.464
  (631 shorter events, 328.1 us)
Async XLA Ops:
  16.5 28.2 %collective-permute-start = (bf16[256,2176]{1,0:T(8,128)(2,1)}, bf16[256,2176]{1,0:T(8,128)(2,1)}, u32[]{:S(2)}, u32[]{:S(2)}) collective-permute-start(bf16[256,2176]{1,0:T(8,128)(2,1)} %pad_maximum_fusion.6.refs_0_), channel_id=1, source_target_pairs={{0,4},{4,8},{8,12},{12,0},{1,5},{5,9},{9,13},{13,1},{2,6},{6,10},{... | collective-permute-start | bytes 3342344 | tf_op jit(solution)/shard_map/ppermute | solution.py:87
  18.1 26.6 %collective-permute-start.1 = (bf16[256,2176]{1,0:T(8,128)(2,1)}, bf16[256,2176]{1,0:T(8,128)(2,1)}, u32[]{:S(2)}, u32[]{:S(2)}) collective-permute-start(bf16[256,2176]{1,0:T(8,128)(2,1)} %pad_maximum_fusion.6.refs_0_), channel_id=1, source_target_pairs={{0,2},{1,3},{2,0},{3,1},{4,6},{5,7},{6,4},{7,5},{8,10},{9,11},{10,... | collective-permute-start | bytes 3342344 | tf_op jit(solution)/shard_map/ppermute | solution.py:87
  19.6 46.8 %collective-permute-start.5 = (bf16[2048,512]{1,0:T(8,128)(2,1)}, bf16[2048,512]{1,0:T(8,128)(2,1)}, u32[]{:S(2)}, u32[]{:S(2)}) collective-permute-start(bf16[2048,512]{1,0:T(8,128)(2,1)} %bitcast.2), channel_id=1, source_target_pairs={{0,16},{16,0},{1,17},{17,1},{2,18},{18,2},{3,19},{19,3},{4,20},{20... | collective-permute-start | bytes 6291464 | tf_op jit(solution)/shard_map/ppermute | solution.py:87
  20.1 60.9 %collective-permute-start.8 = (bf16[256,2176]{1,0:T(8,128)(2,1)}, bf16[256,2176]{1,0:T(8,128)(2,1)}, u32[]{:S(2)}, u32[]{:S(2)}) collective-permute-start(bf16[256,2176]{1,0:T(8,128)(2,1)} %pad_maximum_fusion.6.refs_0_), channel_id=1, source_target_pairs={{0,1},{1,0},{2,3},{3,2},{4,5},{5,4},{6,7},{7,6},{8,9},{9,8},{10,11... | collective-permute-start | bytes 3342344 | tf_op jit(solution)/shard_map/ppermute | solution.py:87
  44.8 29.4 %collective-permute-start.2 = (bf16[256,2176]{1,0:T(8,128)(2,1)}, bf16[256,2176]{1,0:T(8,128)(2,1)}, u32[]{:S(2)}, u32[]{:S(2)}) collective-permute-start(bf16[256,2176]{1,0:T(8,128)(2,1)} %collective-permute-done.refs_0_), channel_id=1, source_target_pairs={{0,4},{4,8},{8,12},{12,0},{1,5},{5,9},{9,13},{13,1},{2,6},{6,10},{... | collective-permute-start | bytes 3342344 | tf_op jit(solution)/shard_map/ppermute | solution.py:87
  45.8 28.4 %collective-permute-start.3 = (bf16[256,2176]{1,0:T(8,128)(2,1)}, bf16[256,2176]{1,0:T(8,128)(2,1)}, u32[]{:S(2)}, u32[]{:S(2)}) collective-permute-start(bf16[256,2176]{1,0:T(8,128)(2,1)} %collective-permute-done.refs_0_), channel_id=1, source_target_pairs={{0,2},{1,3},{2,0},{3,1},{4,6},{5,7},{6,4},{7,5},{8,10},{9,11},{10,... | collective-permute-start | bytes 3342344 | tf_op jit(solution)/shard_map/ppermute | solution.py:87
  66.5 46.0 %collective-permute-start.13 = (bf16[2048,512]{1,0:T(8,128)(2,1)}, bf16[2048,512]{1,0:T(8,128)(2,1)}, u32[]{:S(2)}, u32[]{:S(2)}) collective-permute-start(bf16[2048,512]{1,0:T(8,128)(2,1)} %bitcast.213), channel_id=1, source_target_pairs={{0,16},{16,0},{1,17},{17,1},{2,18},{18,2},{3,19},{19,3},{4,20},{20... | collective-permute-start | bytes 6291464 | tf_op jit(solution)/shard_map/ppermute | solution.py:87
  74.1 29.4 %collective-permute-start.6 = (bf16[256,2176]{1,0:T(8,128)(2,1)}, bf16[256,2176]{1,0:T(8,128)(2,1)}, u32[]{:S(2)}, u32[]{:S(2)}) collective-permute-start(bf16[256,2176]{1,0:T(8,128)(2,1)} %collective-permute-done.2.refs_0_), channel_id=1, source_target_pairs={{0,4},{4,8},{8,12},{12,0},{1,5},{5,9},{9,13},{13,1},{2,6},{6,10},{... | collective-permute-start | bytes 3342344 | tf_op jit(solution)/shard_map/ppermute | solution.py:87
  76.0 27.5 %collective-permute-start.7 = (bf16[256,2176]{1,0:T(8,128)(2,1)}, bf16[256,2176]{1,0:T(8,128)(2,1)}, u32[]{:S(2)}, u32[]{:S(2)}) collective-permute-start(bf16[256,2176]{1,0:T(8,128)(2,1)} %collective-permute-done.2.refs_0_), channel_id=1, source_target_pairs={{0,2},{1,3},{2,0},{3,1},{4,6},{5,7},{6,4},{7,5},{8,10},{9,11},{10,... | collective-permute-start | bytes 3342344 | tf_op jit(solution)/shard_map/ppermute | solution.py:87
  81.1 32.5 %collective-permute-start.11 = (bf16[256,2176]{1,0:T(8,128)(2,1)}, bf16[256,2176]{1,0:T(8,128)(2,1)}, u32[]{:S(2)}, u32[]{:S(2)}) collective-permute-start(bf16[256,2176]{1,0:T(8,128)(2,1)} %collective-permute-done.refs_0_), channel_id=1, source_target_pairs={{0,1},{1,0},{2,3},{3,2},{4,5},{5,4},{6,7},{7,6},{8,9},{9,8},{10,11... | collective-permute-start | bytes 3342344 | tf_op jit(solution)/shard_map/ppermute | solution.py:87
  81.2 32.9 %collective-permute-start.12 = (bf16[256,2176]{1,0:T(8,128)(2,1)}, bf16[256,2176]{1,0:T(8,128)(2,1)}, u32[]{:S(2)}, u32[]{:S(2)}) collective-permute-start(bf16[256,2176]{1,0:T(8,128)(2,1)} %collective-permute-done.3.refs_1_), channel_id=1, source_target_pairs={{0,1},{1,0},{2,3},{3,2},{4,5},{5,4},{6,7},{7,6},{8,9},{9,8},{10,11... | collective-permute-start | bytes 3342344 | tf_op jit(solution)/shard_map/ppermute | solution.py:87
  103.5 26.4 %collective-permute-start.10 = (bf16[256,2176]{1,0:T(8,128)(2,1)}, bf16[256,2176]{1,0:T(8,128)(2,1)S(1)}, u32[]{:S(2)}, u32[]{:S(2)}) collective-permute-start(bf16[256,2176]{1,0:T(8,128)(2,1)} %collective-permute-done.6.refs_0_), channel_id=1, source_target_pairs={{0,2},{1,3},{2,0},{3,1},{4,6},{5,7},{6,4},{7,5},{8,10},{9,11},{10,... | collective-permute-start | bytes 3342344 | tf_op jit(solution)/shard_map/ppermute | solution.py:87
  112.5 44.8 %collective-permute-start.18 = (bf16[512,2048]{1,0:T(8,128)(2,1)S(1)}, bf16[512,2048]{1,0:T(8,128)(2,1)S(1)}, u32[]{:S(2)}, u32[]{:S(2)}) collective-permute-start(bf16[512,2048]{1,0:T(8,128)(2,1)S(1)} %bitcast.215), channel_id=1, source_target_pairs={{0,16},{16,0},{1,17},{17,1},{2,18},{18,2},{3,19},{19,3},{4,20},{20... | collective-permute-start | bytes 6291464 | tf_op jit(solution)/shard_map/ppermute | solution.py:87
  113.6 27.5 %collective-permute-start.14 = (bf16[256,2176]{1,0:T(8,128)(2,1)}, bf16[256,2176]{1,0:T(8,128)(2,1)S(1)}, u32[]{:S(2)}, u32[]{:S(2)}) collective-permute-start(bf16[256,2176]{1,0:T(8,128)(2,1)} %collective-permute-done.6.refs_0_), channel_id=1, source_target_pairs={{0,1},{1,0},{2,3},{3,2},{4,5},{5,4},{6,7},{7,6},{8,9},{9,8},{10,11... | collective-permute-start | bytes 3342344 | tf_op jit(solution)/shard_map/ppermute | solution.py:87
  270.7 26.6 %collective-permute-start.30 = (bf16[256,2048]{1,0:T(8,128)(2,1)S(1)}, bf16[256,2048]{1,0:T(8,128)(2,1)S(1)}, u32[]{:S(2)}, u32[]{:S(2)}) collective-permute-start(bf16[256,2048]{1,0:T(8,128)(2,1)S(1)} %multiply_convert_fusion.refs_0_), channel_id=1, source_target_pairs={{0,4},{4,8},{8,12},{12,0},{1,5},{5,9},{9,13},{13,1},{2,6},{6,10},{... | collective-permute-start | bytes 3145736 | tf_op jit(solution)/shard_map/ppermute | solution.py:87
  271.0 26.3 %collective-permute-start.31 = (bf16[256,2048]{1,0:T(8,128)(2,1)S(1)}, bf16[256,2048]{1,0:T(8,128)(2,1)S(1)}, u32[]{:S(2)}, u32[]{:S(2)}) collective-permute-start(bf16[256,2048]{1,0:T(8,128)(2,1)S(1)} %multiply_convert_fusion.refs_0_), channel_id=1, source_target_pairs={{0,2},{1,3},{2,0},{3,1},{4,6},{5,7},{6,4},{7,5},{8,10},{9,11},{10,... | collective-permute-start | bytes 3145736 | tf_op jit(solution)/shard_map/ppermute | solution.py:87
  299.3 26.7 %collective-permute-start.32 = (bf16[256,2048]{1,0:T(8,128)(2,1)S(1)}, bf16[256,2048]{1,0:T(8,128)(2,1)S(1)}, u32[]{:S(2)}, u32[]{:S(2)}) collective-permute-start(bf16[256,2048]{1,0:T(8,128)(2,1)S(1)} %multiply_convert_fusion.refs_0_), channel_id=1, source_target_pairs={{0,1},{1,0},{2,3},{3,2},{4,5},{5,4},{6,7},{7,6},{8,9},{9,8},{10,11... | collective-permute-start | bytes 3145736 | tf_op jit(solution)/shard_map/ppermute | solution.py:87
  299.4 28.7 %collective-permute-start.33 = (bf16[256,2048]{1,0:T(8,128)(2,1)S(1)}, bf16[256,2048]{1,0:T(8,128)(2,1)}, u32[]{:S(2)}, u32[]{:S(2)}) collective-permute-start(bf16[256,2048]{1,0:T(8,128)(2,1)S(1)} %collective-permute-done.31.refs_1_), channel_id=1, source_target_pairs={{0,1},{1,0},{2,3},{3,2},{4,5},{5,4},{6,7},{7,6},{8,9},{9,8},{10,11... | collective-permute-start | bytes 3145736 | tf_op jit(solution)/shard_map/ppermute | solution.py:87
  301.6 47.2 %collective-permute-start.40 = (bf16[256,2048]{1,0:T(8,128)(2,1)S(1)}, bf16[256,2048]{1,0:T(8,128)(2,1)}, u32[]{:S(2)}, u32[]{:S(2)}) collective-permute-start(bf16[256,2048]{1,0:T(8,128)(2,1)S(1)} %collective-permute-done.30.refs_0_), channel_id=1, source_target_pairs={{0,1},{1,0},{2,3},{3,2},{4,5},{5,4},{6,7},{7,6},{8,9},{9,8},{10,11... | collective-permute-start | bytes 3145736 | tf_op jit(solution)/shard_map/ppermute | solution.py:87
  325.8 44.8 %collective-permute-start.37 = (bf16[256,2048]{1,0:T(8,128)(2,1)S(1)}, bf16[256,2048]{1,0:T(8,128)(2,1)S(1)}, u32[]{:S(2)}, u32[]{:S(2)}) collective-permute-start(bf16[256,2048]{1,0:T(8,128)(2,1)S(1)} %collective-permute-done.35.refs_0_), channel_id=1, source_target_pairs={{0,4},{4,8},{8,12},{12,0},{1,5},{5,9},{9,13},{13,1},{2,6},{6,10},{... | collective-permute-start | bytes 3145736 | tf_op jit(solution)/shard_map/ppermute | solution.py:87
  327.0 43.6 %collective-permute-start.38 = (bf16[256,2048]{1,0:T(8,128)(2,1)S(1)}, bf16[256,2048]{1,0:T(8,128)(2,1)}, u32[]{:S(2)}, u32[]{:S(2)}) collective-permute-start(bf16[256,2048]{1,0:T(8,128)(2,1)S(1)} %collective-permute-done.35.refs_0_), channel_id=1, source_target_pairs={{0,2},{1,3},{2,0},{3,1},{4,6},{5,7},{6,4},{7,5},{8,10},{9,11},{10,... | collective-permute-start | bytes 3145736 | tf_op jit(solution)/shard_map/ppermute | solution.py:87
  370.0 31.6 %collective-permute-start.48 = (bf16[2,256,2048]{2,1,0:T(8,128)(2,1)}, bf16[2,256,2048]{2,1,0:T(8,128)(2,1)S(1)}, u32[]{:S(2)}, u32[]{:S(2)}) collective-permute-start(bf16[2,256,2048]{2,1,0:T(8,128)(2,1)} %get-tuple-element.272), channel_id=1, source_target_pairs={{0,1},{1,0},{2,3},{3,2},{4,5},{5,4},{6,7},{7,6},{8,9},{9,8},{10,11... | collective-permute-start | bytes 6291464 | tf_op jit(solution)/shard_map/ppermute | solution.py:87
  370.8 30.6 %collective-permute-start.39 = (bf16[256,2048]{1,0:T(8,128)(2,1)S(1)}, bf16[256,2048]{1,0:T(8,128)(2,1)}, u32[]{:S(2)}, u32[]{:S(2)}) collective-permute-start(bf16[256,2048]{1,0:T(8,128)(2,1)S(1)} %collective-permute-done.37.refs_0_), channel_id=1, source_target_pairs={{0,2},{1,3},{2,0},{3,1},{4,6},{5,7},{6,4},{7,5},{8,10},{9,11},{10,... | collective-permute-start | bytes 3145736 | tf_op jit(solution)/shard_map/ppermute | solution.py:87
  371.7 36.4 %collective-permute-start.42 = (bf16[256,2048]{1,0:T(8,128)(2,1)S(1)}, bf16[256,2048]{1,0:T(8,128)(2,1)}, u32[]{:S(2)}, u32[]{:S(2)}) collective-permute-start(bf16[256,2048]{1,0:T(8,128)(2,1)S(1)} %collective-permute-done.37.refs_0_), channel_id=1, source_target_pairs={{0,1},{1,0},{2,3},{3,2},{4,5},{5,4},{6,7},{7,6},{8,9},{9,8},{10,11... | collective-permute-start | bytes 3145736 | tf_op jit(solution)/shard_map/ppermute | solution.py:87
  401.0 33.4 %collective-permute-start.47 = (bf16[2,256,2048]{2,1,0:T(8,128)(2,1)}, bf16[2,256,2048]{2,1,0:T(8,128)(2,1)}, u32[]{:S(2)}, u32[]{:S(2)}) collective-permute-start(bf16[2,256,2048]{2,1,0:T(8,128)(2,1)} %get-tuple-element.290), channel_id=1, source_target_pairs={{0,1},{1,0},{2,3},{3,2},{4,5},{5,4},{6,7},{7,6},{8,9},{9,8},{10,11... | collective-permute-start | bytes 6291464 | tf_op jit(solution)/shard_map/ppermute | solution.py:87
  429.3 37.0 %collective-permute-start.34 = (bf16[2,256,2048]{2,1,0:T(8,128)(2,1)}, bf16[2,256,2048]{2,1,0:T(8,128)(2,1)S(1)}, u32[]{:S(2)}, u32[]{:S(2)}) collective-permute-start(bf16[2,256,2048]{2,1,0:T(8,128)(2,1)} %get-tuple-element.261), channel_id=1, source_target_pairs={{0,1},{1,0},{2,3},{3,2},{4,5},{5,4},{6,7},{7,6},{8,9},{9,8},{10,11... | collective-permute-start | bytes 6291464 | tf_op jit(solution)/shard_map/ppermute | solution.py:87
  437.9 26.2 %collective-permute-start.51 = (bf16[256,2048]{1,0:T(8,128)(2,1)S(1)}, bf16[256,2048]{1,0:T(8,128)(2,1)S(1)}, u32[]{:S(2)}, u32[]{:S(2)}) collective-permute-start(bf16[256,2048]{1,0:T(8,128)(2,1)S(1)} %fusion.28), channel_id=1, source_target_pairs={{0,4},{4,8},{8,12},{12,0},{1,5},{5,9},{9,13},{13,1},{2,6},{6,10},{... | collective-permute-start | bytes 3145736 | tf_op jit(solution)/shard_map/ppermute | solution.py:87
  544.5 27.6 %collective-permute-start.61 = (bf16[256,2048]{1,0:T(8,128)(2,1)}, bf16[256,2048]{1,0:T(8,128)(2,1)S(1)}, u32[]{:S(2)}, u32[]{:S(2)}) collective-permute-start(bf16[256,2048]{1,0:T(8,128)(2,1)} %collective-permute-done.56.refs_0_), channel_id=1, source_target_pairs={{0,4},{4,8},{8,12},{12,0},{1,5},{5,9},{9,13},{13,1},{2,6},{6,10},{... | collective-permute-start | bytes 3145736 | tf_op jit(solution)/shard_map/ppermute | solution.py:87
  544.6 27.5 %collective-permute-start.62 = (bf16[256,2048]{1,0:T(8,128)(2,1)}, bf16[256,2048]{1,0:T(8,128)(2,1)}, u32[]{:S(2)}, u32[]{:S(2)}) collective-permute-start(bf16[256,2048]{1,0:T(8,128)(2,1)} %collective-permute-done.56.refs_0_), channel_id=1, source_target_pairs={{0,2},{1,3},{2,0},{3,1},{4,6},{5,7},{6,4},{7,5},{8,10},{9,11},{10,... | collective-permute-start | bytes 3145736 | tf_op jit(solution)/shard_map/ppermute | solution.py:87
  568.8 54.0 %collective-permute-start.60 = (bf16[2,256,2048]{2,1,0:T(8,128)(2,1)}, bf16[2,256,2048]{2,1,0:T(8,128)(2,1)}, u32[]{:S(2)}, u32[]{:S(2)}) collective-permute-start(bf16[2,256,2048]{2,1,0:T(8,128)(2,1)} %get-tuple-element.305), channel_id=1, source_target_pairs={{0,1},{1,0},{2,3},{3,2},{4,5},{5,4},{6,7},{7,6},{8,9},{9,8},{10,11... | collective-permute-start | bytes 6291464 | tf_op jit(solution)/shard_map/ppermute | solution.py:87
  572.1 26.8 %collective-permute-start.63 = (bf16[256,2048]{1,0:T(8,128)(2,1)S(1)}, bf16[256,2048]{1,0:T(8,128)(2,1)}, u32[]{:S(2)}, u32[]{:S(2)}) collective-permute-start(bf16[256,2048]{1,0:T(8,128)(2,1)S(1)} %collective-permute-done.61.refs_0_), channel_id=1, source_target_pairs={{0,4},{4,8},{8,12},{12,0},{1,5},{5,9},{9,13},{13,1},{2,6},{6,10},{... | collective-permute-start | bytes 3145736 | tf_op jit(solution)/shard_map/ppermute | solution.py:87
  572.3 26.6 %collective-permute-start.64 = (bf16[256,2048]{1,0:T(8,128)(2,1)S(1)}, bf16[256,2048]{1,0:T(8,128)(2,1)}, u32[]{:S(2)}, u32[]{:S(2)}) collective-permute-start(bf16[256,2048]{1,0:T(8,128)(2,1)S(1)} %collective-permute-done.61.refs_0_), channel_id=1, source_target_pairs={{0,2},{1,3},{2,0},{3,1},{4,6},{5,7},{6,4},{7,5},{8,10},{9,11},{10,... | collective-permute-start | bytes 3145736 | tf_op jit(solution)/shard_map/ppermute | solution.py:87
  598.9 27.1 %collective-permute-start.70 = (bf16[256,2048]{1,0:T(8,128)(2,1)S(1)}, bf16[256,2048]{1,0:T(8,128)(2,1)}, u32[]{:S(2)}, u32[]{:S(2)}) collective-permute-start(bf16[256,2048]{1,0:T(8,128)(2,1)S(1)} %collective-permute-done.61.refs_0_), channel_id=1, source_target_pairs={{0,1},{1,0},{2,3},{3,2},{4,5},{5,4},{6,7},{7,6},{8,9},{9,8},{10,11... | collective-permute-start | bytes 3145736 | tf_op jit(solution)/shard_map/ppermute | solution.py:87
  598.9 27.1 %collective-permute-start.71 = (bf16[256,2048]{1,0:T(8,128)(2,1)}, bf16[256,2048]{1,0:T(8,128)(2,1)}, u32[]{:S(2)}, u32[]{:S(2)}) collective-permute-start(bf16[256,2048]{1,0:T(8,128)(2,1)} %collective-permute-done.64.refs_1_), channel_id=1, source_target_pairs={{0,1},{1,0},{2,3},{3,2},{4,5},{5,4},{6,7},{7,6},{8,9},{9,8},{10,11... | collective-permute-start | bytes 3145736 | tf_op jit(solution)/shard_map/ppermute | solution.py:87
  621.4 28.4 %collective-permute-start.74 = (bf16[2,256,2048]{2,1,0:T(8,128)(2,1)}, bf16[2,256,2048]{2,1,0:T(8,128)(2,1)}, u32[]{:S(2)}, u32[]{:S(2)}) collective-permute-start(bf16[2,256,2048]{2,1,0:T(8,128)(2,1)} %get-tuple-element.328), channel_id=1, source_target_pairs={{0,1},{1,0},{2,3},{3,2},{4,5},{5,4},{6,7},{7,6},{8,9},{9,8},{10,11... | collective-permute-start | bytes 6291464 | tf_op jit(solution)/shard_map/ppermute | solution.py:87
  621.5 28.2 %collective-permute-start.65 = (bf16[256,2048]{1,0:T(8,128)(2,1)}, bf16[256,2048]{1,0:T(8,128)(2,1)}, u32[]{:S(2)}, u32[]{:S(2)}) collective-permute-start(bf16[256,2048]{1,0:T(8,128)(2,1)} %collective-permute-done.63.refs_0_), channel_id=1, source_target_pairs={{0,2},{1,3},{2,0},{3,1},{4,6},{5,7},{6,4},{7,5},{8,10},{9,11},{10,... | collective-permute-start | bytes 3145736 | tf_op jit(solution)/shard_map/ppermute | solution.py:87
  622.7 30.4 %collective-permute-start.68 = (bf16[256,2048]{1,0:T(8,128)(2,1)}, bf16[256,2048]{1,0:T(8,128)(2,1)}, u32[]{:S(2)}, u32[]{:S(2)}) collective-permute-start(bf16[256,2048]{1,0:T(8,128)(2,1)} %collective-permute-done.63.refs_0_), channel_id=1, source_target_pairs={{0,1},{1,0},{2,3},{3,2},{4,5},{5,4},{6,7},{7,6},{8,9},{9,8},{10,11... | collective-permute-start | bytes 3145736 | tf_op jit(solution)/shard_map/ppermute | solution.py:87
  648.1 28.1 %collective-permute-start.73 = (bf16[2,256,2048]{2,1,0:T(8,128)(2,1)}, bf16[2,256,2048]{2,1,0:T(8,128)(2,1)}, u32[]{:S(2)}, u32[]{:S(2)}) collective-permute-start(bf16[2,256,2048]{2,1,0:T(8,128)(2,1)} %get-tuple-element.326), channel_id=1, source_target_pairs={{0,1},{1,0},{2,3},{3,2},{4,5},{5,4},{6,7},{7,6},{8,9},{9,8},{10,11... | collective-permute-start | bytes 6291464 | tf_op jit(solution)/shard_map/ppermute | solution.py:87
  652.3 28.2 %collective-permute-start.75 = (bf16[256,2048]{1,0:T(8,128)(2,1)S(1)}, bf16[256,2048]{1,0:T(8,128)(2,1)}, u32[]{:S(2)}, u32[]{:S(2)}) collective-permute-start(bf16[256,2048]{1,0:T(8,128)(2,1)S(1)} %fusion.47), channel_id=1, source_target_pairs={{0,2},{1,3},{2,0},{3,1},{4,6},{5,7},{6,4},{7,5},{8,10},{9,11},{10,... | collective-permute-start | bytes 3145736 | tf_op jit(solution)/shard_map/ppermute | solution.py:87
  675.0 37.3 %collective-permute-start.72 = (bf16[2,256,2048]{2,1,0:T(8,128)(2,1)}, bf16[2,256,2048]{2,1,0:T(8,128)(2,1)}, u32[]{:S(2)}, u32[]{:S(2)}) collective-permute-start(bf16[2,256,2048]{2,1,0:T(8,128)(2,1)} %get-tuple-element.324), channel_id=1, source_target_pairs={{0,1},{1,0},{2,3},{3,2},{4,5},{5,4},{6,7},{7,6},{8,9},{9,8},{10,11... | collective-permute-start | bytes 6291464 | tf_op jit(solution)/shard_map/ppermute | solution.py:87
  684.3 28.1 %all-to-all-start = ((f32[16,1,256]{2,1,0:T(1,128)}), f32[16,1,256]{2,1,0:T(1,128)S(1)}, u32[]{:S(2)}, u32[]{:S(2)}) async-start(f32[16,1,256]{2,1,0:T(1,128)} %copy.109), calls=%async_computation | async-start | bytes 32768 | tf_op jit(solution)/shard_map/all_to_all | solution.py:1400
  687.8 512.2 %all-reduce.4.cloned.1.call-start = ((), (), s32[]{:S(2)}) async-start(), calls=%async_computation.1 | async-start | bytes 4194304 | tf_op jit(solution)/shard_map/psum | solution.py:714
  710.4 27.4 %collective-permute-start.77 = (bf16[256,2048]{1,0:T(8,128)(2,1)}, bf16[256,2048]{1,0:T(8,128)(2,1)}, u32[]{:S(2)}, u32[]{:S(2)}) collective-permute-start(bf16[256,2048]{1,0:T(8,128)(2,1)} %fusion.20), channel_id=1, source_target_pairs={{0,4},{4,8},{8,12},{12,0},{1,5},{5,9},{9,13},{13,1},{2,6},{6,10},{... | collective-permute-start | bytes 3145736 | tf_op jit(solution)/shard_map/ppermute | solution.py:87
  804.5 38.4 %collective-permute-start.82 = (f32[18,2048]{1,0:T(8,128)S(1)}, f32[18,2048]{1,0:T(8,128)S(1)}, u32[]{:S(2)}, u32[]{:S(2)}) collective-permute-start(f32[18,2048]{1,0:T(8,128)S(1)} %maximum_maximum_fusion), channel_id=1, source_target_pairs={{0,4},{4,0},{8,12},{12,8},{1,5},{5,1},{9,13},{13,9},{2,6},{6,2},{1... | collective-permute-start | bytes 442376 | tf_op jit(solution)/shard_map/ppermute | solution.py:228
  804.6 38.8 %collective-permute-start.83 = (f32[18,2048]{1,0:T(8,128)S(1)}, f32[18,2048]{1,0:T(8,128)S(1)}, u32[]{:S(2)}, u32[]{:S(2)}) collective-permute-start(f32[18,2048]{1,0:T(8,128)S(1)} %maximum_maximum_fusion), channel_id=1, source_target_pairs={{0,8},{4,12},{8,0},{12,4},{1,9},{5,13},{9,1},{13,5},{2,10},{6,14},... | collective-permute-start | bytes 442376 | tf_op jit(solution)/shard_map/ppermute | solution.py:228
  804.7 40.3 %collective-permute-start.84 = (f32[18,2048]{1,0:T(8,128)S(1)}, f32[18,2048]{1,0:T(8,128)S(1)}, u32[]{:S(2)}, u32[]{:S(2)}) collective-permute-start(f32[18,2048]{1,0:T(8,128)S(1)} %maximum_maximum_fusion), channel_id=1, source_target_pairs={{0,12},{4,8},{8,4},{12,0},{1,13},{5,9},{9,5},{13,1},{2,14},{6,10},... | collective-permute-start | bytes 442376 | tf_op jit(solution)/shard_map/ppermute | solution.py:228
  809.0 36.1 %collective-permute-start.87 = (bf16[256,2048]{1,0:T(8,128)(2,1)}, bf16[256,2048]{1,0:T(8,128)(2,1)S(1)}, u32[]{:S(2)}, u32[]{:S(2)}) collective-permute-start(bf16[256,2048]{1,0:T(8,128)(2,1)} %get-tuple-element.429), channel_id=1, source_target_pairs={{0,1},{1,0},{2,3},{3,2},{4,5},{5,4},{6,7},{7,6},{8,9},{9,8},{10,11... | collective-permute-start | bytes 3145736 | tf_op jit(solution)/shard_map/ppermute | solution.py:87
  842.9 120.9 %collective-permute-start.129 = (bf16[512,2048]{1,0:T(8,128)(2,1)}, bf16[512,2048]{1,0:T(8,128)(2,1)}, u32[]{:S(2)}, u32[]{:S(2)}) collective-permute-start(bf16[512,2048]{1,0:T(8,128)(2,1)} %split.64), channel_id=1, source_target_pairs={{0,16},{16,0},{1,17},{17,1},{2,18},{18,2},{3,19},{19,3},{4,20},{20... | collective-permute-start | bytes 6291464 | tf_op jit(solution)/shard_map/ppermute | solution.py:87
  843.4 127.8 %collective-permute-start.128 = (bf16[2048,512]{1,0:T(8,128)(2,1)}, bf16[2048,512]{1,0:T(8,128)(2,1)S(1)}, u32[]{:S(2)}, u32[]{:S(2)}) collective-permute-start(bf16[2048,512]{1,0:T(8,128)(2,1)} %split.60), channel_id=1, source_target_pairs={{0,16},{16,0},{1,17},{17,1},{2,18},{18,2},{3,19},{19,3},{4,20},{20... | collective-permute-start | bytes 6291464 | tf_op jit(solution)/shard_map/ppermute | solution.py:87
  857.1 34.2 %collective-permute-start.92 = (bf16[1024,128]{1,0:T(8,128)(2,1)S(1)}, bf16[1024,128]{1,0:T(8,128)(2,1)S(1)}, u32[]{:S(2)}, u32[]{:S(2)}) collective-permute-start(bf16[1024,128]{1,0:T(8,128)(2,1)S(1)} %get-tuple-element.446), channel_id=1, source_target_pairs={{0,8},{4,12},{8,0},{12,4},{1,9},{5,13},{9,1},{13,5},{2,10},{6,14},... | collective-permute-start | bytes 786440 | tf_op jit(solution)/shard_map/ppermute | solution.py:593
  860.4 31.0 %collective-permute-start.93 = (bf16[1024,128]{1,0:T(8,128)(2,1)S(1)}, bf16[1024,128]{1,0:T(8,128)(2,1)S(1)}, u32[]{:S(2)}, u32[]{:S(2)}) collective-permute-start(bf16[1024,128]{1,0:T(8,128)(2,1)S(1)} %get-tuple-element.445), channel_id=1, source_target_pairs={{0,12},{4,0},{8,4},{12,8},{1,13},{5,1},{9,5},{13,9},{2,14},{6,2},{... | collective-permute-start | bytes 786440 | tf_op jit(solution)/shard_map/ppermute | solution.py:593
  992.6 34.1 %collective-permute-start.103 = (bf16[2,256,2048]{2,1,0:T(8,128)(2,1)}, bf16[2,256,2048]{2,1,0:T(8,128)(2,1)S(1)}, u32[]{:S(2)}, u32[]{:S(2)}) collective-permute-start(bf16[2,256,2048]{2,1,0:T(8,128)(2,1)} %bitcast.41), channel_id=1, source_target_pairs={{0,1},{1,0},{2,3},{3,2},{4,5},{5,4},{6,7},{7,6},{8,9},{9,8},{10,11... | collective-permute-start | bytes 6291464 | tf_op jit(solution)/shard_map/ppermute | solution.py:87
  995.7 58.0 %collective-permute-start.102 = (bf16[2,256,2048]{2,1,0:T(8,128)(2,1)}, bf16[2,256,2048]{2,1,0:T(8,128)(2,1)}, u32[]{:S(2)}, u32[]{:S(2)}) collective-permute-start(bf16[2,256,2048]{2,1,0:T(8,128)(2,1)} %bitcast.37), channel_id=1, source_target_pairs={{0,1},{1,0},{2,3},{3,2},{4,5},{5,4},{6,7},{7,6},{8,9},{9,8},{10,11... | collective-permute-start | bytes 6291464 | tf_op jit(solution)/shard_map/ppermute | solution.py:87
  998.3 104.2 %collective-permute-start.101 = (bf16[2,256,2048]{2,1,0:T(8,128)(2,1)}, bf16[2,256,2048]{2,1,0:T(8,128)(2,1)S(1)}, u32[]{:S(2)}, u32[]{:S(2)}) collective-permute-start(bf16[2,256,2048]{2,1,0:T(8,128)(2,1)} %bitcast.33), channel_id=1, source_target_pairs={{0,1},{1,0},{2,3},{3,2},{4,5},{5,4},{6,7},{7,6},{8,9},{9,8},{10,11... | collective-permute-start | bytes 6291464 | tf_op jit(solution)/shard_map/ppermute | solution.py:87
  1052.8 34.1 %collective-permute-start.107 = (bf16[256,2048]{1,0:T(8,128)(2,1)}, bf16[256,2048]{1,0:T(8,128)(2,1)S(1)}, u32[]{:S(2)}, u32[]{:S(2)}) collective-permute-start(bf16[256,2048]{1,0:T(8,128)(2,1)} %fusion.50), channel_id=1, source_target_pairs={{0,2},{1,3},{2,0},{3,1},{4,6},{5,7},{6,4},{7,5},{8,10},{9,11},{10,... | collective-permute-start | bytes 3145736 | tf_op jit(solution)/shard_map/ppermute | solution.py:87
  1053.8 34.2 %collective-permute-start.108 = (bf16[256,2048]{1,0:T(8,128)(2,1)}, bf16[256,2048]{1,0:T(8,128)(2,1)}, u32[]{:S(2)}, u32[]{:S(2)}) collective-permute-start(bf16[256,2048]{1,0:T(8,128)(2,1)} %fusion.7), channel_id=1, source_target_pairs={{0,4},{4,8},{8,12},{12,0},{1,5},{5,9},{9,13},{13,1},{2,6},{6,10},{... | collective-permute-start | bytes 3145736 | tf_op jit(solution)/shard_map/ppermute | solution.py:87
  1082.3 74.5 %collective-permute-start.127 = (bf16[2048,512]{1,0:T(8,128)(2,1)}, bf16[2048,512]{1,0:T(8,128)(2,1)}, u32[]{:S(2)}, u32[]{:S(2)}) collective-permute-start(bf16[2048,512]{1,0:T(8,128)(2,1)} %split.58), channel_id=1, source_target_pairs={{0,16},{16,0},{1,17},{17,1},{2,18},{18,2},{3,19},{19,3},{4,20},{20... | collective-permute-start | bytes 6291464 | tf_op jit(solution)/shard_map/ppermute | solution.py:87
  1101.4 50.6 %collective-permute-start.114 = (bf16[256,2048]{1,0:T(8,128)(2,1)}, bf16[256,2048]{1,0:T(8,128)(2,1)}, u32[]{:S(2)}, u32[]{:S(2)}) collective-permute-start(bf16[256,2048]{1,0:T(8,128)(2,1)} %fusion.49), channel_id=1, source_target_pairs={{0,2},{1,3},{2,0},{3,1},{4,6},{5,7},{6,4},{7,5},{8,10},{9,11},{10,... | collective-permute-start | bytes 3145736 | tf_op jit(solution)/shard_map/ppermute | solution.py:87
  1102.5 49.5 %collective-permute-start.115 = (bf16[256,2048]{1,0:T(8,128)(2,1)S(1)}, bf16[256,2048]{1,0:T(8,128)(2,1)}, u32[]{:S(2)}, u32[]{:S(2)}) collective-permute-start(bf16[256,2048]{1,0:T(8,128)(2,1)S(1)} %fusion.10), channel_id=1, source_target_pairs={{0,4},{4,8},{8,12},{12,0},{1,5},{5,9},{9,13},{13,1},{2,6},{6,10},{... | collective-permute-start | bytes 3145736 | tf_op jit(solution)/shard_map/ppermute | solution.py:87
  1105.1 29.2 %collective-permute-start.119 = (f32[3,2048]{1,0:T(4,128)S(1)}, f32[3,2048]{1,0:T(4,128)S(1)}, u32[]{:S(2)}, u32[]{:S(2)}) collective-permute-start(f32[3,2048]{1,0:T(4,128)S(1)} %copy-done.83), channel_id=1, source_target_pairs={{0,12},{4,8},{8,4},{12,0},{1,13},{5,9},{9,5},{13,1},{2,14},{6,10},... | collective-permute-start | bytes 73736 | tf_op jit(solution)/shard_map/ppermute | solution.py:228
  1107.1 40.3 %collective-permute-start.120 = (bf16[1024,384]{1,0:T(8,128)(2,1)}, bf16[1024,384]{1,0:T(8,128)(2,1)S(1)}, u32[]{:S(2)}, u32[]{:S(2)}) collective-permute-start(bf16[1024,384]{1,0:T(8,128)(2,1)} %collective-permute-done.109.in_ref), channel_id=1, source_target_pairs={{0,16},{16,0},{1,17},{17,1},{2,18},{18,2},{3,19},{19,3},{4,20},{20... | collective-permute-start | bytes 2359304 | tf_op jit(solution)/shard_map/ppermute | solution.py:87
  1155.9 29.5 %collective-permute-start.121 = (bf16[256,2048]{1,0:T(8,128)(2,1)S(1)}, bf16[256,2048]{1,0:T(8,128)(2,1)S(1)}, u32[]{:S(2)}, u32[]{:S(2)}) collective-permute-start(bf16[256,2048]{1,0:T(8,128)(2,1)S(1)} %fusion.48), channel_id=1, source_target_pairs={{0,2},{1,3},{2,0},{3,1},{4,6},{5,7},{6,4},{7,5},{8,10},{9,11},{10,... | collective-permute-start | bytes 3145736 | tf_op jit(solution)/shard_map/ppermute | solution.py:87
  1156.8 40.1 %collective-permute-start.122 = (bf16[256,2048]{1,0:T(8,128)(2,1)S(1)}, bf16[256,2048]{1,0:T(8,128)(2,1)}, u32[]{:S(2)}, u32[]{:S(2)}) collective-permute-start(bf16[256,2048]{1,0:T(8,128)(2,1)S(1)} %fusion.13), channel_id=1, source_target_pairs={{0,4},{4,8},{8,12},{12,0},{1,5},{5,9},{9,13},{13,1},{2,6},{6,10},{... | collective-permute-start | bytes 3145736 | tf_op jit(solution)/shard_map/ppermute | solution.py:87
  1178.3 29.5 %collective-permute-start.125 = (bf16[1024,384]{1,0:T(8,128)(2,1)S(1)}, bf16[1024,384]{1,0:T(8,128)(2,1)}, u32[]{:S(2)}, u32[]{:S(2)}) collective-permute-start(bf16[1024,384]{1,0:T(8,128)(2,1)S(1)} %collective-permute-done.124.in_ref), channel_id=1, source_target_pairs={{0,16},{16,0},{1,17},{17,1},{2,18},{18,2},{3,19},{19,3},{4,20},{20... | collective-permute-start | bytes 2359304 | tf_op jit(solution)/shard_map/ppermute | solution.py:87
  (183 other events, 2565.7 us)
Sparse Core Ops, SparseCore 0:
  857.0 127.8 all-reduce.3

commit v3 on v2

--- a/solution.py
+++ b/solution.py
@@ -21,6 +21,12 @@
 TOKEN_AXES = ("context", "expert")
 ALL_AXES = ("dp", "context", "expert")
 VMEM_LIMIT = 56 * 2**20
+
+
+def takes(microseconds):
+    return pl.CostEstimate(
+        flops=int(microseconds * 1.1e9), bytes_accessed=int(microseconds * 3e6), transcendentals=0
+    )
 
 
 def rms_scale(values):
@@ -167,8 +173,11 @@
     return results, done
 
 
-def scatter_expert(kept, sent, waiting=None, beside=()):
-    terms = kept.astype(jnp.float32) + partner(low(sent)).astype(jnp.float32)
+def core_sum(kept, sent):
+    return kept.astype(jnp.float32) + partner(low(sent)).astype(jnp.float32)
+
+
+def scatter_chips(terms, waiting=None, beside=()):
     running = low(terms[1])
     running, waiting, beside = together(running, waiting, beside)
     if waiting is not None:
@@ -176,19 +185,34 @@
     for d in range(2, terms.shape[0]):
         running = low(terms[d] + next_chip(running).astype(jnp.float32))
     total = terms[0] + next_chip(running).astype(jnp.float32)
+    rest = None
     if waiting is not None:
-        total = total + waiting.astype(jnp.float32)
-    return total, beside
-
-
-def scatter_chunks(term, works):
+        count = total.shape[0]
+        total = total + waiting[:count].astype(jnp.float32)
+        rest = waiting[count:]
+    return total, rest, beside
+
+
+def scatter_chunks(term, works, rider=None):
     ring = lax.axis_size("context")
+    order = (*range(1, ring), 0)
     total, result = (None, ())
-    for i, s in enumerate((*range(1, ring), 0)):
+    terms = core_sum(*term(order[0]))
+    for i in range(ring):
         arrays, work = works[i]
-        kept, sent = term(s)
+        ahead = core_sum(*term(order[i + 1])) if i + 1 < ring else None
         waiting = None if total is None else low(total)
-        total, (result, arrays) = scatter_expert(kept, sent, waiting, (result, arrays))
+        if i:
+            if rider is not None:
+                waiting = jnp.concatenate([waiting, rider(result)])
+            total, rest, (result, arrays, ahead) = scatter_chips(
+                terms, waiting, (result, arrays, ahead)
+            )
+            if rider is not None:
+                arrays = (rest, *arrays)
+        else:
+            total, _, (result, arrays) = scatter_chips(terms, waiting, (result, arrays))
+        terms = ahead
         result = work(result, *arrays)
     return total, result
 
@@ -303,11 +327,7 @@
         dict(enumerate(before)),
         [],
         count,
-        pl.CostEstimate(
-            flops=2 * count * tok_rows * width * columns,
-            bytes_accessed=4 * count * tok_rows * width + 2 * width * columns,
-            transcendentals=0,
-        ),
+        takes(8.5),
         (places,),
     )
 
@@ -405,7 +425,7 @@
     return jnp.concatenate([distances, places])
 
 
-def block_call(kernel, arrays, in_specs, out_specs, out_shape, count, places=None):
+def block_call(kernel, arrays, in_specs, out_specs, out_shape, count, time, places=None):
     prefetch = [] if places is None else [places]
     return pl.pallas_call(
         kernel,
@@ -417,9 +437,7 @@
         ),
         out_shape=out_shape,
         compiler_params=pltpu.CompilerParams(vmem_limit_bytes=VMEM_LIMIT),
-        cost_estimate=pl.CostEstimate(
-            flops=2**22, bytes_accessed=2**23, transcendentals=0
-        ),
+        cost_estimate=takes(time),
     )(*prefetch, *arrays)
 
 
@@ -498,11 +516,7 @@
             jax.ShapeDtypeStruct((rows, HD), jnp.bfloat16),
         ],
         compiler_params=pltpu.CompilerParams(vmem_limit_bytes=VMEM_LIMIT),
-        cost_estimate=pl.CostEstimate(
-            flops=8 * rows * rows * HD // 2,
-            bytes_accessed=8 * rows * HD,
-            transcendentals=rows * rows // 2,
-        ),
+        cost_estimate=takes(20.0),
     )(length, places, queries, keys, values)
 
 
@@ -576,16 +590,103 @@
         ),
         out_shape=[jax.ShapeDtypeStruct((rows, HD), jnp.float32)] * 3,
         compiler_params=pltpu.CompilerParams(vmem_limit_bytes=VMEM_LIMIT),
-        cost_estimate=pl.CostEstimate(
-            flops=20 * rows * rows * HD // 2,
-            bytes_accessed=20 * rows * HD,
-            transcendentals=rows * rows // 2,
+        cost_estimate=takes(30.0),
+    )(length, queries, grads, logs, delta, keys, values)
+
+
+def finish(kept, received):
+    halves = [part + other.astype(jnp.float32) for part, other in zip(kept, received)]
+    return [jnp.concatenate(halves[i : i + 2])[None] for i in (0, 2, 4)]
+
+
+def place_kernel(order_ref, in_ref, out_ref):
+    out_ref[...] = in_ref[...].astype(out_ref.dtype)
+
+
+def place(blocks, order, dtype):
+    count, rows, width = blocks.shape
+    return pl.pallas_call(
+        place_kernel,
+        grid_spec=pltpu.PrefetchScalarGridSpec(
+            num_scalar_prefetch=1,
+            grid=(count,),
+            in_specs=[pl.BlockSpec((1, rows, width), lambda b, order: (order[b], 0, 0))],
+            out_specs=pl.BlockSpec((1, rows, width), lambda b, order: (b, 0, 0)),
         ),
-    )(length, queries, grads, logs, delta, keys, values)
-
-
-def finish(pending):
-    return [(kept + received.astype(jnp.float32))[None] for kept, received in pending]
+        out_shape=jax.ShapeDtypeStruct(blocks.shape, dtype),
+        compiler_params=pltpu.CompilerParams(vmem_limit_bytes=VMEM_LIMIT),
+        cost_estimate=takes(4.0),
+    )(order, blocks)
+
+
+class OutputTotal:
+    def __init__(self, ring, grad):
+        self.ring, self.width = (ring, grad.shape[1])
+        self.state = ring_parts(grad.reshape(ring, HD, self.width), "dp", 1)
+
+    def over_dp(self):
+        self.state = list(ring_sum_begin(self.state, "dp"))
+        self.taken = 0
+
+    def step(self):
+        ring = self.ring
+        if not self.taken:
+            kept, received = self.state
+            total = kept + received.astype(jnp.float32)
+            self.state = [total[(ring - d) % ring] for d in range(ring)]
+            arrived = 0.0
+        else:
+            *self.state, arrived = self.state
+            arrived = arrived.astype(jnp.float32)
+        self.taken += 1
+        self.state = [*self.state, next_on("context", low(self.state[self.taken] + arrived))]
+
+    def finish(self):
+        for _ in range(self.taken, self.ring - 1):
+            self.step()
+        *parts, arrived = self.state
+        self.state = [low(parts[0] + arrived.astype(jnp.float32))]
+
+    def collect(self):
+        self.state = [*self.state, next_on("context", self.state[-1])]
+
+    def exchange(self):
+        here = jnp.stack(self.state)
+        self.state = [here, *ring_gather(here, "dp")[1:]]
+
+    def total(self):
+        ring, size = (self.ring, lax.axis_size("dp"))
+        z, y = (lax.axis_index("context"), lax.axis_index("dp"))
+        order = jnp.stack(
+            [((y - j) % size) * ring + (z - i) % ring for i in range(ring) for j in range(size)]
+        ).astype(jnp.int32)
+        placed = place(jnp.concatenate(self.state), order, jnp.float32)
+        return placed.reshape(ring * HD, self.width)
+
+
+def context_terms_kernel(*refs, count):
+    blocks, weight_ref, outs = (refs[:count], refs[count], refs[count + 1 :])
+    for i, block_ref in enumerate(blocks):
+
+        @pl.when(pl.program_id(0) == i)
+        def _(block_ref=block_ref):
+            terms = low(contract_last(block_ref[...], weight_ref[...]))
+            for d, out_ref in enumerate(outs):
+                out_ref[...] = terms[:, d * HD : (d + 1) * HD]
+
+
+def context_terms(blocks, weight, ring):
+    count = len(blocks)
+    tok_rows, width = blocks[0].shape
+    return pl.pallas_call(
+        functools.partial(context_terms_kernel, count=count),
+        grid=(count,),
+        in_specs=[fixed_spec(tok_rows, width)] * count + [fixed_spec(*weight.shape)],
+        out_specs=[rows_spec(tok_rows, HD)] * ring,
+        out_shape=[jax.ShapeDtypeStruct((count * tok_rows, HD), jnp.bfloat16)] * ring,
+        compiler_params=pltpu.CompilerParams(vmem_limit_bytes=VMEM_LIMIT),
+        cost_estimate=takes(6.0),
+    )(*blocks, weight)
 
 
 def permute_by(axis, values, distance):
@@ -631,18 +732,16 @@
             experts.pick(results[3][:, 0, :])
             return results[3]
 
-        gates, ups, downs = experts.weights
+        arriving = experts.arriving
         _, done = gather_chunks(
             jnp.concatenate([normed, experts.chosen], axis=1),
             project,
-            [(), (tables, gates), (), ups],
+            [arriving[0], (tables, arriving[1]), arriving[2], (arriving[3], count)],
             1,
         )
-        tables, gates = done[1]
-        self.count_total = count
+        tables, second = done[1]
+        fourth, self.count_total = done[3]
         self.raw, self.normed, squares = made[0]
-        squares, downs = together(squares, downs)
-        experts.weights = (gates, done[3], downs)
         totals = small_sum(squares, TOKEN_AXES)
         self.common = (self.raw, totals, self.gains, *tables)
         self.common_specs = [
@@ -659,10 +758,14 @@
             [rows_spec(block, HD)] * 3,
             [jax.ShapeDtypeStruct((rows, HD), jnp.bfloat16)] * 3,
             ring,
-        )
+            7.5,
+        )
+        self.queries, fifth = together(self.queries, arriving[4])
         self.context, self.logs, pieces = flash_forward(
             self.queries, self.keys, self.values, self.length, self.places, block, share
         )
+        pieces, sixth = together(pieces, arriving[5])
+        experts.arriving = [done[0], second, done[2], fourth, fifth, sixth]
         pieces = jnp.split(pieces, ring)
         self.context_block = jnp.concatenate(
             [pieces[0]] + [permute_by("context", pieces[d], -d) for d in range(1, ring)], axis=1
@@ -675,20 +778,25 @@
             contract(part, self.output_weight, 1, 0).reshape(shape)
             for part in (self.context_block[:half], self.context_block[half:])
         )
-        return scatter_expert(kept, sent)[0]
+        return scatter_chips(core_sum(kept, sent))[0]
 
     def backward(self, grad_attn, sums, pending):
         tok_rows, ring, block, rows = (self.tok_rows, self.ring, self.block, self.rows)
+        kept, received = (list(part) for part in zip(*pending))
         block_grad = gather_expert(grad_attn)
-        sums, block_grad[-1] = together(small_sum(sums, ("context",)), block_grad[-1])
-        block_grad = jnp.concatenate(block_grad)
-        grad_context = low(contract_last(block_grad, self.output_weight))
-        sums, grad_context = together(sums, grad_context)
+        sums, block_grad[-1], received[2] = together(
+            small_sum(sums, ("context",)), block_grad[-1], received[2]
+        )
+        pieces = context_terms(block_grad, self.output_weight, ring)
+        sums, pieces = together(sums, pieces)
         sums = small_sum(sums, ("expert",))
-        pieces = jnp.split(grad_context, ring, axis=1)
+        output_grad = contract_rows(self.context_block, jnp.concatenate(block_grad))
+        output_sum = OutputTotal(ring, output_grad)
         pieces = jnp.concatenate(
             [pieces[0]] + [permute_by("context", pieces[d], d) for d in range(1, ring)]
         )
+        pieces, output_sum.state, received[3] = together(pieces, output_sum.state, received[3])
+        output_sum.over_dp()
         grad_context, delta = block_call(
             functools.partial(context_grad_kernel, share=self.share),
             (pieces, self.context),
@@ -699,19 +807,11 @@
                 jax.ShapeDtypeStruct((8, rows), jnp.float32),
             ],
             ring,
+            5.0,
             self.places,
         )
         sums, delta = together(sums, delta)
         sums = small_sum(sums, ("dp",))
-        output_grad = contract_rows(self.context_block, block_grad)
-        head = lax.axis_index("context")
-        output_grad = jnp.concatenate(
-            [
-                lax.dynamic_slice_in_dim(output_grad, (h + ring - head) % ring * HD, HD, 0)
-                for h in range(ring)
-            ]
-        )
-        output_total = lax.psum(low(output_grad), ("dp", "context"))
         query_grad, key_grad, value_grad = flash_backward(
             self.queries,
             self.keys,
@@ -722,9 +822,10 @@
             self.length,
             block,
         )
-        kept, received = zip(*pending)
-        query_grad, kept = together(query_grad, kept)
-        self.finished = finish(zip(kept, received))
+        query_grad, kept, received[4], output_sum.state = together(
+            query_grad, kept, received[4], output_sum.state
+        )
+        output_sum.step()
         dots, gain_grads = block_call(
             turn_grad_kernel,
             (*self.common, query_grad, key_grad),
@@ -735,8 +836,14 @@
                 jax.ShapeDtypeStruct((8, HD), jnp.float32),
             ],
             ring,
-        )
+            10.0,
+        )
+        dots, output_sum.state = together(dots, output_sum.state)
+        output_sum.step()
         dots = small_sum(dots, TOKEN_AXES)
+        dots, received[5], output_sum.state = together(dots, received[5], output_sum.state)
+        output_sum.step()
+        self.finished = finish(kept, received)
         grad_joint, relative = block_call(
             functools.partial(norm_grad_kernel, share=self.share),
             (*self.common, query_grad, key_grad, value_grad, dots),
@@ -744,92 +851,93 @@
             [rows_spec(block, 3 * HD), distance_spec(block, 3 * HD)],
             [jax.ShapeDtypeStruct((rows, 3 * HD), jnp.bfloat16)] * 2,
             ring,
+            12.0,
             self.places,
         )
+        grad_joint, relative, output_sum.state = together(grad_joint, relative, output_sum.state)
+        output_sum.finish()
+        output_sum.collect()
+        head = lax.axis_index("context")
         half = block // 2
+        width = self.weight.shape[0]
+        joint_grad = contract_rows(grad_joint, self.normed)
+        here = (lax.axis_index("expert") * ring + head) * HD
+        gains = lax.dynamic_update_slice(
+            jnp.zeros((2, width), jnp.float32), gain_grads[:2], (0, here)
+        )
+        parts = ring_parts(joint_grad.reshape(3, HD, width), "dp", 1)
+        mine, others = ring_sum_begin([part.reshape(-1, width) for part in parts], "dp")
+        relative, mine, output_sum.state = together(relative, mine, output_sum.state)
 
         def term(s):
             return tuple(
                 contract_last(relative[start : start + half], self.weight).reshape(
-                    -1, tok_rows, self.weight.shape[0]
+                    -1, tok_rows, width
                 )
                 for start in (s * block, s * block + half)
             )
 
-        joint = JointTotal(ring, self.weight.shape[0] // lax.axis_size("dp"))
-
-        def first(_, rows, right, gain_grads):
-            joint_grad = contract_rows(rows, right)
-            product = jnp.sum(joint_grad * self.weight.astype(jnp.float32), axis=1)
-            here = (lax.axis_index("expert") * ring + head) * HD
-            gains = lax.dynamic_update_slice(
-                jnp.zeros((2, product.shape[0]), jnp.float32), gain_grads[:2], (0, here)
-            )
-            share = ring_sum(ring_parts(joint_grad, "dp", 0), "dp")
-            return (low(share), jnp.concatenate([product[None], gains]), ())
+        joint = JointTotal(ring)
+
+        def first(_):
+            for _ in range(ring - 2):
+                output_sum.collect()
+            return low(mine + others.astype(jnp.float32)), (), output_sum.state
 
         def later(i):
-            def work(result):
-                piece, gains, outs = result
-                joint.outs = outs
+            def work(result, rest):
+                piece, joint.outs, output_sum.state = result
                 joint.add(piece, i)
-                axes = ("expert", "context", "dp")
-                gains = small_sum(gains, axes[i : i + 1])
-                return (next_on("context", piece), gains, joint.outs)
+                if not i:
+                    output_sum.exchange()
+                return rest, joint.outs, output_sum.state
 
             return work
 
-        works = [((self.normed, grad_joint, gain_grads), first)]
-        works += [((), later(i)) for i in range(ring - 1)]
-        total, (piece, gains, joint.outs) = scatter_chunks(term, works)
-        if ring < 4:
-            gains = small_sum(gains, ("expert", "context", "dp")[ring - 1 :])
+        works = [((), first)] + [((), later(i)) for i in range(ring - 1)]
+        total, result = scatter_chunks(term, works, lambda result: result[0])
+        piece, joint.outs, output_sum.state = result
         joint.add(piece, ring - 1)
-        output_total, total = together(output_total, total)
-        return (
-            total,
-            sums,
-            gains[0],
-            *joint.outs,
-            *lax.dynamic_slice_in_dim(
-                gains[1:], lax.axis_index("expert") * ring * HD, ring * HD, 1
-            ),
-            output_total.astype(jnp.float32),
-        )
-
-
-def spread_kernel(place_ref, in_ref, *refs):
-    for i, out_ref in enumerate(refs[-3:]):
-        out_ref[...] = in_ref[:, i * HD : (i + 1) * HD].astype(jnp.float32)
+        return total, sums, gains, *joint.outs, output_sum.total()
+
+
+def spread_kernel(place_ref, *refs, size):
+    parts, outs = (refs[:size], refs[-3:])
+    rows = HD // size
+    for i, out_ref in enumerate(outs):
+        slabs = []
+        for j in range(size):
+            slab = 0.0
+            for d, part in enumerate(parts):
+                here = part[i * rows : (i + 1) * rows, :].astype(jnp.float32)
+                slab = slab + jnp.where(place_ref[1 + d] == j, here, 0.0)
+            slabs.append(slab)
+        out_ref[...] = jnp.concatenate(slabs, axis=0).T
 
 
 class JointTotal:
-    def __init__(self, ring, rows):
-        self.ring, self.rows = (ring, rows)
+    def __init__(self, ring):
+        self.ring = ring
         self.outs = ()
 
     def add(self, piece, distance):
-        ring, rows, size = (self.ring, self.rows, lax.axis_size("dp"))
+        ring, size = (self.ring, lax.axis_size("dp"))
         head = (lax.axis_index("context") + ring - distance) % ring
-        for j, part in enumerate(ring_gather(piece, "dp")):
-            half = (lax.axis_index("dp") + size - j) % size
-            self.outs = pl.pallas_call(
-                spread_kernel,
-                grid_spec=pltpu.PrefetchScalarGridSpec(
-                    num_scalar_prefetch=1,
-                    grid=(1,),
-                    in_specs=[fixed_spec(rows, 3 * HD)]
-                    + [pl.BlockSpec(memory_space=pl.ANY)] * len(self.outs),
-                    out_specs=[pl.BlockSpec((rows, HD), lambda i, place: (place[0], place[1]))]
-                    * 3,
-                ),
-                out_shape=[jax.ShapeDtypeStruct((rows * size, ring * HD), jnp.float32)] * 3,
-                input_output_aliases={2 + i: i for i in range(len(self.outs))},
-                compiler_params=pltpu.CompilerParams(vmem_limit_bytes=VMEM_LIMIT),
-                cost_estimate=pl.CostEstimate(
-                    flops=0, bytes_accessed=18 * rows * HD, transcendentals=0
-                ),
-            )(jnp.stack([half, head]).astype(jnp.int32), part, *self.outs)
+        parts = ring_gather(piece, "dp")
+        width = piece.shape[1]
+        place = [head] + [(lax.axis_index("dp") + size - d) % size for d in range(size)]
+        out = ((width, ring * HD), jnp.float32, pl.BlockSpec((width, HD), lambda i, p: (0, p[0])))
+        self.outs = chunk_call(
+            functools.partial(spread_kernel, size=size),
+            parts,
+            [fixed_spec(*piece.shape)] * size,
+            [out] * 3,
+            dict(enumerate(self.outs)),
+            [],
+            1,
+            takes(5.0),
+            (jnp.stack(place).astype(jnp.int32),),
+        )
 
 
 class BlockAttention:
@@ -909,7 +1017,7 @@
         )
 
     def backward(self, grad_attn, sums, pending):
-        self.finished = finish(pending)
+        self.finished = finish(*zip(*pending))
         sums = small_sum(sums, ALL_AXES)
         rows, heads = (self.rows, self.heads)
         block_grad = gather_block(grad_attn)
@@ -985,16 +1093,11 @@
             ),
             ("dp", "context"),
         )
-        gain_product = jnp.sum(joint_total * self.weight.astype(jnp.float32), axis=1)
-        gain_product = lax.psum(gain_product, "expert")
-        return (
-            grad_normed,
-            sums,
-            gain_product,
-            *jnp.split(joint_total, 3, axis=1),
-            *gains_total,
-            output_total,
-        )
+        gains = jnp.zeros((2, self.weight.shape[0]), jnp.float32)
+        here = lax.axis_index("expert") * self.head_width
+        own = jnp.stack(gains_total) / (lax.axis_size("dp") * lax.axis_size("context"))
+        gains = lax.dynamic_update_slice(gains, own, (0, here))
+        return (grad_normed, sums, gains, *jnp.split(joint_total, 3, axis=1), output_total)
 
 
 UNIT_TILE = 256
@@ -1068,12 +1171,26 @@
     for i in range(count):
         terms = contract_rows(pick_ref[i], rows_ref[pl.ds(i * capacity, capacity), :])
         if i < half:
-            kept_ref[i] = low(terms)
+            kept_ref[i, :tok_rows, :] = low(terms)
         else:
-            sent_ref[i - half] = low(terms)
-
-
-def expert_backward_kernel(*refs, count, unit_tiles):
+            sent_ref[i - half, :tok_rows, :] = low(terms)
+
+
+def spread_scalars(expert, values_ref, kept_ref, sent_ref):
+    count, tok_rows = values_ref.shape
+    half = count // 2
+    for i in range(count):
+        out_ref, place = (kept_ref, i) if i < half else (sent_ref, i - half)
+        values = values_ref[i : i + 1, :]
+        first = low(values).astype(jnp.float32)
+        both = jnp.concatenate([first, values - first], axis=1)
+        rows, width = (out_ref.shape[1] - tok_rows, out_ref.shape[2])
+        out_ref[place, tok_rows:, :] = jnp.zeros((rows, width), jnp.bfloat16)
+        row = lax.broadcasted_iota(jnp.int32, (rows, 2 * tok_rows), 0)
+        out_ref[place, tok_rows:, : 2 * tok_rows] = low(jnp.where(row == expert, both, 0.0))
+
+
+def expert_backward_kernel(expert_ref, *refs, count, unit_tiles):
     blocks = refs[:count]
     (
         pick_ref,
@@ -1134,6 +1251,17 @@
         )
         spread_tokens(pick_ref, rows_ref, kept_ref, sent_ref)
 
+        @pl.when(step == unit_tiles)
+        def _():
+            spread_scalars(expert_ref[0], gate_grad_ref, kept_ref, sent_ref)
+
+        @pl.when(step > unit_tiles)
+        def _():
+            tok_rows = gate_grad_ref.shape[1]
+            for out_ref in (kept_ref, sent_ref):
+                rest = out_ref.shape[0], out_ref.shape[1] - tok_rows, out_ref.shape[2]
+                out_ref[:, tok_rows:, :] = jnp.zeros(rest, jnp.bfloat16)
+
 
 def chunk_call(kernel, arrays, in_specs, outs, before, scratch, steps, cost, prefetch=()):
     first = len(prefetch) + len(arrays)
@@ -1163,11 +1291,10 @@
         self.router_weight = jnp.pad(router_weight, ((0, 0), (0, HD - self.experts_all)))
         expert_ids = jnp.arange(HD, dtype=jnp.int32)
         self.chosen = low(jnp.any(routes[:, :, None] == expert_ids, axis=1))
-        gates = ring_gather(gate_weight[0], "dp")
-        _, up_first = together(gates[-1], up_weight[0])
-        ups = ring_gather(up_first, "dp")
-        _, down_first = together(ups[-1], down_weight[0])
-        self.weights = (gates, ups, ring_gather(down_first, "dp"))
+        self.own = (gate_weight[0], up_weight[0], down_weight[0])
+        self.arriving = [
+            ring_gather(half, "dp")[1:] for w in self.own for half in jnp.split(w, 2)
+        ]
         self.picks = []
 
     def here(self, blocks):
@@ -1185,10 +1312,12 @@
         self.picks.append(low(matches & member[:, None, :]))
 
     def begin(self):
-        self.gate_weight, self.up_weight = (
-            jnp.concatenate(parts, axis=1) for parts in self.weights[:2]
-        )
-        self.down_weight = jnp.concatenate(self.weights[2], axis=0)
+        whole = []
+        for i, own in enumerate(self.own):
+            halves = zip(*self.arriving[2 * i : 2 * i + 2])
+            whole.append([own] + [jnp.concatenate(pair) for pair in halves])
+        self.gate_weight, self.up_weight = (jnp.concatenate(w, axis=1) for w in whole[:2])
+        self.down_weight = jnp.concatenate(whole[2])
         self.units = self.gate_weight.shape[1]
         self.picks = jnp.stack(self.picks)
         self.chained, self.chained_back = ((), ())
@@ -1199,7 +1328,7 @@
         width = self.gate_weight.shape[0]
         return ring, count, count * capacity, tok_rows, width
 
-    def plan(self, s):
+    def plan(self, s, more=0):
         ring, count, rows, tok_rows, width = self.shapes()
         tiles = self.units // UNIT_TILE
         tile = math.gcd(WIDTH_TILE, width)
@@ -1213,9 +1342,9 @@
         half = count // 2
         all_rows = ring * rows
         term = (
-            (half, tok_rows, width),
+            (half, tok_rows + more, width),
             jnp.bfloat16,
-            pl.BlockSpec((half, tok_rows, tile), lambda j, *_: (0, 0, column(j))),
+            pl.BlockSpec((half, tok_rows + more, tile), lambda j, *_: (0, 0, column(j))),
         )
         unit_spec = pl.BlockSpec((rows, UNIT_TILE), lambda j, *_: (s, unit(j)))
         whole_spec = pl.BlockSpec((rows, width), lambda j, *_: (s, 0))
@@ -1225,11 +1354,7 @@
         pick_spec = pl.BlockSpec((None, *self.picks.shape[1:]), lambda j, *_: (s, 0, 0, 0))
         narrow = ((all_rows, self.units), jnp.bfloat16, unit_spec)
         wide = ((all_rows, width), jnp.bfloat16, whole_spec)
-        cost = pl.CostEstimate(
-            flops=6 * rows * width * self.units,
-            bytes_accessed=6 * self.units * width + 12 * rows * width,
-            transcendentals=rows * self.units,
-        )
+        cost = takes(21.0)
         return (
             unit,
             column,
@@ -1313,7 +1438,7 @@
 
     def forward(self, ffn_in):
         last = lax.axis_size("context") - 1
-        done, _ = gather_chunks(ffn_in, self.forward_chunk, slack=1)
+        done, _ = gather_chunks(ffn_in, self.forward_chunk)
         idle = ((), lambda result: result)
         works = [((), lambda result: done[last])] + [idle] * last
         mixture, _ = scatter_chunks(lambda s: self.terms[s], works)
@@ -1336,7 +1461,7 @@
             narrow,
             wide,
             cost,
-        ) = self.plan(s)
+        ) = self.plan(s, -(-self.experts_all // 16) * 16)
         chunk_rows, gate_part, up_part, hidden, out, row_gates = self.chained
         results = chunk_call(
             functools.partial(expert_backward_kernel, count=count, unit_tiles=tiles),
@@ -1378,6 +1503,7 @@
             ],
             tiles + width // tile,
             cost,
+            (self.expert.reshape(1).astype(jnp.int32),),
         )
         self.chained_back = results[1:4]
         self.terms_back[s] = results[4:]
@@ -1385,7 +1511,7 @@
 
     def backward(self, grad_out):
         last = lax.axis_size("context") - 1
-        gate_grads, _ = gather_chunks(low(grad_out), self.backward_chunk, slack=1)
+        self.gate_done, _ = gather_chunks(low(grad_out), self.backward_chunk)
         grad_rows_out, grad_gate, grad_up = self.chained_back
         chunk_rows, hidden = (self.chained[0], self.chained[3])
         size = lax.axis_size("dp")
@@ -1393,28 +1519,41 @@
         def parts(left, right, axis):
             return jnp.split(contract_rows(left, right), size, axis=axis)
 
-        def first(_):
-            return gate_grads[last]
-
-        def second(_, grad, rows, right):
-            grad_gates = lax.all_to_all(
-                reorder(grad, absolute_to_relative()),
-                TOKEN_AXES,
-                split_axis=0,
-                concat_axis=0,
-                tiled=True,
-            ).T
-            return grad_gates, parts(rows, right, 1)
-
-        def third(result, rows, right):
-            return *result, parts(rows, right, 1)
-
-        works = [((), first)] + [((), lambda result: result)] * last
-        works[1] = ((jnp.concatenate(gate_grads), chunk_rows, grad_gate), second)
+        pending = []
+
+        def product(left, right, axis):
+            shares = parts(left, right, axis)
+            halves = zip(*(jnp.split(share, 2) for share in shares))
+            return [list(half) for half in halves]
+
+        def begin(half):
+            pending.append(ring_sum_begin(half, "dp"))
+            return pending[-1][1]
+
+        def second(_, *arrays):
+            self.gates_grad = product(*arrays, 1)
+            return self.gates_grad[0][0], ()
+
+        def third(_, *arrays):
+            self.ups_grad = product(*arrays, 1)
+            return self.ups_grad[0][0], begin(self.gates_grad[0])
+
+        def fourth(_, *arrays):
+            self.downs_grad = product(*arrays, 0)
+            return self.downs_grad[0][0], begin(self.gates_grad[1])
+
+        works = [((), lambda result: result)] * (last + 1)
+        works[0] = ((), lambda _: self.gate_done[last])
+        works[1] = ((chunk_rows, grad_gate), second)
         works[2] = ((chunk_rows, grad_up), third)
-        grad_ffn, (grad_gates, *grads) = scatter_chunks(lambda s: self.terms_back[s], works)
-        grads.append(parts(hidden, grad_rows_out, 0))
-        pending = [ring_sum_begin(part, "dp") for part in grads]
+        works[-1] = ((hidden, grad_rows_out), fourth)
+        total, done = scatter_chunks(lambda s: self.terms_back[s], works)
+        total, done = together(total, done)
+        tok_rows = self.picks.shape[3]
+        grad_ffn, rest = (total[:tok_rows], total[tok_rows:])
+        grad_gates = (rest[:, :tok_rows] + rest[:, tok_rows : 2 * tok_rows])[: self.experts_all].T
+        for half in (*self.ups_grad, *self.downs_grad):
+            begin(half)
         return grad_ffn, grad_gates, pending
 
 
@@ -1451,7 +1590,6 @@
     normed = low(tokens * inverse_one * attn_gain)
     heads_here = query_weight.shape[1] // HD
     count_total = small_sum(jnp.full((8, 128), length, jnp.int32), ("dp",))
-    count_total, gate_weight = together(count_total, gate_weight)
     experts = Experts(
         expert_routes, capacity, router_weight, gate_weight, up_weight, down_weight
     )
@@ -1513,17 +1651,15 @@
             jnp.broadcast_to(local_loss, ffn_gain_grad.shape)[None],
         ]
     )
-    (
-        grad_normed,
-        sums,
-        attn_gain_product,
-        query_total,
-        key_total,
-        value_total,
-        query_gain_total,
-        key_gain_total,
-        output_total,
-    ) = attention.backward(low(grad_residual), sums, pending)
+    grad_normed, sums, gains, query_total, key_total, value_total, output_total = (
+        attention.backward(low(grad_residual), sums, pending)
+    )
+    attn_gain_grad = jnp.sum(tokens * inverse_one * grad_normed, axis=0)
+    gains = small_sum(jnp.concatenate([attn_gain_grad[None], gains]), ("dp", *TOKEN_AXES))
+    head_width = query_gain.shape[0]
+    query_gain_total, key_gain_total = lax.dynamic_slice_in_dim(
+        gains[1:], lax.axis_index("expert") * head_width, head_width, 1
+    )
     weighted_one = grad_normed * attn_gain
     input_grad = (
         grad_residual
@@ -1536,7 +1672,7 @@
         low(output_full),
         loss_total / count_total,
         input_grad,
-        attn_gain_product / attn_gain,
+        gains[0],
         query_total,
         key_total,
         value_total,

time: 1230 us -> 1190 us (0.967)
  starting transfers between devices: 134 us -> 103 us
  between operations: 19.4 us -> 6.16 us
    concatenate x3 -> x9, other arithmetic: 2.93 us -> 25.6 us  [the longest x2 10.1 us: begin(): jnp.concatenate(w, axis=1)]
    ppermute x27, starting transfers between devices: 42.9 us -> 25.7 us  [small_sum(): lax.ppermute(values, axis, tuple(((i, i ^ bits) for i in range(size))))]
    ppermute x6, waiting for transfers between devices: 50.9 us -> 34.6 us  [permute_by(): lax.ppermute(values, axis, tuple(((i, (i + distance) % size) for i in ran...]
    ppermute x97 -> x108, waiting for transfers between devices: 383 us -> 400 us  [moved(): return jax.tree.map(lambda v: lax.ppermute(v, axis, pairs), values)]
    ppermute x97 -> x108, starting transfers between devices: 83.8 us -> 67.7 us  [moved(): return jax.tree.map(lambda v: lax.ppermute(v, axis, pairs), values)]
    pallas_call x12 -> x16, Pallas kernels: 203 us -> 219 us  [chunk_call(): pl.pallas_call(kernel, grid_spec=pltpu.PrefetchScalarGridSpec(num_scalar_...]
    split x9, local copies, waits for them, and re-layouts: 7.63 us -> 22.7 us  [the longest x6 15 us: product(): halves = zip(*(jnp.split(share, 2) for share in shares))]
    unnamed x236 -> x282, local copies, waits for them, and re-layouts: 30.1 us -> 20.3 us
  transfers between devices with their start and end apart: 132 -> 141, of which waited for: 49 -> 52; matrix products, arithmetic and copies ran while one was open for 19% -> 20% of each run, Pallas kernels for 24% -> 28%
where the time goes in v3:
time: 1190 us
  waiting for transfers between devices  466 us (39%)
  Pallas kernels  331 us (28%)
  other arithmetic  124 us (10%)
  starting transfers between devices  103 us (9%)
  matrix products  89.2 us (7%)
  local copies, waits for them, and re-layouts  66.2 us (6%)
    ppermute x108, waiting for transfers between devices, moved(): return jax.tree.map(lambda v: lax.ppermute(v, axis, pairs), values)  400 us
    pallas_call x16, Pallas kernels, chunk_call(): pl.pallas_call(kernel, grid_spec=pltpu.PrefetchScalarGridSpec(num_scalar_...  219 us
    dot_general x19, matrix products, contract(): lax.dot_general(left, right, (((left_dim,), (right_dim,)), ((), ())), pre...  86.6 us
    ppermute x108, starting transfers between devices, moved(): return jax.tree.map(lambda v: lax.ppermute(v, axis, pairs), values)  67.7 us
    pallas_call x1, Pallas kernels, flash_backward(): pl.pallas_call(functools.partial(flash_backward_kernel, block=block), gri...  38.7 us
    ppermute x6, waiting for transfers between devices, permute_by(): lax.ppermute(values, axis, tuple(((i, (i + distance) % size) for i in ran...  34.6 us
    pallas_call x4, Pallas kernels, block_call(): pl.pallas_call(kernel, grid_spec=pltpu.PrefetchScalarGridSpec(num_scalar_...  34.1 us
    ppermute x27, waiting for transfers between devices, small_sum(): lax.ppermute(values, axis, tuple(((i, i ^ bits) for i in range(size))))  31.8 us
  transfers between devices with their start and end apart: 141, of which 52 were waited for; matrix products, arithmetic and copies ran while one was open for 20% of the time, Pallas kernels for 28%

profile of v3, /device:TPU:0, one launch (start us, length us, event | category | flops | bytes accessed | tf_op | source)
XLA Modules:
  0.0 1185.5 jit_solution(13354785597928015064)
XLA Ops:
  19.2 9.4 fusion.56
  28.5 10.2 collective-permute-done.2
  48.6 12.2 %collective-permute-done.5 = bf16[1024,512]{1,0:T(8,128)(2,1)} collective-permute-done((bf16[1024,512]{1,0:T(8,128)(2,1)}, bf16[1024,512]{1,0:T(8,128)(2,1)}, u32[]{:S(2)}, u32[]{:S(2)}) %collective-permute-start.5) | collective-permute-done | bytes 1048608 | tf_op jit(solution)/shard_map/ppermute | solution.py:93
  62.3 4.3 collective-permute-done.3.refs_0_
  70.9 8.6 shard_map.271
  79.6 6.3 collective-permute-done.10
  87.4 6.5 collective-permute-done.6.refs_0_
  96.6 13.3 %collective-permute-done.15 = s32[8,128]{1,0:T(8,128)S(1)} collective-permute-done((s32[8,128]{1,0:T(8,128)S(1)}, s32[8,128]{1,0:T(8,128)S(1)}, u32[]{:S(2)}, u32[]{:S(2)}) %collective-permute-start.15) | collective-permute-done | bytes 4128 | tf_op jit(solution)/shard_map/ppermute | solution.py:252
  113.4 8.5 shard_map.272
  124.9 8.5 shard_map.273
  134.8 9.0 shard_map.274
  158.1 7.5 shard_map.275
  165.6 26.2 %shard_map.276 = (bf16[4096,128]{1,0:T(8,128)(2,1)}, f32[8,4096]{1,0:T(8,128)}, bf16[4096,128]{1,0:T(8,128)(2,1)}) custom-call(s32[1]{0:T(128)} %copy.142.length_ref, s32[8]{0:T(128)} %pad_add_fusion.places_ref, bf16[4096,128]{1,0:T(8,128)(2,1)} %get-tuple-element.259.q_ref, bf16[4096,128]{1,0:T(8,128)(2,1)} %get-tuple-element.260.k_ref, ...), custom_call_target="tpu_custom_call" | custom-call | flops 22000001024 | bytes 60000000 | tf_op jit(solution)/shard_map/pallas_call | solution.py:501
  197.6 6.8 collective-permute-done.30
  204.4 10.3 collective-permute-done.29
  230.6 19.9 %collective-permute-done.32 = bf16[256,2048]{1,0:T(8,128)(2,1)S(1)} collective-permute-done((bf16[256,2048]{1,0:T(8,128)(2,1)S(1)}, bf16[256,2048]{1,0:T(8,128)(2,1)S(1)}, u32[]{:S(2)}, u32[]{:S(2)}) %collective-permute-start.32) | collective-permute-done | bytes 1048608 | tf_op jit(solution)/shard_map/ppermute | solution.py:93
  252.0 5.3 collective-permute-start.33
  258.1 6.0 maximum_maximum_fusion.1.refs_7_.refs_11_
  264.2 16.6 %collective-permute-done.33.refs_0_ = bf16[256,2048]{1,0:T(8,128)(2,1)S(1)} collective-permute-done((bf16[256,2048]{1,0:T(8,128)(2,1)S(1)}, bf16[256,2048]{1,0:T(8,128)(2,1)S(1)}, u32[]{:S(2)}, u32[]{:S(2)}) %collective-permute-start.33) | collective-permute-done | bytes 1048608 | tf_op jit(solution)/shard_map/ppermute | solution.py:93
  283.6 5.6 pad_maximum_fusion.refs_8_.refs_9_
  291.4 21.0 %shard_map.277 = (bf16[2560,2048]{1,0:T(8,128)(2,1)}, bf16[2560,1024]{1,0:T(8,128)(2,1)}, bf16[2560,1024]{1,0:T(8,128)(2,1)}, bf16[2560,1024]{1,0:T(8,128)(2,1)}...) custom-call(s32[1]{0:T(128)} %bitcast.expert_ref, ...), custom_call_target="tpu_custom_call" | custom-call | flops 23100000256 | bytes 63000000 | tf_op jit(solution)/shard_map/pallas_call | solution.py:1268
  312.4 4.6 collective-permute-done.35.refs_0_
  320.8 21.2 %shard_map.278 = (bf16[2560,2048]{1,0:T(8,128)(2,1)}, bf16[2560,1024]{1,0:T(8,128)(2,1)}, bf16[2560,1024]{1,0:T(8,128)(2,1)}, bf16[2560,1024]{1,0:T(8,128)(2,1)}...) custom-call(s32[1]{0:T(128)} %bitcast.expert_ref, ...), custom_call_target="tpu_custom_call", output_to_operand_aliasing={{0}: (10, {}), {1}: (11, {}), {2}: (12, {}), {3}: (13, {}),... | custom-call | flops 23100000256 | bytes 63000000 | tf_op jit(solution)/shard_map/pallas_call | solution.py:1268
  348.7 21.2 %shard_map.279 = (bf16[2560,2048]{1,0:T(8,128)(2,1)}, bf16[2560,1024]{1,0:T(8,128)(2,1)}, bf16[2560,1024]{1,0:T(8,128)(2,1)}, bf16[2560,1024]{1,0:T(8,128)(2,1)}...) custom-call(s32[1]{0:T(128)} %bitcast.expert_ref, ...), custom_call_target="tpu_custom_call", output_to_operand_aliasing={{0}: (10, {}), {1}: (11, {}), {2}: (12, {}), {3}: (13, {}),... | custom-call | flops 23100000256 | bytes 63000000 | tf_op jit(solution)/shard_map/pallas_call | solution.py:1268
  375.0 21.2 %shard_map.280 = (bf16[2560,2048]{1,0:T(8,128)(2,1)}, bf16[2560,1024]{1,0:T(8,128)(2,1)}, bf16[2560,1024]{1,0:T(8,128)(2,1)}, bf16[2560,1024]{1,0:T(8,128)(2,1)}...) custom-call(s32[1]{0:T(128)} %bitcast.expert_ref, ...), custom_call_target="tpu_custom_call", output_to_operand_aliasing={{0}: (10, {}), {1}: (11, {}), {2}: (12, {}), {3}: (13, {}),... | custom-call | flops 23100000256 | bytes 63000000 | tf_op jit(solution)/shard_map/pallas_call | solution.py:1268
  400.3 21.8 %collective-permute-done.47 = bf16[256,2048]{1,0:T(8,128)(2,1)S(1)} collective-permute-done((bf16[256,2048]{1,0:T(8,128)(2,1)S(1)}, bf16[256,2048]{1,0:T(8,128)(2,1)S(1)}, u32[]{:S(2)}, u32[]{:S(2)}) %collective-permute-start.47) | collective-permute-done | bytes 1048608 | tf_op jit(solution)/shard_map/ppermute | solution.py:93
  426.6 22.8 %collective-permute-done.53 = bf16[256,2048]{1,0:T(8,128)(2,1)S(1)} collective-permute-done((bf16[256,2048]{1,0:T(8,128)(2,1)S(1)}, bf16[256,2048]{1,0:T(8,128)(2,1)S(1)}, u32[]{:S(2)}, u32[]{:S(2)}) %collective-permute-start.53) | collective-permute-done | bytes 1048608 | tf_op jit(solution)/shard_map/ppermute | solution.py:93
  451.5 23.6 %collective-permute-done.56 = bf16[256,2048]{1,0:T(8,128)(2,1)S(1)} collective-permute-done((bf16[256,2048]{1,0:T(8,128)(2,1)S(1)}, bf16[256,2048]{1,0:T(8,128)(2,1)S(1)}, u32[]{:S(2)}, u32[]{:S(2)}) %collective-permute-start.56) | collective-permute-done | bytes 1048608 | tf_op jit(solution)/shard_map/ppermute | solution.py:93
  477.9 21.9 %collective-permute-done.58 = bf16[256,2048]{1,0:T(8,128)(2,1)} collective-permute-done((bf16[256,2048]{1,0:T(8,128)(2,1)S(1)}, bf16[256,2048]{1,0:T(8,128)(2,1)}, u32[]{:S(2)}, u32[]{:S(2)}) %collective-permute-start.58) | collective-permute-done | bytes 1048608 | tf_op jit(solution)/shard_map/ppermute | solution.py:93
  505.9 23.2 %collective-permute-done.59.refs_0_ = bf16[256,2048]{1,0:T(8,128)(2,1)} collective-permute-done((bf16[256,2048]{1,0:T(8,128)(2,1)}, bf16[256,2048]{1,0:T(8,128)(2,1)}, u32[]{:S(2)}, u32[]{:S(2)}) %collective-permute-start.59) | collective-permute-done | bytes 1048608 | tf_op jit(solution)/shard_map/ppermute | solution.py:93
  535.0 17.6 %collective-permute-done.61.refs_0_ = bf16[256,2048]{1,0:T(8,128)(2,1)S(1)} collective-permute-done((bf16[256,2048]{1,0:T(8,128)(2,1)}, bf16[256,2048]{1,0:T(8,128)(2,1)S(1)}, u32[]{:S(2)}, u32[]{:S(2)}) %collective-permute-start.61) | collective-permute-done | bytes 1048608 | tf_op jit(solution)/shard_map/ppermute | solution.py:93
  554.6 20.9 %shard_map.281 = (f32[4,256]{1,0:T(4,128)}, bf16[2560,2048]{1,0:T(8,128)(2,1)}, bf16[2560,1024]{1,0:T(8,128)(2,1)}, bf16[2560,1024]{1,0:T(8,128)(2,1)}, bf16[2,2...) custom-call(s32[1]{0:T(128)} %bitcast.expert_ref, bf16[256,2048]{1,0:T(8,128)(2,1)} %multiply_convert_fusion.1.refs_0_, ...), custom_call_target="tpu_custom_call" | custom-call | flops 23100000256 | bytes 63000000 | tf_op jit(solution)/shard_map/pallas_call | solution.py:1268
  577.8 20.7 %shard_map.282 = (f32[4,256]{1,0:T(4,128)}, bf16[2560,2048]{1,0:T(8,128)(2,1)}, bf16[2560,1024]{1,0:T(8,128)(2,1)}, bf16[2560,1024]{1,0:T(8,128)(2,1)}, bf16[2,2...) custom-call(s32[1]{0:T(128)} %bitcast.expert_ref, ...), custom_call_target="tpu_custom_call", output_to_operand_aliasing={{1}: (13, {}), {2}: (14, {}), {3}: (15, {})} | custom-call | flops 23100000256 | bytes 63000000 | tf_op jit(solution)/shard_map/pallas_call | solution.py:1268
  602.8 21.2 %shard_map.283 = (f32[4,256]{1,0:T(4,128)}, bf16[2560,2048]{1,0:T(8,128)(2,1)}, bf16[2560,1024]{1,0:T(8,128)(2,1)}, bf16[2560,1024]{1,0:T(8,128)(2,1)}, bf16[2,2...) custom-call(s32[1]{0:T(128)} %bitcast.expert_ref, ...), custom_call_target="tpu_custom_call", output_to_operand_aliasing={{1}: (13, {}), {2}: (14, {}), {3}: (15, {})} | custom-call | flops 23100000256 | bytes 63000000 | tf_op jit(solution)/shard_map/pallas_call | solution.py:1268
  628.7 20.7 %shard_map.284 = (f32[4,256]{1,0:T(4,128)}, bf16[2560,2048]{1,0:T(8,128)(2,1)}, bf16[2560,1024]{1,0:T(8,128)(2,1)}, bf16[2560,1024]{1,0:T(8,128)(2,1)}, bf16[2,2...) custom-call(s32[1]{0:T(128)} %bitcast.expert_ref, ...), custom_call_target="tpu_custom_call", output_to_operand_aliasing={{1}: (13, {}), {2}: (14, {}), {3}: (15, {})} | custom-call | flops 23100000256 | bytes 63000000 | tf_op jit(solution)/shard_map/pallas_call | solution.py:1268
  657.4 22.5 %collective-permute-done.73 = bf16[272,2048]{1,0:T(8,128)(2,1)S(1)} collective-permute-done((bf16[272,2048]{1,0:T(8,128)(2,1)S(1)}, bf16[272,2048]{1,0:T(8,128)(2,1)S(1)}, u32[]{:S(2)}, u32[]{:S(2)}) %collective-permute-start.73) | collective-permute-done | bytes 1114144 | tf_op jit(solution)/shard_map/ppermute | solution.py:93
  683.0 16.9 %fusion.116 = (bf16[2048,1024]{1,0:T(8,128)(2,1)}, f32[2048,1024]{1,0:T(8,128)S(1)}) fusion(bf16[2560,2048]{1,0:T(8,128)(2,1)} %get-tuple-element.353, bf16[2560,1024]{1,0:T(8,128)(2,1)} %get-tuple-element.346), kind=kOutput, calls=%fused_computation.314 | convolution fusion | flops 10739515392 | bytes 28311552 | tf_op jit(solution)/shard_map/dot_general | solution.py:64
  712.9 16.9 %fusion.118 = (bf16[2048,1024]{1,0:T(8,128)(2,1)}, f32[2048,1024]{1,0:T(8,128)S(1)}) fusion(bf16[2560,2048]{1,0:T(8,128)(2,1)} %get-tuple-element.353, bf16[2560,1024]{1,0:T(8,128)(2,1)} %get-tuple-element.354), kind=kOutput, calls=%fused_computation.316 | convolution fusion | flops 10739515392 | bytes 28311552 | tf_op jit(solution)/shard_map/dot_general | solution.py:64
  732.6 4.7 collective-permute-done.82
  739.9 17.1 %fusion.119 = (bf16[1024,2048]{1,0:T(8,128)(2,1)}, f32[1024,2048]{1,0:T(8,128)S(1)}) fusion(bf16[2560,1024]{1,0:T(8,128)(2,1)} %get-tuple-element.359, bf16[2560,2048]{1,0:T(8,128)(2,1)} %get-tuple-element.360), kind=kOutput, calls=%fused_computation.317 | convolution fusion | flops 10739515392 | bytes 28311552 | tf_op jit(solution)/shard_map/dot_general | solution.py:64
  759.4 4.2 collective-permute-done.85
  774.7 17.0 %collective-permute-done.90.refs_1_ = bf16[256,2048]{1,0:T(8,128)(2,1)} collective-permute-done((bf16[256,2048]{1,0:T(8,128)(2,1)}, bf16[256,2048]{1,0:T(8,128)(2,1)}, u32[]{:S(2)}, u32[]{:S(2)}) %collective-permute-start.90) | collective-permute-done | bytes 1048608 | tf_op jit(solution)/shard_map/ppermute | solution.py:93
  797.6 4.8 collective-permute-done.89
  805.9 6.7 shard_map.285
  814.8 4.1 fusion
  831.4 13.7 %collective-permute-done.98 = bf16[1024,128]{1,0:T(8,128)(2,1)S(1)} collective-permute-done((bf16[1024,128]{1,0:T(8,128)(2,1)S(1)}, bf16[1024,128]{1,0:T(8,128)(2,1)S(1)}, u32[]{:S(2)}, u32[]{:S(2)}) %collective-permute-start.98) | collective-permute-done | bytes 262176 | tf_op jit(solution)/shard_map/ppermute | solution.py:694
  846.2 4.9 shard_map.286
  853.1 38.7 %shard_map.287 = (f32[4096,128]{1,0:T(8,128)}, f32[4096,128]{1,0:T(8,128)}, f32[4096,128]{1,0:T(8,128)}) custom-call(s32[1]{0:T(128)} %copy.142.length_ref, bf16[4096,128]{1,0:T(8,128)(2,1)} %get-tuple-element.259.q_ref, bf16[4096,128]{1,0:T(8,128)(2,1)} %get-tuple-element.377.do_ref, f32[8,4096]{1,0:T(8,128)} %get-tuple-element.378.log_ref, ...), custom_call_target="tpu_custom_call" | custom-call | flops 32999999488 | bytes 90000000 | tf_op jit(solution)/shard_map/pallas_call | solution.py:576
  894.3 4.4 collective-permute-done.103
  900.1 10.0 shard_map.288
  927.6 7.6 collective-permute-done.112
  935.3 11.8 shard_map.289
  947.3 11.2 fusion.120
  976.9 6.7 collective-permute-done.119
  990.6 20.4 %collective-permute-done.117 = bf16[256,2048]{1,0:T(8,128)(2,1)S(1)} collective-permute-done((bf16[256,2048]{1,0:T(8,128)(2,1)S(1)}, bf16[256,2048]{1,0:T(8,128)(2,1)S(1)}, u32[]{:S(2)}, u32[]{:S(2)}) %collective-permute-start.117) | collective-permute-done | bytes 1048608 | tf_op jit(solution)/shard_map/ppermute | solution.py:93
  1021.0 14.8 %collective-permute-done.124.refs_1_ = bf16[192,2048]{1,0:T(8,128)(2,1)} collective-permute-done((bf16[192,2048]{1,0:T(8,128)(2,1)S(1)}, bf16[192,2048]{1,0:T(8,128)(2,1)}, u32[]{:S(2)}, u32[]{:S(2)}) %collective-permute-start.124) | collective-permute-done | bytes 786464 | tf_op jit(solution)/shard_map/ppermute | solution.py:93
  1039.9 16.2 %collective-permute-done.123 = bf16[448,2048]{1,0:T(8,128)(2,1)} collective-permute-done((bf16[448,2048]{1,0:T(8,128)(2,1)}, bf16[448,2048]{1,0:T(8,128)(2,1)}, u32[]{:S(2)}, u32[]{:S(2)}) %collective-permute-start.123) | collective-permute-done | bytes 1835040 | tf_op jit(solution)/shard_map/ppermute | solution.py:93
  1071.0 13.8 %collective-permute-done.129.refs_1_ = bf16[192,2048]{1,0:T(8,128)(2,1)S(1)} collective-permute-done((bf16[192,2048]{1,0:T(8,128)(2,1)S(1)}, bf16[192,2048]{1,0:T(8,128)(2,1)S(1)}, u32[]{:S(2)}, u32[]{:S(2)}) %collective-permute-start.129) | collective-permute-done | bytes 786464 | tf_op jit(solution)/shard_map/ppermute | solution.py:93
  1089.7 14.1 %collective-permute-done.128 = bf16[448,2048]{1,0:T(8,128)(2,1)} collective-permute-done((bf16[448,2048]{1,0:T(8,128)(2,1)}, bf16[448,2048]{1,0:T(8,128)(2,1)}, u32[]{:S(2)}, u32[]{:S(2)}) %collective-permute-start.128) | collective-permute-done | bytes 1835040 | tf_op jit(solution)/shard_map/ppermute | solution.py:93
  1122.0 6.8 shard_map.294
  1128.8 8.7 collective-permute-done.130
  1137.5 15.3 %collective-permute-done.131 = bf16[448,2048]{1,0:T(8,128)(2,1)S(1)} collective-permute-done((bf16[448,2048]{1,0:T(8,128)(2,1)}, bf16[448,2048]{1,0:T(8,128)(2,1)S(1)}, u32[]{:S(2)}, u32[]{:S(2)}) %collective-permute-start.131) | collective-permute-done | bytes 1835040 | tf_op jit(solution)/shard_map/ppermute | solution.py:93
  1173.7 5.3 collective-permute-done.139.refs_1_
  1180.0 4.2 shard_map.293
  (704 shorter events, 331.2 us)
Async XLA Ops:
  6.5 32.2 %collective-permute-start = (bf16[256,2176]{1,0:T(8,128)(2,1)}, bf16[256,2176]{1,0:T(8,128)(2,1)}, u32[]{:S(2)}, u32[]{:S(2)}) collective-permute-start(bf16[256,2176]{1,0:T(8,128)(2,1)} %pad_maximum_fusion.9.refs_0_), channel_id=1, source_target_pairs={{0,4},{4,8},{8,12},{12,0},{1,5},{5,9},{9,13},{13,1},{2,6},{6,10},{... | collective-permute-start | bytes 3342344 | tf_op jit(solution)/shard_map/ppermute | solution.py:93
  9.5 29.2 %collective-permute-start.1 = (bf16[256,2176]{1,0:T(8,128)(2,1)}, bf16[256,2176]{1,0:T(8,128)(2,1)}, u32[]{:S(2)}, u32[]{:S(2)}) collective-permute-start(bf16[256,2176]{1,0:T(8,128)(2,1)} %pad_maximum_fusion.9.refs_0_), channel_id=1, source_target_pairs={{0,2},{1,3},{2,0},{3,1},{4,6},{5,7},{6,4},{7,5},{8,10},{9,11},{10,... | collective-permute-start | bytes 3342344 | tf_op jit(solution)/shard_map/ppermute | solution.py:93
  11.0 59.5 %collective-permute-start.8 = (bf16[256,2176]{1,0:T(8,128)(2,1)}, bf16[256,2176]{1,0:T(8,128)(2,1)}, u32[]{:S(2)}, u32[]{:S(2)}) collective-permute-start(bf16[256,2176]{1,0:T(8,128)(2,1)} %pad_maximum_fusion.9.refs_0_), channel_id=1, source_target_pairs={{0,1},{1,0},{2,3},{3,2},{4,5},{5,4},{6,7},{7,6},{8,9},{9,8},{10,11... | collective-permute-start | bytes 3342344 | tf_op jit(solution)/shard_map/ppermute | solution.py:93
  12.4 26.3 %collective-permute-start.2 = (bf16[1024,512]{1,0:T(8,128)(2,1)}, bf16[1024,512]{1,0:T(8,128)(2,1)}, u32[]{:S(2)}, u32[]{:S(2)}) collective-permute-start(bf16[1024,512]{1,0:T(8,128)(2,1)} %get-tuple-element.494), channel_id=1, source_target_pairs={{0,16},{16,0},{1,17},{17,1},{2,18},{18,2},{3,19},{19,3},{4,20},{20... | collective-permute-start | bytes 3145736 | tf_op jit(solution)/shard_map/ppermute | solution.py:93
  14.0 46.8 %collective-permute-start.5 = (bf16[1024,512]{1,0:T(8,128)(2,1)}, bf16[1024,512]{1,0:T(8,128)(2,1)}, u32[]{:S(2)}, u32[]{:S(2)}) collective-permute-start(bf16[1024,512]{1,0:T(8,128)(2,1)} %get-tuple-element.493), channel_id=1, source_target_pairs={{0,16},{16,0},{1,17},{17,1},{2,18},{18,2},{3,19},{19,3},{4,20},{20... | collective-permute-start | bytes 3145736 | tf_op jit(solution)/shard_map/ppermute | solution.py:93
  38.7 27.9 %collective-permute-start.3 = (bf16[256,2176]{1,0:T(8,128)(2,1)}, bf16[256,2176]{1,0:T(8,128)(2,1)}, u32[]{:S(2)}, u32[]{:S(2)}) collective-permute-start(bf16[256,2176]{1,0:T(8,128)(2,1)} %collective-permute-done.refs_0_), channel_id=1, source_target_pairs={{0,4},{4,8},{8,12},{12,0},{1,5},{5,9},{9,13},{13,1},{2,6},{6,10},{... | collective-permute-start | bytes 3342344 | tf_op jit(solution)/shard_map/ppermute | solution.py:93
  40.3 26.4 %collective-permute-start.4 = (bf16[256,2176]{1,0:T(8,128)(2,1)}, bf16[256,2176]{1,0:T(8,128)(2,1)}, u32[]{:S(2)}, u32[]{:S(2)}) collective-permute-start(bf16[256,2176]{1,0:T(8,128)(2,1)} %collective-permute-done.refs_0_), channel_id=1, source_target_pairs={{0,2},{1,3},{2,0},{3,1},{4,6},{5,7},{6,4},{7,5},{8,10},{9,11},{10,... | collective-permute-start | bytes 3342344 | tf_op jit(solution)/shard_map/ppermute | solution.py:93
  66.6 27.3 %collective-permute-start.6 = (bf16[256,2176]{1,0:T(8,128)(2,1)}, bf16[256,2176]{1,0:T(8,128)(2,1)}, u32[]{:S(2)}, u32[]{:S(2)}) collective-permute-start(bf16[256,2176]{1,0:T(8,128)(2,1)} %collective-permute-done.3.refs_0_), channel_id=1, source_target_pairs={{0,4},{4,8},{8,12},{12,0},{1,5},{5,9},{9,13},{13,1},{2,6},{6,10},{... | collective-permute-start | bytes 3342344 | tf_op jit(solution)/shard_map/ppermute | solution.py:93
  68.0 27.5 %collective-permute-start.7 = (bf16[256,2176]{1,0:T(8,128)(2,1)}, bf16[256,2176]{1,0:T(8,128)(2,1)}, u32[]{:S(2)}, u32[]{:S(2)}) collective-permute-start(bf16[256,2176]{1,0:T(8,128)(2,1)} %collective-permute-done.3.refs_0_), channel_id=1, source_target_pairs={{0,2},{1,3},{2,0},{3,1},{4,6},{5,7},{6,4},{7,5},{8,10},{9,11},{10,... | collective-permute-start | bytes 3342344 | tf_op jit(solution)/shard_map/ppermute | solution.py:93
  70.4 41.6 %collective-permute-start.12 = (bf16[256,2176]{1,0:T(8,128)(2,1)}, bf16[256,2176]{1,0:T(8,128)(2,1)S(1)}, u32[]{:S(2)}, u32[]{:S(2)}) collective-permute-start(bf16[256,2176]{1,0:T(8,128)(2,1)} %collective-permute-done.refs_0_), channel_id=1, source_target_pairs={{0,1},{1,0},{2,3},{3,2},{4,5},{5,4},{6,7},{7,6},{8,9},{9,8},{10,11... | collective-permute-start | bytes 3342344 | tf_op jit(solution)/shard_map/ppermute | solution.py:93
  70.4 41.6 %collective-permute-start.13 = (bf16[256,2176]{1,0:T(8,128)(2,1)}, bf16[256,2176]{1,0:T(8,128)(2,1)S(1)}, u32[]{:S(2)}, u32[]{:S(2)}) collective-permute-start(bf16[256,2176]{1,0:T(8,128)(2,1)} %collective-permute-done.4.refs_1_), channel_id=1, source_target_pairs={{0,1},{1,0},{2,3},{3,2},{4,5},{5,4},{6,7},{7,6},{8,9},{9,8},{10,11... | collective-permute-start | bytes 3342344 | tf_op jit(solution)/shard_map/ppermute | solution.py:93
  85.9 35.9 %collective-permute-start.14 = (bf16[1024,512]{1,0:T(8,128)(2,1)S(1)}, bf16[1024,512]{1,0:T(8,128)(2,1)S(1)}, u32[]{:S(2)}, u32[]{:S(2)}) collective-permute-start(bf16[1024,512]{1,0:T(8,128)(2,1)S(1)} %copy-done.63), channel_id=1, source_target_pairs={{0,16},{16,0},{1,17},{17,1},{2,18},{18,2},{3,19},{19,3},{4,20},{20... | collective-permute-start | bytes 3145736 | tf_op jit(solution)/shard_map/ppermute | solution.py:93
  95.4 26.6 %collective-permute-start.11 = (bf16[256,2176]{1,0:T(8,128)(2,1)}, bf16[256,2176]{1,0:T(8,128)(2,1)S(1)}, u32[]{:S(2)}, u32[]{:S(2)}) collective-permute-start(bf16[256,2176]{1,0:T(8,128)(2,1)} %collective-permute-done.6.refs_0_), channel_id=1, source_target_pairs={{0,2},{1,3},{2,0},{3,1},{4,6},{5,7},{6,4},{7,5},{8,10},{9,11},{10,... | collective-permute-start | bytes 3342344 | tf_op jit(solution)/shard_map/ppermute | solution.py:93
  109.9 55.7 %collective-permute-start.26 = (bf16[256,2048]{1,0:T(8,128)(2,1)S(1)}, bf16[256,2048]{1,0:T(8,128)(2,1)}, u32[]{:S(2)}, u32[]{:S(2)}) collective-permute-start(bf16[256,2048]{1,0:T(8,128)(2,1)S(1)} %copy-done.62), channel_id=1, source_target_pairs={{0,16},{16,0},{1,17},{17,1},{2,18},{18,2},{3,19},{19,3},{4,20},{20... | collective-permute-start | bytes 3145736 | tf_op jit(solution)/shard_map/ppermute | solution.py:93
  124.4 67.4 %collective-permute-start.27 = (bf16[256,2048]{1,0:T(8,128)(2,1)}, bf16[256,2048]{1,0:T(8,128)(2,1)}, u32[]{:S(2)}, u32[]{:S(2)}) collective-permute-start(bf16[256,2048]{1,0:T(8,128)(2,1)} %get-tuple-element.489), channel_id=1, source_target_pairs={{0,16},{16,0},{1,17},{17,1},{2,18},{18,2},{3,19},{19,3},{4,20},{20... | collective-permute-start | bytes 3145736 | tf_op jit(solution)/shard_map/ppermute | solution.py:93
  224.9 25.6 %collective-permute-start.32 = (bf16[256,2048]{1,0:T(8,128)(2,1)S(1)}, bf16[256,2048]{1,0:T(8,128)(2,1)S(1)}, u32[]{:S(2)}, u32[]{:S(2)}) collective-permute-start(bf16[256,2048]{1,0:T(8,128)(2,1)S(1)} %fusion.46), channel_id=1, source_target_pairs={{0,2},{1,3},{2,0},{3,1},{4,6},{5,7},{6,4},{7,5},{8,10},{9,11},{10,... | collective-permute-start | bytes 3145736 | tf_op jit(solution)/shard_map/ppermute | solution.py:93
  252.0 28.7 %collective-permute-start.33 = (bf16[256,2048]{1,0:T(8,128)(2,1)S(1)}, bf16[256,2048]{1,0:T(8,128)(2,1)S(1)}, u32[]{:S(2)}, u32[]{:S(2)}) collective-permute-start(bf16[256,2048]{1,0:T(8,128)(2,1)S(1)} %multiply_convert_fusion.refs_0_), channel_id=1, source_target_pairs={{0,4},{4,8},{8,12},{12,0},{1,5},{5,9},{9,13},{13,1},{2,6},{6,10},{... | collective-permute-start | bytes 3145736 | tf_op jit(solution)/shard_map/ppermute | solution.py:93
  264.1 26.3 %collective-permute-start.37 = (bf16[256,2048]{1,0:T(8,128)(2,1)S(1)}, bf16[256,2048]{1,0:T(8,128)(2,1)S(1)}, u32[]{:S(2)}, u32[]{:S(2)}) collective-permute-start(bf16[256,2048]{1,0:T(8,128)(2,1)S(1)} %multiply_convert_fusion.refs_0_), channel_id=1, source_target_pairs={{0,1},{1,0},{2,3},{3,2},{4,5},{5,4},{6,7},{7,6},{8,9},{9,8},{10,11... | collective-permute-start | bytes 3145736 | tf_op jit(solution)/shard_map/ppermute | solution.py:93
  289.2 27.7 %collective-permute-start.35 = (bf16[256,2048]{1,0:T(8,128)(2,1)S(1)}, bf16[256,2048]{1,0:T(8,128)(2,1)S(1)}, u32[]{:S(2)}, u32[]{:S(2)}) collective-permute-start(bf16[256,2048]{1,0:T(8,128)(2,1)S(1)} %collective-permute-done.33.refs_0_), channel_id=1, source_target_pairs={{0,4},{4,8},{8,12},{12,0},{1,5},{5,9},{9,13},{13,1},{2,6},{6,10},{... | collective-permute-start | bytes 3145736 | tf_op jit(solution)/shard_map/ppermute | solution.py:93
  290.1 26.9 %collective-permute-start.36 = (bf16[256,2048]{1,0:T(8,128)(2,1)S(1)}, bf16[256,2048]{1,0:T(8,128)(2,1)}, u32[]{:S(2)}, u32[]{:S(2)}) collective-permute-start(bf16[256,2048]{1,0:T(8,128)(2,1)S(1)} %collective-permute-done.33.refs_0_), channel_id=1, source_target_pairs={{0,2},{1,3},{2,0},{3,1},{4,6},{5,7},{6,4},{7,5},{8,10},{9,11},{10,... | collective-permute-start | bytes 3145736 | tf_op jit(solution)/shard_map/ppermute | solution.py:93
  290.4 27.1 %collective-permute-start.41 = (bf16[256,2048]{1,0:T(8,128)(2,1)S(1)}, bf16[256,2048]{1,0:T(8,128)(2,1)}, u32[]{:S(2)}, u32[]{:S(2)}) collective-permute-start(bf16[256,2048]{1,0:T(8,128)(2,1)S(1)} %collective-permute-done.33.refs_0_), channel_id=1, source_target_pairs={{0,1},{1,0},{2,3},{3,2},{4,5},{5,4},{6,7},{7,6},{8,9},{9,8},{10,11... | collective-permute-start | bytes 3145736 | tf_op jit(solution)/shard_map/ppermute | solution.py:93
  317.0 27.4 %collective-permute-start.39 = (bf16[256,2048]{1,0:T(8,128)(2,1)S(1)}, bf16[256,2048]{1,0:T(8,128)(2,1)S(1)}, u32[]{:S(2)}, u32[]{:S(2)}) collective-permute-start(bf16[256,2048]{1,0:T(8,128)(2,1)S(1)} %collective-permute-done.35.refs_0_), channel_id=1, source_target_pairs={{0,4},{4,8},{8,12},{12,0},{1,5},{5,9},{9,13},{13,1},{2,6},{6,10},{... | collective-permute-start | bytes 3145736 | tf_op jit(solution)/shard_map/ppermute | solution.py:93
  317.0 27.3 %collective-permute-start.40 = (bf16[256,2048]{1,0:T(8,128)(2,1)S(1)}, bf16[256,2048]{1,0:T(8,128)(2,1)S(1)}, u32[]{:S(2)}, u32[]{:S(2)}) collective-permute-start(bf16[256,2048]{1,0:T(8,128)(2,1)S(1)} %collective-permute-done.35.refs_0_), channel_id=1, source_target_pairs={{0,2},{1,3},{2,0},{3,1},{4,6},{5,7},{6,4},{7,5},{8,10},{9,11},{10,... | collective-permute-start | bytes 3145736 | tf_op jit(solution)/shard_map/ppermute | solution.py:93
  317.4 27.8 %collective-permute-start.43 = (bf16[256,2048]{1,0:T(8,128)(2,1)S(1)}, bf16[256,2048]{1,0:T(8,128)(2,1)}, u32[]{:S(2)}, u32[]{:S(2)}) collective-permute-start(bf16[256,2048]{1,0:T(8,128)(2,1)S(1)} %collective-permute-done.35.refs_0_), channel_id=1, source_target_pairs={{0,1},{1,0},{2,3},{3,2},{4,5},{5,4},{6,7},{7,6},{8,9},{9,8},{10,11... | collective-permute-start | bytes 3145736 | tf_op jit(solution)/shard_map/ppermute | solution.py:93
  344.4 26.3 %collective-permute-start.46 = (bf16[2,256,2048]{2,1,0:T(8,128)(2,1)}, bf16[2,256,2048]{2,1,0:T(8,128)(2,1)S(1)}, u32[]{:S(2)}, u32[]{:S(2)}) collective-permute-start(bf16[2,256,2048]{2,1,0:T(8,128)(2,1)} %get-tuple-element.283), channel_id=1, source_target_pairs={{0,1},{1,0},{2,3},{3,2},{4,5},{5,4},{6,7},{7,6},{8,9},{9,8},{10,11... | collective-permute-start | bytes 6291464 | tf_op jit(solution)/shard_map/ppermute | solution.py:93
  345.2 29.8 %collective-permute-start.49 = (bf16[256,2048]{1,0:T(8,128)(2,1)S(1)}, bf16[256,2048]{1,0:T(8,128)(2,1)}, u32[]{:S(2)}, u32[]{:S(2)}) collective-permute-start(bf16[256,2048]{1,0:T(8,128)(2,1)S(1)} %collective-permute-done.39.refs_0_), channel_id=1, source_target_pairs={{0,1},{1,0},{2,3},{3,2},{4,5},{5,4},{6,7},{7,6},{8,9},{9,8},{10,11... | collective-permute-start | bytes 3145736 | tf_op jit(solution)/shard_map/ppermute | solution.py:93
  370.1 53.6 %collective-permute-start.54 = (bf16[2,256,2048]{2,1,0:T(8,128)(2,1)}, bf16[2,256,2048]{2,1,0:T(8,128)(2,1)}, u32[]{:S(2)}, u32[]{:S(2)}) collective-permute-start(bf16[2,256,2048]{2,1,0:T(8,128)(2,1)} %get-tuple-element.274), channel_id=1, source_target_pairs={{0,1},{1,0},{2,3},{3,2},{4,5},{5,4},{6,7},{7,6},{8,9},{9,8},{10,11... | collective-permute-start | bytes 6291464 | tf_op jit(solution)/shard_map/ppermute | solution.py:93
  370.7 26.8 %collective-permute-start.45 = (bf16[2,256,2048]{2,1,0:T(8,128)(2,1)}, bf16[2,256,2048]{2,1,0:T(8,128)(2,1)}, u32[]{:S(2)}, u32[]{:S(2)}) collective-permute-start(bf16[2,256,2048]{2,1,0:T(8,128)(2,1)} %get-tuple-element.292), channel_id=1, source_target_pairs={{0,1},{1,0},{2,3},{3,2},{4,5},{5,4},{6,7},{7,6},{8,9},{9,8},{10,11... | collective-permute-start | bytes 6291464 | tf_op jit(solution)/shard_map/ppermute | solution.py:93
  396.3 26.2 %collective-permute-start.51 = (bf16[2,256,2048]{2,1,0:T(8,128)(2,1)}, bf16[2,256,2048]{2,1,0:T(8,128)(2,1)S(1)}, u32[]{:S(2)}, u32[]{:S(2)}) collective-permute-start(bf16[2,256,2048]{2,1,0:T(8,128)(2,1)} %get-tuple-element.302), channel_id=1, source_target_pairs={{0,1},{1,0},{2,3},{3,2},{4,5},{5,4},{6,7},{7,6},{8,9},{9,8},{10,11... | collective-permute-start | bytes 6291464 | tf_op jit(solution)/shard_map/ppermute | solution.py:93
  423.3 26.1 %collective-permute-start.53 = (bf16[256,2048]{1,0:T(8,128)(2,1)S(1)}, bf16[256,2048]{1,0:T(8,128)(2,1)S(1)}, u32[]{:S(2)}, u32[]{:S(2)}) collective-permute-start(bf16[256,2048]{1,0:T(8,128)(2,1)S(1)} %fusion.33), channel_id=1, source_target_pairs={{0,4},{4,8},{8,12},{12,0},{1,5},{5,9},{9,13},{13,1},{2,6},{6,10},{... | collective-permute-start | bytes 3145736 | tf_op jit(solution)/shard_map/ppermute | solution.py:93
  423.4 26.0 %collective-permute-start.52 = (bf16[256,2048]{1,0:T(8,128)(2,1)S(1)}, bf16[256,2048]{1,0:T(8,128)(2,1)S(1)}, u32[]{:S(2)}, u32[]{:S(2)}) collective-permute-start(bf16[256,2048]{1,0:T(8,128)(2,1)S(1)} %fusion.47), channel_id=1, source_target_pairs={{0,2},{1,3},{2,0},{3,1},{4,6},{5,7},{6,4},{7,5},{8,10},{9,11},{10,... | collective-permute-start | bytes 3145736 | tf_op jit(solution)/shard_map/ppermute | solution.py:93
  505.9 47.2 %collective-permute-start.69 = (bf16[256,2048]{1,0:T(8,128)(2,1)}, bf16[256,2048]{1,0:T(8,128)(2,1)S(1)}, u32[]{:S(2)}, u32[]{:S(2)}) collective-permute-start(bf16[256,2048]{1,0:T(8,128)(2,1)} %multiply_convert_fusion.1.refs_0_), channel_id=1, source_target_pairs={{0,1},{1,0},{2,3},{3,2},{4,5},{5,4},{6,7},{7,6},{8,9},{9,8},{10,11... | collective-permute-start | bytes 3145736 | tf_op jit(solution)/shard_map/ppermute | solution.py:93
  534.5 42.8 %collective-permute-start.67 = (bf16[256,2048]{1,0:T(8,128)(2,1)}, bf16[256,2048]{1,0:T(8,128)(2,1)}, u32[]{:S(2)}, u32[]{:S(2)}) collective-permute-start(bf16[256,2048]{1,0:T(8,128)(2,1)} %collective-permute-done.59.refs_0_), channel_id=1, source_target_pairs={{0,1},{1,0},{2,3},{3,2},{4,5},{5,4},{6,7},{7,6},{8,9},{9,8},{10,11... | collective-permute-start | bytes 3145736 | tf_op jit(solution)/shard_map/ppermute | solution.py:93
  553.1 48.2 %collective-permute-start.65 = (bf16[256,2048]{1,0:T(8,128)(2,1)S(1)}, bf16[256,2048]{1,0:T(8,128)(2,1)}, u32[]{:S(2)}, u32[]{:S(2)}) collective-permute-start(bf16[256,2048]{1,0:T(8,128)(2,1)S(1)} %collective-permute-done.61.refs_0_), channel_id=1, source_target_pairs={{0,1},{1,0},{2,3},{3,2},{4,5},{5,4},{6,7},{7,6},{8,9},{9,8},{10,11... | collective-permute-start | bytes 3145736 | tf_op jit(solution)/shard_map/ppermute | solution.py:93
  575.6 48.5 %collective-permute-start.80 = (bf16[2,272,2048]{2,1,0:T(8,128)(2,1)}, bf16[2,272,2048]{2,1,0:T(8,128)(2,1)S(1)}, u32[]{:S(2)}, u32[]{:S(2)}) collective-permute-start(bf16[2,272,2048]{2,1,0:T(8,128)(2,1)} %get-tuple-element.349), channel_id=1, source_target_pairs={{0,1},{1,0},{2,3},{3,2},{4,5},{5,4},{6,7},{7,6},{8,9},{9,8},{10,11... | collective-permute-start | bytes 6684680 | tf_op jit(solution)/shard_map/ppermute | solution.py:93
  575.7 25.6 %collective-permute-start.74 = (bf16[256,2048]{1,0:T(8,128)(2,1)S(1)}, bf16[256,2048]{1,0:T(8,128)(2,1)S(1)}, u32[]{:S(2)}, u32[]{:S(2)}) collective-permute-start(bf16[256,2048]{1,0:T(8,128)(2,1)S(1)} %collective-permute-done.63.refs_0_), channel_id=1, source_target_pairs={{0,2},{1,3},{2,0},{3,1},{4,6},{5,7},{6,4},{7,5},{8,10},{9,11},{10,... | collective-permute-start | bytes 3145736 | tf_op jit(solution)/shard_map/ppermute | solution.py:93
  577.3 51.3 %collective-permute-start.75 = (bf16[256,2048]{1,0:T(8,128)(2,1)S(1)}, bf16[256,2048]{1,0:T(8,128)(2,1)}, u32[]{:S(2)}, u32[]{:S(2)}) collective-permute-start(bf16[256,2048]{1,0:T(8,128)(2,1)S(1)} %collective-permute-done.63.refs_0_), channel_id=1, source_target_pairs={{0,1},{1,0},{2,3},{3,2},{4,5},{5,4},{6,7},{7,6},{8,9},{9,8},{10,11... | collective-permute-start | bytes 3145736 | tf_op jit(solution)/shard_map/ppermute | solution.py:93
  601.3 48.6 %collective-permute-start.72 = (bf16[2,272,2048]{2,1,0:T(8,128)(2,1)}, bf16[2,272,2048]{2,1,0:T(8,128)(2,1)}, u32[]{:S(2)}, u32[]{:S(2)}) collective-permute-start(bf16[2,272,2048]{2,1,0:T(8,128)(2,1)} %get-tuple-element.332), channel_id=1, source_target_pairs={{0,1},{1,0},{2,3},{3,2},{4,5},{5,4},{6,7},{7,6},{8,9},{9,8},{10,11... | collective-permute-start | bytes 6684680 | tf_op jit(solution)/shard_map/ppermute | solution.py:93
  601.3 27.4 %collective-permute-start.76 = (bf16[256,2048]{1,0:T(8,128)(2,1)S(1)}, bf16[256,2048]{1,0:T(8,128)(2,1)}, u32[]{:S(2)}, u32[]{:S(2)}) collective-permute-start(bf16[256,2048]{1,0:T(8,128)(2,1)S(1)} %collective-permute-done.74.refs_1_), channel_id=1, source_target_pairs={{0,1},{1,0},{2,3},{3,2},{4,5},{5,4},{6,7},{7,6},{8,9},{9,8},{10,11... | collective-permute-start | bytes 3145736 | tf_op jit(solution)/shard_map/ppermute | solution.py:93
  624.0 30.8 %collective-permute-start.71 = (bf16[2,272,2048]{2,1,0:T(8,128)(2,1)}, bf16[2,272,2048]{2,1,0:T(8,128)(2,1)}, u32[]{:S(2)}, u32[]{:S(2)}) collective-permute-start(bf16[2,272,2048]{2,1,0:T(8,128)(2,1)} %get-tuple-element.330), channel_id=1, source_target_pairs={{0,1},{1,0},{2,3},{3,2},{4,5},{5,4},{6,7},{7,6},{8,9},{9,8},{10,11... | collective-permute-start | bytes 6684680 | tf_op jit(solution)/shard_map/ppermute | solution.py:93
  649.4 30.8 %collective-permute-start.77 = (bf16[2,272,2048]{2,1,0:T(8,128)(2,1)}, bf16[2,272,2048]{2,1,0:T(8,128)(2,1)S(1)}, u32[]{:S(2)}, u32[]{:S(2)}) collective-permute-start(bf16[2,272,2048]{2,1,0:T(8,128)(2,1)} %get-tuple-element.341), channel_id=1, source_target_pairs={{0,1},{1,0},{2,3},{3,2},{4,5},{5,4},{6,7},{7,6},{8,9},{9,8},{10,11... | collective-permute-start | bytes 6684680 | tf_op jit(solution)/shard_map/ppermute | solution.py:93
  653.2 26.6 %collective-permute-start.73 = (bf16[272,2048]{1,0:T(8,128)(2,1)S(1)}, bf16[272,2048]{1,0:T(8,128)(2,1)S(1)}, u32[]{:S(2)}, u32[]{:S(2)}) collective-permute-start(bf16[272,2048]{1,0:T(8,128)(2,1)S(1)} %fusion.43), channel_id=1, source_target_pairs={{0,2},{1,3},{2,0},{3,1},{4,6},{5,7},{6,4},{7,5},{8,10},{9,11},{10,... | collective-permute-start | bytes 3342344 | tf_op jit(solution)/shard_map/ppermute | solution.py:93
  681.0 27.7 %collective-permute-start.79 = (bf16[272,2048]{1,0:T(8,128)(2,1)S(1)}, bf16[272,2048]{1,0:T(8,128)(2,1)}, u32[]{:S(2)}, u32[]{:S(2)}) collective-permute-start(bf16[272,2048]{1,0:T(8,128)(2,1)S(1)} %fusion.14), channel_id=1, source_target_pairs={{0,4},{4,8},{8,12},{12,0},{1,5},{5,9},{9,13},{13,1},{2,6},{6,10},{... | collective-permute-start | bytes 3342344 | tf_op jit(solution)/shard_map/ppermute | solution.py:93
  681.3 27.3 %collective-permute-start.78 = (bf16[272,2048]{1,0:T(8,128)(2,1)S(1)}, bf16[272,2048]{1,0:T(8,128)(2,1)}, u32[]{:S(2)}, u32[]{:S(2)}) collective-permute-start(bf16[272,2048]{1,0:T(8,128)(2,1)S(1)} %fusion.42), channel_id=1, source_target_pairs={{0,2},{1,3},{2,0},{3,1},{4,6},{5,7},{6,4},{7,5},{8,10},{9,11},{10,... | collective-permute-start | bytes 3342344 | tf_op jit(solution)/shard_map/ppermute | solution.py:93
  702.9 35.0 %collective-permute-start.83 = (bf16[1024,512]{1,0:T(8,128)(2,1)}, bf16[1024,512]{1,0:T(8,128)(2,1)}, u32[]{:S(2)}, u32[]{:S(2)}) collective-permute-start(bf16[1024,512]{1,0:T(8,128)(2,1)} %get-tuple-element.480), channel_id=1, source_target_pairs={{0,16},{16,0},{1,17},{17,1},{2,18},{18,2},{3,19},{19,3},{4,20},{20... | collective-permute-start | bytes 3145736 | tf_op jit(solution)/shard_map/ppermute | solution.py:93
  702.9 61.2 %collective-permute-start.86 = (bf16[1024,512]{1,0:T(8,128)(2,1)}, bf16[1024,512]{1,0:T(8,128)(2,1)}, u32[]{:S(2)}, u32[]{:S(2)}) collective-permute-start(bf16[1024,512]{1,0:T(8,128)(2,1)} %get-tuple-element.479), channel_id=1, source_target_pairs={{0,16},{16,0},{1,17},{17,1},{2,18},{18,2},{3,19},{19,3},{4,20},{20... | collective-permute-start | bytes 3145736 | tf_op jit(solution)/shard_map/ppermute | solution.py:93
  710.7 26.6 %collective-permute-start.82 = (bf16[272,2048]{1,0:T(8,128)(2,1)S(1)}, bf16[272,2048]{1,0:T(8,128)(2,1)S(1)}, u32[]{:S(2)}, u32[]{:S(2)}) collective-permute-start(bf16[272,2048]{1,0:T(8,128)(2,1)S(1)} %fusion.12), channel_id=1, source_target_pairs={{0,4},{4,8},{8,12},{12,0},{1,5},{5,9},{9,13},{13,1},{2,6},{6,10},{... | collective-permute-start | bytes 3342344 | tf_op jit(solution)/shard_map/ppermute | solution.py:93
  737.9 25.7 %collective-permute-start.85 = (bf16[272,2048]{1,0:T(8,128)(2,1)S(1)}, bf16[272,2048]{1,0:T(8,128)(2,1)S(1)}, u32[]{:S(2)}, u32[]{:S(2)}) collective-permute-start(bf16[272,2048]{1,0:T(8,128)(2,1)S(1)} %fusion.16), channel_id=1, source_target_pairs={{0,4},{4,8},{8,12},{12,0},{1,5},{5,9},{9,13},{13,1},{2,6},{6,10},{... | collective-permute-start | bytes 3342344 | tf_op jit(solution)/shard_map/ppermute | solution.py:93
  774.7 31.2 %collective-permute-start.92 = (bf16[1024,512]{1,0:T(8,128)(2,1)S(1)}, bf16[1024,512]{1,0:T(8,128)(2,1)S(1)}, u32[]{:S(2)}, u32[]{:S(2)}) collective-permute-start(bf16[1024,512]{1,0:T(8,128)(2,1)S(1)} %get-tuple-element.478), channel_id=1, source_target_pairs={{0,16},{16,0},{1,17},{17,1},{2,18},{18,2},{3,19},{19,3},{4,20},{20... | collective-permute-start | bytes 3145736 | tf_op jit(solution)/shard_map/ppermute | solution.py:93
  774.7 31.2 %collective-permute-start.93 = (bf16[256,2048]{1,0:T(8,128)(2,1)}, bf16[256,2048]{1,0:T(8,128)(2,1)}, u32[]{:S(2)}, u32[]{:S(2)}) collective-permute-start(bf16[256,2048]{1,0:T(8,128)(2,1)} %get-tuple-element.461.refs_0_), channel_id=1, source_target_pairs={{0,1},{1,0},{2,3},{3,2},{4,5},{5,4},{6,7},{7,6},{8,9},{9,8},{10,11... | collective-permute-start | bytes 3145736 | tf_op jit(solution)/shard_map/ppermute | solution.py:93
  802.5 43.8 %collective-permute-start.100 = (bf16[1024,512]{1,0:T(8,128)(2,1)}, bf16[1024,512]{1,0:T(8,128)(2,1)S(1)}, u32[]{:S(2)}, u32[]{:S(2)}) collective-permute-start(bf16[1024,512]{1,0:T(8,128)(2,1)} %get-tuple-element.477), channel_id=1, source_target_pairs={{0,16},{16,0},{1,17},{17,1},{2,18},{18,2},{3,19},{19,3},{4,20},{20... | collective-permute-start | bytes 3145736 | tf_op jit(solution)/shard_map/ppermute | solution.py:93
  805.8 88.5 %collective-permute-start.102 = (bf16[256,2048]{1,0:T(8,128)(2,1)}, bf16[256,2048]{1,0:T(8,128)(2,1)S(1)}, u32[]{:S(2)}, u32[]{:S(2)}) collective-permute-start(bf16[256,2048]{1,0:T(8,128)(2,1)} %get-tuple-element.476), channel_id=1, source_target_pairs={{0,16},{16,0},{1,17},{17,1},{2,18},{18,2},{3,19},{19,3},{4,20},{20... | collective-permute-start | bytes 3145736 | tf_op jit(solution)/shard_map/ppermute | solution.py:93
  829.4 98.2 %collective-permute-start.111 = (bf16[256,2048]{1,0:T(8,128)(2,1)}, bf16[256,2048]{1,0:T(8,128)(2,1)S(1)}, u32[]{:S(2)}, u32[]{:S(2)}) collective-permute-start(bf16[256,2048]{1,0:T(8,128)(2,1)} %get-tuple-element.475), channel_id=1, source_target_pairs={{0,16},{16,0},{1,17},{17,1},{2,18},{18,2},{3,19},{19,3},{4,20},{20... | collective-permute-start | bytes 3145736 | tf_op jit(solution)/shard_map/ppermute | solution.py:93
  851.1 40.7 %collective-permute-start.101 = (f32[18,2048]{1,0:T(8,128)S(1)}, f32[18,2048]{1,0:T(8,128)S(1)}, u32[]{:S(2)}, u32[]{:S(2)}) collective-permute-start(f32[18,2048]{1,0:T(8,128)S(1)} %add_add_fusion), channel_id=1, source_target_pairs={{0,16},{16,0},{1,17},{17,1},{2,18},{18,2},{3,19},{19,3},{4,20},{20... | collective-permute-start | bytes 442376 | tf_op jit(solution)/shard_map/ppermute | solution.py:252
  853.1 45.6 %collective-permute-start.103 = (bf16[4,64,2048]{2,1,0:T(8,128)(2,1)}, bf16[4,64,2048]{2,1,0:T(8,128)(2,1)S(1)}, u32[]{:S(2)}, u32[]{:S(2)}) collective-permute-start(bf16[4,64,2048]{2,1,0:T(8,128)(2,1)} %constant_dynamic-slice_fusion.2), channel_id=1, source_target_pairs={{0,16},{16,0},{1,17},{17,1},{2,18},{18,2},{3,19},{19,3},{4,20},{20... | collective-permute-start | bytes 3145736 | tf_op jit(solution)/shard_map/ppermute | solution.py:93
  983.6 31.8 %collective-permute-start.126 = (bf16[2,256,2048]{2,1,0:T(8,128)(2,1)}, bf16[2,256,2048]{2,1,0:T(8,128)(2,1)S(1)}, u32[]{:S(2)}, u32[]{:S(2)}) collective-permute-start(bf16[2,256,2048]{2,1,0:T(8,128)(2,1)} %bitcast.64), channel_id=1, source_target_pairs={{0,1},{1,0},{2,3},{3,2},{4,5},{5,4},{6,7},{7,6},{8,9},{9,8},{10,11... | collective-permute-start | bytes 6291464 | tf_op jit(solution)/shard_map/ppermute | solution.py:93
  983.6 29.1 %collective-permute-start.120 = (bf16[64,2048]{1,0:T(8,128)(2,1)S(1)}, bf16[64,2048]{1,0:T(8,128)(2,1)S(1)}, u32[]{:S(2)}, u32[]{:S(2)}) collective-permute-start(bf16[64,2048]{1,0:T(8,128)(2,1)S(1)} %collective-permute-done.119), channel_id=1, source_target_pairs={{0,4},{4,8},{8,12},{12,0},{1,5},{5,9},{9,13},{13,1},{2,6},{6,10},{... | collective-permute-start | bytes 786440 | tf_op jit(solution)/shard_map/ppermute | solution.py:93
  1012.8 43.4 %collective-permute-start.123 = (bf16[448,2048]{1,0:T(8,128)(2,1)}, bf16[448,2048]{1,0:T(8,128)(2,1)}, u32[]{:S(2)}, u32[]{:S(2)}) collective-permute-start(bf16[448,2048]{1,0:T(8,128)(2,1)} %pad_maximum_fusion.5), channel_id=1, source_target_pairs={{0,4},{4,8},{8,12},{12,0},{1,5},{5,9},{9,13},{13,1},{2,6},{6,10},{... | collective-permute-start | bytes 5505032 | tf_op jit(solution)/shard_map/ppermute | solution.py:93
  1016.2 41.2 %collective-permute-start.122 = (bf16[256,2048]{1,0:T(8,128)(2,1)}, bf16[256,2048]{1,0:T(8,128)(2,1)S(1)}, u32[]{:S(2)}, u32[]{:S(2)}) collective-permute-start(bf16[256,2048]{1,0:T(8,128)(2,1)} %fusion.51), channel_id=1, source_target_pairs={{0,2},{1,3},{2,0},{3,1},{4,6},{5,7},{6,4},{7,5},{8,10},{9,11},{10,... | collective-permute-start | bytes 3145736 | tf_op jit(solution)/shard_map/ppermute | solution.py:93
  1018.0 43.4 %collective-permute-start.125 = (bf16[4,64,2048]{2,1,0:T(8,128)(2,1)S(1)}, bf16[4,64,2048]{2,1,0:T(8,128)(2,1)}, u32[]{:S(2)}, u32[]{:S(2)}) collective-permute-start(bf16[4,64,2048]{2,1,0:T(8,128)(2,1)S(1)} %pad_maximum_fusion.12), channel_id=1, source_target_pairs={{0,16},{16,0},{1,17},{17,1},{2,18},{18,2},{3,19},{19,3},{4,20},{20... | collective-permute-start | bytes 3145736 | tf_op jit(solution)/shard_map/ppermute | solution.py:93
  1061.4 42.4 %collective-permute-start.128 = (bf16[448,2048]{1,0:T(8,128)(2,1)}, bf16[448,2048]{1,0:T(8,128)(2,1)}, u32[]{:S(2)}, u32[]{:S(2)}) collective-permute-start(bf16[448,2048]{1,0:T(8,128)(2,1)} %pad_maximum_fusion.6), channel_id=1, source_target_pairs={{0,4},{4,8},{8,12},{12,0},{1,5},{5,9},{9,13},{13,1},{2,6},{6,10},{... | collective-permute-start | bytes 5505032 | tf_op jit(solution)/shard_map/ppermute | solution.py:93
  1065.5 40.5 %collective-permute-start.127 = (bf16[256,2048]{1,0:T(8,128)(2,1)S(1)}, bf16[256,2048]{1,0:T(8,128)(2,1)S(1)}, u32[]{:S(2)}, u32[]{:S(2)}) collective-permute-start(bf16[256,2048]{1,0:T(8,128)(2,1)S(1)} %copy-done.60), channel_id=1, source_target_pairs={{0,2},{1,3},{2,0},{3,1},{4,6},{5,7},{6,4},{7,5},{8,10},{9,11},{10,... | collective-permute-start | bytes 3145736 | tf_op jit(solution)/shard_map/ppermute | solution.py:93
  1111.3 41.6 %collective-permute-start.131 = (bf16[448,2048]{1,0:T(8,128)(2,1)}, bf16[448,2048]{1,0:T(8,128)(2,1)S(1)}, u32[]{:S(2)}, u32[]{:S(2)}) collective-permute-start(bf16[448,2048]{1,0:T(8,128)(2,1)} %pad_maximum_fusion.7), channel_id=1, source_target_pairs={{0,4},{4,8},{8,12},{12,0},{1,5},{5,9},{9,13},{13,1},{2,6},{6,10},{... | collective-permute-start | bytes 5505032 | tf_op jit(solution)/shard_map/ppermute | solution.py:93
  1119.1 36.3 %collective-permute-start.140 = (bf16[192,2048]{1,0:T(8,128)(2,1)}, bf16[192,2048]{1,0:T(8,128)(2,1)S(1)}, u32[]{:S(2)}, u32[]{:S(2)}) collective-permute-start(bf16[192,2048]{1,0:T(8,128)(2,1)} %slice.304.refs_0_), channel_id=1, source_target_pairs={{0,16},{16,0},{1,17},{17,1},{2,18},{18,2},{3,19},{19,3},{4,20},{20... | collective-permute-start | bytes 2359304 | tf_op jit(solution)/shard_map/ppermute | solution.py:93
  (215 other events, 2802.2 us)

commit v4 on v3

--- a/solution.py
+++ b/solution.py
@@ -144,6 +144,10 @@
         precision=lax.Precision.HIGHEST,
     )
     return moved.reshape(blocks.shape)
+
+
+def after_exchange(values, token):
+    return together(values, partner(token[:16, :HD]))[0]
 
 
 def gather_expert(rows):
@@ -1522,7 +1526,7 @@
         pending = []
 
         def product(left, right, axis):
-            shares = parts(left, right, axis)
+            shares = parts(after_exchange(left, left), right, axis)
             halves = zip(*(jnp.split(share, 2) for share in shares))
             return [list(half) for half in halves]
 

time: 1190 us -> 1190 us (level)
  no operation moved by 1% of the time
where the time goes in v4:
time: 1190 us
  waiting for transfers between devices  462 us (39%)
  Pallas kernels  331 us (28%)
  other arithmetic  124 us (10%)
  starting transfers between devices  109 us (9%)
  matrix products  89.2 us (7%)
  local copies, waits for them, and re-layouts  64.9 us (5%)
    ppermute x108, waiting for transfers between devices, moved(): return jax.tree.map(lambda v: lax.ppermute(v, axis, pairs), values)  394 us
    pallas_call x16, Pallas kernels, chunk_call(): pl.pallas_call(kernel, grid_spec=pltpu.PrefetchScalarGridSpec(num_scalar_...  219 us
    dot_general x19, matrix products, contract(): lax.dot_general(left, right, (((left_dim,), (right_dim,)), ((), ())), pre...  86.6 us
    ppermute x108, starting transfers between devices, moved(): return jax.tree.map(lambda v: lax.ppermute(v, axis, pairs), values)  74.8 us
    pallas_call x1, Pallas kernels, flash_backward(): pl.pallas_call(functools.partial(flash_backward_kernel, block=block), gri...  38.7 us
    ppermute x6, waiting for transfers between devices, permute_by(): lax.ppermute(values, axis, tuple(((i, (i + distance) % size) for i in ran...  36.4 us
    pallas_call x4, Pallas kernels, block_call(): pl.pallas_call(kernel, grid_spec=pltpu.PrefetchScalarGridSpec(num_scalar_...  34.1 us
    ppermute x27, waiting for transfers between devices, small_sum(): lax.ppermute(values, axis, tuple(((i, i ^ bits) for i in range(size))))  31.5 us
  transfers between devices with their start and end apart: 141, of which 52 were waited for; matrix products, arithmetic and copies ran while one was open for 20% of the time, Pallas kernels for 28%

profile of v4, /device:TPU:0, one launch (start us, length us, event | category | flops | bytes accessed | tf_op | source)
XLA Modules:
  0.0 1186.7 jit_solution(13354785597928015064)
XLA Ops:
  19.2 9.4 fusion.56
  28.5 10.2 collective-permute-done.2
  48.6 12.2 %collective-permute-done.5 = bf16[1024,512]{1,0:T(8,128)(2,1)} collective-permute-done((bf16[1024,512]{1,0:T(8,128)(2,1)}, bf16[1024,512]{1,0:T(8,128)(2,1)}, u32[]{:S(2)}, u32[]{:S(2)}) %collective-permute-start.5) | collective-permute-done | bytes 1048608 | tf_op jit(solution)/shard_map/ppermute | solution.py:93
  62.3 4.3 collective-permute-done.3.refs_0_
  70.9 8.6 shard_map.271
  79.6 6.3 collective-permute-done.10
  87.4 6.5 collective-permute-done.6.refs_0_
  96.6 13.3 %collective-permute-done.15 = s32[8,128]{1,0:T(8,128)S(1)} collective-permute-done((s32[8,128]{1,0:T(8,128)S(1)}, s32[8,128]{1,0:T(8,128)S(1)}, u32[]{:S(2)}, u32[]{:S(2)}) %collective-permute-start.15) | collective-permute-done | bytes 4128 | tf_op jit(solution)/shard_map/ppermute | solution.py:256
  113.4 8.5 shard_map.272
  124.9 8.5 shard_map.273
  134.8 9.0 shard_map.274
  158.1 7.5 shard_map.275
  165.6 26.2 %shard_map.276 = (bf16[4096,128]{1,0:T(8,128)(2,1)}, f32[8,4096]{1,0:T(8,128)}, bf16[4096,128]{1,0:T(8,128)(2,1)}) custom-call(s32[1]{0:T(128)} %copy.142.length_ref, s32[8]{0:T(128)} %pad_add_fusion.places_ref, bf16[4096,128]{1,0:T(8,128)(2,1)} %get-tuple-element.259.q_ref, bf16[4096,128]{1,0:T(8,128)(2,1)} %get-tuple-element.260.k_ref, ...), custom_call_target="tpu_custom_call" | custom-call | flops 22000001024 | bytes 60000000 | tf_op jit(solution)/shard_map/pallas_call | solution.py:505
  197.6 6.8 collective-permute-done.30
  204.4 10.3 collective-permute-done.29
  226.4 4.1 maximum_maximum_fusion.refs_6_.refs_10_
  230.6 19.9 %collective-permute-done.32 = bf16[256,2048]{1,0:T(8,128)(2,1)S(1)} collective-permute-done((bf16[256,2048]{1,0:T(8,128)(2,1)S(1)}, bf16[256,2048]{1,0:T(8,128)(2,1)S(1)}, u32[]{:S(2)}, u32[]{:S(2)}) %collective-permute-start.32) | collective-permute-done | bytes 1048608 | tf_op jit(solution)/shard_map/ppermute | solution.py:93
  252.0 5.3 collective-permute-start.33
  258.1 6.0 maximum_maximum_fusion.1.refs_7_.refs_11_
  264.2 16.6 %collective-permute-done.33.refs_0_ = bf16[256,2048]{1,0:T(8,128)(2,1)S(1)} collective-permute-done((bf16[256,2048]{1,0:T(8,128)(2,1)S(1)}, bf16[256,2048]{1,0:T(8,128)(2,1)S(1)}, u32[]{:S(2)}, u32[]{:S(2)}) %collective-permute-start.33) | collective-permute-done | bytes 1048608 | tf_op jit(solution)/shard_map/ppermute | solution.py:93
  283.6 5.6 pad_maximum_fusion.refs_8_.refs_9_
  291.4 21.0 %shard_map.277 = (bf16[2560,2048]{1,0:T(8,128)(2,1)}, bf16[2560,1024]{1,0:T(8,128)(2,1)}, bf16[2560,1024]{1,0:T(8,128)(2,1)}, bf16[2560,1024]{1,0:T(8,128)(2,1)}...) custom-call(s32[1]{0:T(128)} %bitcast.expert_ref, ...), custom_call_target="tpu_custom_call" | custom-call | flops 23100000256 | bytes 63000000 | tf_op jit(solution)/shard_map/pallas_call | solution.py:1272
  312.4 4.6 collective-permute-done.35.refs_0_
  320.8 21.2 %shard_map.278 = (bf16[2560,2048]{1,0:T(8,128)(2,1)}, bf16[2560,1024]{1,0:T(8,128)(2,1)}, bf16[2560,1024]{1,0:T(8,128)(2,1)}, bf16[2560,1024]{1,0:T(8,128)(2,1)}...) custom-call(s32[1]{0:T(128)} %bitcast.expert_ref, ...), custom_call_target="tpu_custom_call", output_to_operand_aliasing={{0}: (10, {}), {1}: (11, {}), {2}: (12, {}), {3}: (13, {}),... | custom-call | flops 23100000256 | bytes 63000000 | tf_op jit(solution)/shard_map/pallas_call | solution.py:1272
  348.7 21.2 %shard_map.279 = (bf16[2560,2048]{1,0:T(8,128)(2,1)}, bf16[2560,1024]{1,0:T(8,128)(2,1)}, bf16[2560,1024]{1,0:T(8,128)(2,1)}, bf16[2560,1024]{1,0:T(8,128)(2,1)}...) custom-call(s32[1]{0:T(128)} %bitcast.expert_ref, ...), custom_call_target="tpu_custom_call", output_to_operand_aliasing={{0}: (10, {}), {1}: (11, {}), {2}: (12, {}), {3}: (13, {}),... | custom-call | flops 23100000256 | bytes 63000000 | tf_op jit(solution)/shard_map/pallas_call | solution.py:1272
  375.0 21.2 %shard_map.280 = (bf16[2560,2048]{1,0:T(8,128)(2,1)}, bf16[2560,1024]{1,0:T(8,128)(2,1)}, bf16[2560,1024]{1,0:T(8,128)(2,1)}, bf16[2560,1024]{1,0:T(8,128)(2,1)}...) custom-call(s32[1]{0:T(128)} %bitcast.expert_ref, ...), custom_call_target="tpu_custom_call", output_to_operand_aliasing={{0}: (10, {}), {1}: (11, {}), {2}: (12, {}), {3}: (13, {}),... | custom-call | flops 23100000256 | bytes 63000000 | tf_op jit(solution)/shard_map/pallas_call | solution.py:1272
  400.3 21.8 %collective-permute-done.47 = bf16[256,2048]{1,0:T(8,128)(2,1)S(1)} collective-permute-done((bf16[256,2048]{1,0:T(8,128)(2,1)S(1)}, bf16[256,2048]{1,0:T(8,128)(2,1)S(1)}, u32[]{:S(2)}, u32[]{:S(2)}) %collective-permute-start.47) | collective-permute-done | bytes 1048608 | tf_op jit(solution)/shard_map/ppermute | solution.py:93
  426.6 22.8 %collective-permute-done.53 = bf16[256,2048]{1,0:T(8,128)(2,1)S(1)} collective-permute-done((bf16[256,2048]{1,0:T(8,128)(2,1)S(1)}, bf16[256,2048]{1,0:T(8,128)(2,1)S(1)}, u32[]{:S(2)}, u32[]{:S(2)}) %collective-permute-start.53) | collective-permute-done | bytes 1048608 | tf_op jit(solution)/shard_map/ppermute | solution.py:93
  451.5 23.6 %collective-permute-done.56 = bf16[256,2048]{1,0:T(8,128)(2,1)S(1)} collective-permute-done((bf16[256,2048]{1,0:T(8,128)(2,1)S(1)}, bf16[256,2048]{1,0:T(8,128)(2,1)S(1)}, u32[]{:S(2)}, u32[]{:S(2)}) %collective-permute-start.56) | collective-permute-done | bytes 1048608 | tf_op jit(solution)/shard_map/ppermute | solution.py:93
  477.9 21.9 %collective-permute-done.58 = bf16[256,2048]{1,0:T(8,128)(2,1)} collective-permute-done((bf16[256,2048]{1,0:T(8,128)(2,1)S(1)}, bf16[256,2048]{1,0:T(8,128)(2,1)}, u32[]{:S(2)}, u32[]{:S(2)}) %collective-permute-start.58) | collective-permute-done | bytes 1048608 | tf_op jit(solution)/shard_map/ppermute | solution.py:93
  505.9 23.2 %collective-permute-done.59.refs_0_ = bf16[256,2048]{1,0:T(8,128)(2,1)} collective-permute-done((bf16[256,2048]{1,0:T(8,128)(2,1)}, bf16[256,2048]{1,0:T(8,128)(2,1)}, u32[]{:S(2)}, u32[]{:S(2)}) %collective-permute-start.59) | collective-permute-done | bytes 1048608 | tf_op jit(solution)/shard_map/ppermute | solution.py:93
  535.0 17.6 %collective-permute-done.61.refs_0_ = bf16[256,2048]{1,0:T(8,128)(2,1)S(1)} collective-permute-done((bf16[256,2048]{1,0:T(8,128)(2,1)}, bf16[256,2048]{1,0:T(8,128)(2,1)S(1)}, u32[]{:S(2)}, u32[]{:S(2)}) %collective-permute-start.61) | collective-permute-done | bytes 1048608 | tf_op jit(solution)/shard_map/ppermute | solution.py:93
  554.6 20.9 %shard_map.281 = (f32[4,256]{1,0:T(4,128)}, bf16[2560,2048]{1,0:T(8,128)(2,1)}, bf16[2560,1024]{1,0:T(8,128)(2,1)}, bf16[2560,1024]{1,0:T(8,128)(2,1)}, bf16[2,2...) custom-call(s32[1]{0:T(128)} %bitcast.expert_ref, bf16[256,2048]{1,0:T(8,128)(2,1)} %multiply_convert_fusion.1.refs_0_, ...), custom_call_target="tpu_custom_call" | custom-call | flops 23100000256 | bytes 63000000 | tf_op jit(solution)/shard_map/pallas_call | solution.py:1272
  577.8 20.7 %shard_map.282 = (f32[4,256]{1,0:T(4,128)}, bf16[2560,2048]{1,0:T(8,128)(2,1)}, bf16[2560,1024]{1,0:T(8,128)(2,1)}, bf16[2560,1024]{1,0:T(8,128)(2,1)}, bf16[2,2...) custom-call(s32[1]{0:T(128)} %bitcast.expert_ref, ...), custom_call_target="tpu_custom_call", output_to_operand_aliasing={{1}: (13, {}), {2}: (14, {}), {3}: (15, {})} | custom-call | flops 23100000256 | bytes 63000000 | tf_op jit(solution)/shard_map/pallas_call | solution.py:1272
  602.8 21.2 %shard_map.283 = (f32[4,256]{1,0:T(4,128)}, bf16[2560,2048]{1,0:T(8,128)(2,1)}, bf16[2560,1024]{1,0:T(8,128)(2,1)}, bf16[2560,1024]{1,0:T(8,128)(2,1)}, bf16[2,2...) custom-call(s32[1]{0:T(128)} %bitcast.expert_ref, ...), custom_call_target="tpu_custom_call", output_to_operand_aliasing={{1}: (13, {}), {2}: (14, {}), {3}: (15, {})} | custom-call | flops 23100000256 | bytes 63000000 | tf_op jit(solution)/shard_map/pallas_call | solution.py:1272
  628.7 20.7 %shard_map.284 = (f32[4,256]{1,0:T(4,128)}, bf16[2560,2048]{1,0:T(8,128)(2,1)}, bf16[2560,1024]{1,0:T(8,128)(2,1)}, bf16[2560,1024]{1,0:T(8,128)(2,1)}, bf16[2,2...) custom-call(s32[1]{0:T(128)} %bitcast.expert_ref, ...), custom_call_target="tpu_custom_call", output_to_operand_aliasing={{1}: (13, {}), {2}: (14, {}), {3}: (15, {})} | custom-call | flops 23100000256 | bytes 63000000 | tf_op jit(solution)/shard_map/pallas_call | solution.py:1272
  657.4 22.5 %collective-permute-done.73 = bf16[272,2048]{1,0:T(8,128)(2,1)S(1)} collective-permute-done((bf16[272,2048]{1,0:T(8,128)(2,1)S(1)}, bf16[272,2048]{1,0:T(8,128)(2,1)S(1)}, u32[]{:S(2)}, u32[]{:S(2)}) %collective-permute-start.73) | collective-permute-done | bytes 1114144 | tf_op jit(solution)/shard_map/ppermute | solution.py:93
  683.0 16.9 %fusion.116 = (bf16[2048,1024]{1,0:T(8,128)(2,1)}, f32[2048,1024]{1,0:T(8,128)S(1)}) fusion(bf16[2560,2048]{1,0:T(8,128)(2,1)} %get-tuple-element.353, bf16[2560,1024]{1,0:T(8,128)(2,1)} %get-tuple-element.346), kind=kOutput, calls=%fused_computation.314 | convolution fusion | flops 10739515392 | bytes 28311552 | tf_op jit(solution)/shard_map/dot_general | solution.py:64
  712.9 16.9 %fusion.118 = (bf16[2048,1024]{1,0:T(8,128)(2,1)}, f32[2048,1024]{1,0:T(8,128)S(1)}) fusion(bf16[2560,2048]{1,0:T(8,128)(2,1)} %get-tuple-element.353, bf16[2560,1024]{1,0:T(8,128)(2,1)} %get-tuple-element.354), kind=kOutput, calls=%fused_computation.316 | convolution fusion | flops 10739515392 | bytes 28311552 | tf_op jit(solution)/shard_map/dot_general | solution.py:64
  732.6 4.7 collective-permute-done.82
  739.9 17.1 %fusion.119 = (bf16[1024,2048]{1,0:T(8,128)(2,1)}, f32[1024,2048]{1,0:T(8,128)S(1)}) fusion(bf16[2560,1024]{1,0:T(8,128)(2,1)} %get-tuple-element.359, bf16[2560,2048]{1,0:T(8,128)(2,1)} %get-tuple-element.360), kind=kOutput, calls=%fused_computation.317 | convolution fusion | flops 10739515392 | bytes 28311552 | tf_op jit(solution)/shard_map/dot_general | solution.py:64
  759.4 4.2 collective-permute-done.85
  776.2 15.5 %collective-permute-done.90.refs_1_ = bf16[256,2048]{1,0:T(8,128)(2,1)} collective-permute-done((bf16[256,2048]{1,0:T(8,128)(2,1)}, bf16[256,2048]{1,0:T(8,128)(2,1)}, u32[]{:S(2)}, u32[]{:S(2)}) %collective-permute-start.90) | collective-permute-done | bytes 1048608 | tf_op jit(solution)/shard_map/ppermute | solution.py:93
  797.6 4.8 collective-permute-done.89
  807.4 6.7 shard_map.285
  816.3 4.1 fusion
  831.4 15.3 %collective-permute-done.98 = bf16[1024,128]{1,0:T(8,128)(2,1)S(1)} collective-permute-done((bf16[1024,128]{1,0:T(8,128)(2,1)S(1)}, bf16[1024,128]{1,0:T(8,128)(2,1)S(1)}, u32[]{:S(2)}, u32[]{:S(2)}) %collective-permute-start.98) | collective-permute-done | bytes 262176 | tf_op jit(solution)/shard_map/ppermute | solution.py:698
  847.8 4.9 shard_map.286
  854.6 38.7 %shard_map.287 = (f32[4096,128]{1,0:T(8,128)}, f32[4096,128]{1,0:T(8,128)}, f32[4096,128]{1,0:T(8,128)}) custom-call(s32[1]{0:T(128)} %copy.142.length_ref, bf16[4096,128]{1,0:T(8,128)(2,1)} %get-tuple-element.259.q_ref, bf16[4096,128]{1,0:T(8,128)(2,1)} %get-tuple-element.377.do_ref, f32[8,4096]{1,0:T(8,128)} %get-tuple-element.378.log_ref, ...), custom_call_target="tpu_custom_call" | custom-call | flops 32999999488 | bytes 90000000 | tf_op jit(solution)/shard_map/pallas_call | solution.py:580
  900.1 10.0 shard_map.288
  927.6 7.6 collective-permute-done.112
  935.3 11.8 shard_map.289
  947.3 11.2 fusion.120
  976.8 6.7 collective-permute-done.119
  990.5 20.4 %collective-permute-done.117 = bf16[256,2048]{1,0:T(8,128)(2,1)S(1)} collective-permute-done((bf16[256,2048]{1,0:T(8,128)(2,1)S(1)}, bf16[256,2048]{1,0:T(8,128)(2,1)S(1)}, u32[]{:S(2)}, u32[]{:S(2)}) %collective-permute-start.117) | collective-permute-done | bytes 1048608 | tf_op jit(solution)/shard_map/ppermute | solution.py:93
  1020.9 14.8 %collective-permute-done.124.refs_1_ = bf16[192,2048]{1,0:T(8,128)(2,1)} collective-permute-done((bf16[192,2048]{1,0:T(8,128)(2,1)S(1)}, bf16[192,2048]{1,0:T(8,128)(2,1)}, u32[]{:S(2)}, u32[]{:S(2)}) %collective-permute-start.124) | collective-permute-done | bytes 786464 | tf_op jit(solution)/shard_map/ppermute | solution.py:93
  1039.8 16.2 %collective-permute-done.123 = bf16[448,2048]{1,0:T(8,128)(2,1)} collective-permute-done((bf16[448,2048]{1,0:T(8,128)(2,1)}, bf16[448,2048]{1,0:T(8,128)(2,1)}, u32[]{:S(2)}, u32[]{:S(2)}) %collective-permute-start.123) | collective-permute-done | bytes 1835040 | tf_op jit(solution)/shard_map/ppermute | solution.py:93
  1072.4 12.4 %collective-permute-done.129.refs_1_ = bf16[192,2048]{1,0:T(8,128)(2,1)S(1)} collective-permute-done((bf16[192,2048]{1,0:T(8,128)(2,1)S(1)}, bf16[192,2048]{1,0:T(8,128)(2,1)S(1)}, u32[]{:S(2)}, u32[]{:S(2)}) %collective-permute-start.129) | collective-permute-done | bytes 786464 | tf_op jit(solution)/shard_map/ppermute | solution.py:93
  1089.6 14.2 %collective-permute-done.128 = bf16[448,2048]{1,0:T(8,128)(2,1)} collective-permute-done((bf16[448,2048]{1,0:T(8,128)(2,1)}, bf16[448,2048]{1,0:T(8,128)(2,1)}, u32[]{:S(2)}, u32[]{:S(2)}) %collective-permute-start.128) | collective-permute-done | bytes 1835040 | tf_op jit(solution)/shard_map/ppermute | solution.py:93
  1123.4 6.8 shard_map.294
  1130.1 7.3 collective-permute-done.130
  1137.4 15.3 %collective-permute-done.131 = bf16[448,2048]{1,0:T(8,128)(2,1)S(1)} collective-permute-done((bf16[448,2048]{1,0:T(8,128)(2,1)}, bf16[448,2048]{1,0:T(8,128)(2,1)S(1)}, u32[]{:S(2)}, u32[]{:S(2)}) %collective-permute-start.131) | collective-permute-done | bytes 1835040 | tf_op jit(solution)/shard_map/ppermute | solution.py:93
  1175.1 5.2 collective-permute-done.139.refs_1_
  1181.2 4.2 shard_map.293
  (704 shorter events, 335.7 us)
Async XLA Ops:
  6.5 32.2 %collective-permute-start = (bf16[256,2176]{1,0:T(8,128)(2,1)}, bf16[256,2176]{1,0:T(8,128)(2,1)}, u32[]{:S(2)}, u32[]{:S(2)}) collective-permute-start(bf16[256,2176]{1,0:T(8,128)(2,1)} %pad_maximum_fusion.9.refs_0_), channel_id=1, source_target_pairs={{0,4},{4,8},{8,12},{12,0},{1,5},{5,9},{9,13},{13,1},{2,6},{6,10},{... | collective-permute-start | bytes 3342344 | tf_op jit(solution)/shard_map/ppermute | solution.py:93
  9.5 29.2 %collective-permute-start.1 = (bf16[256,2176]{1,0:T(8,128)(2,1)}, bf16[256,2176]{1,0:T(8,128)(2,1)}, u32[]{:S(2)}, u32[]{:S(2)}) collective-permute-start(bf16[256,2176]{1,0:T(8,128)(2,1)} %pad_maximum_fusion.9.refs_0_), channel_id=1, source_target_pairs={{0,2},{1,3},{2,0},{3,1},{4,6},{5,7},{6,4},{7,5},{8,10},{9,11},{10,... | collective-permute-start | bytes 3342344 | tf_op jit(solution)/shard_map/ppermute | solution.py:93
  11.0 59.5 %collective-permute-start.8 = (bf16[256,2176]{1,0:T(8,128)(2,1)}, bf16[256,2176]{1,0:T(8,128)(2,1)}, u32[]{:S(2)}, u32[]{:S(2)}) collective-permute-start(bf16[256,2176]{1,0:T(8,128)(2,1)} %pad_maximum_fusion.9.refs_0_), channel_id=1, source_target_pairs={{0,1},{1,0},{2,3},{3,2},{4,5},{5,4},{6,7},{7,6},{8,9},{9,8},{10,11... | collective-permute-start | bytes 3342344 | tf_op jit(solution)/shard_map/ppermute | solution.py:93
  12.4 26.3 %collective-permute-start.2 = (bf16[1024,512]{1,0:T(8,128)(2,1)}, bf16[1024,512]{1,0:T(8,128)(2,1)}, u32[]{:S(2)}, u32[]{:S(2)}) collective-permute-start(bf16[1024,512]{1,0:T(8,128)(2,1)} %get-tuple-element.494), channel_id=1, source_target_pairs={{0,16},{16,0},{1,17},{17,1},{2,18},{18,2},{3,19},{19,3},{4,20},{20... | collective-permute-start | bytes 3145736 | tf_op jit(solution)/shard_map/ppermute | solution.py:93
  14.0 46.8 %collective-permute-start.5 = (bf16[1024,512]{1,0:T(8,128)(2,1)}, bf16[1024,512]{1,0:T(8,128)(2,1)}, u32[]{:S(2)}, u32[]{:S(2)}) collective-permute-start(bf16[1024,512]{1,0:T(8,128)(2,1)} %get-tuple-element.493), channel_id=1, source_target_pairs={{0,16},{16,0},{1,17},{17,1},{2,18},{18,2},{3,19},{19,3},{4,20},{20... | collective-permute-start | bytes 3145736 | tf_op jit(solution)/shard_map/ppermute | solution.py:93
  38.7 27.9 %collective-permute-start.3 = (bf16[256,2176]{1,0:T(8,128)(2,1)}, bf16[256,2176]{1,0:T(8,128)(2,1)}, u32[]{:S(2)}, u32[]{:S(2)}) collective-permute-start(bf16[256,2176]{1,0:T(8,128)(2,1)} %collective-permute-done.refs_0_), channel_id=1, source_target_pairs={{0,4},{4,8},{8,12},{12,0},{1,5},{5,9},{9,13},{13,1},{2,6},{6,10},{... | collective-permute-start | bytes 3342344 | tf_op jit(solution)/shard_map/ppermute | solution.py:93
  40.3 26.4 %collective-permute-start.4 = (bf16[256,2176]{1,0:T(8,128)(2,1)}, bf16[256,2176]{1,0:T(8,128)(2,1)}, u32[]{:S(2)}, u32[]{:S(2)}) collective-permute-start(bf16[256,2176]{1,0:T(8,128)(2,1)} %collective-permute-done.refs_0_), channel_id=1, source_target_pairs={{0,2},{1,3},{2,0},{3,1},{4,6},{5,7},{6,4},{7,5},{8,10},{9,11},{10,... | collective-permute-start | bytes 3342344 | tf_op jit(solution)/shard_map/ppermute | solution.py:93
  66.6 27.3 %collective-permute-start.6 = (bf16[256,2176]{1,0:T(8,128)(2,1)}, bf16[256,2176]{1,0:T(8,128)(2,1)}, u32[]{:S(2)}, u32[]{:S(2)}) collective-permute-start(bf16[256,2176]{1,0:T(8,128)(2,1)} %collective-permute-done.3.refs_0_), channel_id=1, source_target_pairs={{0,4},{4,8},{8,12},{12,0},{1,5},{5,9},{9,13},{13,1},{2,6},{6,10},{... | collective-permute-start | bytes 3342344 | tf_op jit(solution)/shard_map/ppermute | solution.py:93
  68.0 27.5 %collective-permute-start.7 = (bf16[256,2176]{1,0:T(8,128)(2,1)}, bf16[256,2176]{1,0:T(8,128)(2,1)}, u32[]{:S(2)}, u32[]{:S(2)}) collective-permute-start(bf16[256,2176]{1,0:T(8,128)(2,1)} %collective-permute-done.3.refs_0_), channel_id=1, source_target_pairs={{0,2},{1,3},{2,0},{3,1},{4,6},{5,7},{6,4},{7,5},{8,10},{9,11},{10,... | collective-permute-start | bytes 3342344 | tf_op jit(solution)/shard_map/ppermute | solution.py:93
  70.4 41.6 %collective-permute-start.12 = (bf16[256,2176]{1,0:T(8,128)(2,1)}, bf16[256,2176]{1,0:T(8,128)(2,1)S(1)}, u32[]{:S(2)}, u32[]{:S(2)}) collective-permute-start(bf16[256,2176]{1,0:T(8,128)(2,1)} %collective-permute-done.refs_0_), channel_id=1, source_target_pairs={{0,1},{1,0},{2,3},{3,2},{4,5},{5,4},{6,7},{7,6},{8,9},{9,8},{10,11... | collective-permute-start | bytes 3342344 | tf_op jit(solution)/shard_map/ppermute | solution.py:93
  70.4 41.6 %collective-permute-start.13 = (bf16[256,2176]{1,0:T(8,128)(2,1)}, bf16[256,2176]{1,0:T(8,128)(2,1)S(1)}, u32[]{:S(2)}, u32[]{:S(2)}) collective-permute-start(bf16[256,2176]{1,0:T(8,128)(2,1)} %collective-permute-done.4.refs_1_), channel_id=1, source_target_pairs={{0,1},{1,0},{2,3},{3,2},{4,5},{5,4},{6,7},{7,6},{8,9},{9,8},{10,11... | collective-permute-start | bytes 3342344 | tf_op jit(solution)/shard_map/ppermute | solution.py:93
  85.9 35.9 %collective-permute-start.14 = (bf16[1024,512]{1,0:T(8,128)(2,1)S(1)}, bf16[1024,512]{1,0:T(8,128)(2,1)S(1)}, u32[]{:S(2)}, u32[]{:S(2)}) collective-permute-start(bf16[1024,512]{1,0:T(8,128)(2,1)S(1)} %copy-done.63), channel_id=1, source_target_pairs={{0,16},{16,0},{1,17},{17,1},{2,18},{18,2},{3,19},{19,3},{4,20},{20... | collective-permute-start | bytes 3145736 | tf_op jit(solution)/shard_map/ppermute | solution.py:93
  95.4 26.6 %collective-permute-start.11 = (bf16[256,2176]{1,0:T(8,128)(2,1)}, bf16[256,2176]{1,0:T(8,128)(2,1)S(1)}, u32[]{:S(2)}, u32[]{:S(2)}) collective-permute-start(bf16[256,2176]{1,0:T(8,128)(2,1)} %collective-permute-done.6.refs_0_), channel_id=1, source_target_pairs={{0,2},{1,3},{2,0},{3,1},{4,6},{5,7},{6,4},{7,5},{8,10},{9,11},{10,... | collective-permute-start | bytes 3342344 | tf_op jit(solution)/shard_map/ppermute | solution.py:93
  109.9 55.7 %collective-permute-start.26 = (bf16[256,2048]{1,0:T(8,128)(2,1)S(1)}, bf16[256,2048]{1,0:T(8,128)(2,1)}, u32[]{:S(2)}, u32[]{:S(2)}) collective-permute-start(bf16[256,2048]{1,0:T(8,128)(2,1)S(1)} %copy-done.62), channel_id=1, source_target_pairs={{0,16},{16,0},{1,17},{17,1},{2,18},{18,2},{3,19},{19,3},{4,20},{20... | collective-permute-start | bytes 3145736 | tf_op jit(solution)/shard_map/ppermute | solution.py:93
  124.4 67.4 %collective-permute-start.27 = (bf16[256,2048]{1,0:T(8,128)(2,1)}, bf16[256,2048]{1,0:T(8,128)(2,1)}, u32[]{:S(2)}, u32[]{:S(2)}) collective-permute-start(bf16[256,2048]{1,0:T(8,128)(2,1)} %get-tuple-element.489), channel_id=1, source_target_pairs={{0,16},{16,0},{1,17},{17,1},{2,18},{18,2},{3,19},{19,3},{4,20},{20... | collective-permute-start | bytes 3145736 | tf_op jit(solution)/shard_map/ppermute | solution.py:93
  224.9 25.6 %collective-permute-start.32 = (bf16[256,2048]{1,0:T(8,128)(2,1)S(1)}, bf16[256,2048]{1,0:T(8,128)(2,1)S(1)}, u32[]{:S(2)}, u32[]{:S(2)}) collective-permute-start(bf16[256,2048]{1,0:T(8,128)(2,1)S(1)} %fusion.46), channel_id=1, source_target_pairs={{0,2},{1,3},{2,0},{3,1},{4,6},{5,7},{6,4},{7,5},{8,10},{9,11},{10,... | collective-permute-start | bytes 3145736 | tf_op jit(solution)/shard_map/ppermute | solution.py:93
  252.0 28.7 %collective-permute-start.33 = (bf16[256,2048]{1,0:T(8,128)(2,1)S(1)}, bf16[256,2048]{1,0:T(8,128)(2,1)S(1)}, u32[]{:S(2)}, u32[]{:S(2)}) collective-permute-start(bf16[256,2048]{1,0:T(8,128)(2,1)S(1)} %multiply_convert_fusion.refs_0_), channel_id=1, source_target_pairs={{0,4},{4,8},{8,12},{12,0},{1,5},{5,9},{9,13},{13,1},{2,6},{6,10},{... | collective-permute-start | bytes 3145736 | tf_op jit(solution)/shard_map/ppermute | solution.py:93
  264.1 26.3 %collective-permute-start.37 = (bf16[256,2048]{1,0:T(8,128)(2,1)S(1)}, bf16[256,2048]{1,0:T(8,128)(2,1)S(1)}, u32[]{:S(2)}, u32[]{:S(2)}) collective-permute-start(bf16[256,2048]{1,0:T(8,128)(2,1)S(1)} %multiply_convert_fusion.refs_0_), channel_id=1, source_target_pairs={{0,1},{1,0},{2,3},{3,2},{4,5},{5,4},{6,7},{7,6},{8,9},{9,8},{10,11... | collective-permute-start | bytes 3145736 | tf_op jit(solution)/shard_map/ppermute | solution.py:93
  289.2 27.7 %collective-permute-start.35 = (bf16[256,2048]{1,0:T(8,128)(2,1)S(1)}, bf16[256,2048]{1,0:T(8,128)(2,1)S(1)}, u32[]{:S(2)}, u32[]{:S(2)}) collective-permute-start(bf16[256,2048]{1,0:T(8,128)(2,1)S(1)} %collective-permute-done.33.refs_0_), channel_id=1, source_target_pairs={{0,4},{4,8},{8,12},{12,0},{1,5},{5,9},{9,13},{13,1},{2,6},{6,10},{... | collective-permute-start | bytes 3145736 | tf_op jit(solution)/shard_map/ppermute | solution.py:93
  290.1 26.9 %collective-permute-start.36 = (bf16[256,2048]{1,0:T(8,128)(2,1)S(1)}, bf16[256,2048]{1,0:T(8,128)(2,1)}, u32[]{:S(2)}, u32[]{:S(2)}) collective-permute-start(bf16[256,2048]{1,0:T(8,128)(2,1)S(1)} %collective-permute-done.33.refs_0_), channel_id=1, source_target_pairs={{0,2},{1,3},{2,0},{3,1},{4,6},{5,7},{6,4},{7,5},{8,10},{9,11},{10,... | collective-permute-start | bytes 3145736 | tf_op jit(solution)/shard_map/ppermute | solution.py:93
  290.4 27.1 %collective-permute-start.41 = (bf16[256,2048]{1,0:T(8,128)(2,1)S(1)}, bf16[256,2048]{1,0:T(8,128)(2,1)}, u32[]{:S(2)}, u32[]{:S(2)}) collective-permute-start(bf16[256,2048]{1,0:T(8,128)(2,1)S(1)} %collective-permute-done.33.refs_0_), channel_id=1, source_target_pairs={{0,1},{1,0},{2,3},{3,2},{4,5},{5,4},{6,7},{7,6},{8,9},{9,8},{10,11... | collective-permute-start | bytes 3145736 | tf_op jit(solution)/shard_map/ppermute | solution.py:93
  317.0 27.4 %collective-permute-start.39 = (bf16[256,2048]{1,0:T(8,128)(2,1)S(1)}, bf16[256,2048]{1,0:T(8,128)(2,1)S(1)}, u32[]{:S(2)}, u32[]{:S(2)}) collective-permute-start(bf16[256,2048]{1,0:T(8,128)(2,1)S(1)} %collective-permute-done.35.refs_0_), channel_id=1, source_target_pairs={{0,4},{4,8},{8,12},{12,0},{1,5},{5,9},{9,13},{13,1},{2,6},{6,10},{... | collective-permute-start | bytes 3145736 | tf_op jit(solution)/shard_map/ppermute | solution.py:93
  317.0 27.3 %collective-permute-start.40 = (bf16[256,2048]{1,0:T(8,128)(2,1)S(1)}, bf16[256,2048]{1,0:T(8,128)(2,1)S(1)}, u32[]{:S(2)}, u32[]{:S(2)}) collective-permute-start(bf16[256,2048]{1,0:T(8,128)(2,1)S(1)} %collective-permute-done.35.refs_0_), channel_id=1, source_target_pairs={{0,2},{1,3},{2,0},{3,1},{4,6},{5,7},{6,4},{7,5},{8,10},{9,11},{10,... | collective-permute-start | bytes 3145736 | tf_op jit(solution)/shard_map/ppermute | solution.py:93
  317.4 27.8 %collective-permute-start.43 = (bf16[256,2048]{1,0:T(8,128)(2,1)S(1)}, bf16[256,2048]{1,0:T(8,128)(2,1)}, u32[]{:S(2)}, u32[]{:S(2)}) collective-permute-start(bf16[256,2048]{1,0:T(8,128)(2,1)S(1)} %collective-permute-done.35.refs_0_), channel_id=1, source_target_pairs={{0,1},{1,0},{2,3},{3,2},{4,5},{5,4},{6,7},{7,6},{8,9},{9,8},{10,11... | collective-permute-start | bytes 3145736 | tf_op jit(solution)/shard_map/ppermute | solution.py:93
  344.4 26.3 %collective-permute-start.46 = (bf16[2,256,2048]{2,1,0:T(8,128)(2,1)}, bf16[2,256,2048]{2,1,0:T(8,128)(2,1)S(1)}, u32[]{:S(2)}, u32[]{:S(2)}) collective-permute-start(bf16[2,256,2048]{2,1,0:T(8,128)(2,1)} %get-tuple-element.283), channel_id=1, source_target_pairs={{0,1},{1,0},{2,3},{3,2},{4,5},{5,4},{6,7},{7,6},{8,9},{9,8},{10,11... | collective-permute-start | bytes 6291464 | tf_op jit(solution)/shard_map/ppermute | solution.py:93
  345.2 29.8 %collective-permute-start.49 = (bf16[256,2048]{1,0:T(8,128)(2,1)S(1)}, bf16[256,2048]{1,0:T(8,128)(2,1)}, u32[]{:S(2)}, u32[]{:S(2)}) collective-permute-start(bf16[256,2048]{1,0:T(8,128)(2,1)S(1)} %collective-permute-done.39.refs_0_), channel_id=1, source_target_pairs={{0,1},{1,0},{2,3},{3,2},{4,5},{5,4},{6,7},{7,6},{8,9},{9,8},{10,11... | collective-permute-start | bytes 3145736 | tf_op jit(solution)/shard_map/ppermute | solution.py:93
  370.1 53.6 %collective-permute-start.54 = (bf16[2,256,2048]{2,1,0:T(8,128)(2,1)}, bf16[2,256,2048]{2,1,0:T(8,128)(2,1)}, u32[]{:S(2)}, u32[]{:S(2)}) collective-permute-start(bf16[2,256,2048]{2,1,0:T(8,128)(2,1)} %get-tuple-element.274), channel_id=1, source_target_pairs={{0,1},{1,0},{2,3},{3,2},{4,5},{5,4},{6,7},{7,6},{8,9},{9,8},{10,11... | collective-permute-start | bytes 6291464 | tf_op jit(solution)/shard_map/ppermute | solution.py:93
  370.7 26.8 %collective-permute-start.45 = (bf16[2,256,2048]{2,1,0:T(8,128)(2,1)}, bf16[2,256,2048]{2,1,0:T(8,128)(2,1)}, u32[]{:S(2)}, u32[]{:S(2)}) collective-permute-start(bf16[2,256,2048]{2,1,0:T(8,128)(2,1)} %get-tuple-element.292), channel_id=1, source_target_pairs={{0,1},{1,0},{2,3},{3,2},{4,5},{5,4},{6,7},{7,6},{8,9},{9,8},{10,11... | collective-permute-start | bytes 6291464 | tf_op jit(solution)/shard_map/ppermute | solution.py:93
  396.3 26.2 %collective-permute-start.51 = (bf16[2,256,2048]{2,1,0:T(8,128)(2,1)}, bf16[2,256,2048]{2,1,0:T(8,128)(2,1)S(1)}, u32[]{:S(2)}, u32[]{:S(2)}) collective-permute-start(bf16[2,256,2048]{2,1,0:T(8,128)(2,1)} %get-tuple-element.302), channel_id=1, source_target_pairs={{0,1},{1,0},{2,3},{3,2},{4,5},{5,4},{6,7},{7,6},{8,9},{9,8},{10,11... | collective-permute-start | bytes 6291464 | tf_op jit(solution)/shard_map/ppermute | solution.py:93
  423.3 26.1 %collective-permute-start.53 = (bf16[256,2048]{1,0:T(8,128)(2,1)S(1)}, bf16[256,2048]{1,0:T(8,128)(2,1)S(1)}, u32[]{:S(2)}, u32[]{:S(2)}) collective-permute-start(bf16[256,2048]{1,0:T(8,128)(2,1)S(1)} %fusion.33), channel_id=1, source_target_pairs={{0,4},{4,8},{8,12},{12,0},{1,5},{5,9},{9,13},{13,1},{2,6},{6,10},{... | collective-permute-start | bytes 3145736 | tf_op jit(solution)/shard_map/ppermute | solution.py:93
  423.4 26.0 %collective-permute-start.52 = (bf16[256,2048]{1,0:T(8,128)(2,1)S(1)}, bf16[256,2048]{1,0:T(8,128)(2,1)S(1)}, u32[]{:S(2)}, u32[]{:S(2)}) collective-permute-start(bf16[256,2048]{1,0:T(8,128)(2,1)S(1)} %fusion.47), channel_id=1, source_target_pairs={{0,2},{1,3},{2,0},{3,1},{4,6},{5,7},{6,4},{7,5},{8,10},{9,11},{10,... | collective-permute-start | bytes 3145736 | tf_op jit(solution)/shard_map/ppermute | solution.py:93
  505.9 47.2 %collective-permute-start.69 = (bf16[256,2048]{1,0:T(8,128)(2,1)}, bf16[256,2048]{1,0:T(8,128)(2,1)S(1)}, u32[]{:S(2)}, u32[]{:S(2)}) collective-permute-start(bf16[256,2048]{1,0:T(8,128)(2,1)} %multiply_convert_fusion.1.refs_0_), channel_id=1, source_target_pairs={{0,1},{1,0},{2,3},{3,2},{4,5},{5,4},{6,7},{7,6},{8,9},{9,8},{10,11... | collective-permute-start | bytes 3145736 | tf_op jit(solution)/shard_map/ppermute | solution.py:93
  534.5 42.8 %collective-permute-start.67 = (bf16[256,2048]{1,0:T(8,128)(2,1)}, bf16[256,2048]{1,0:T(8,128)(2,1)}, u32[]{:S(2)}, u32[]{:S(2)}) collective-permute-start(bf16[256,2048]{1,0:T(8,128)(2,1)} %collective-permute-done.59.refs_0_), channel_id=1, source_target_pairs={{0,1},{1,0},{2,3},{3,2},{4,5},{5,4},{6,7},{7,6},{8,9},{9,8},{10,11... | collective-permute-start | bytes 3145736 | tf_op jit(solution)/shard_map/ppermute | solution.py:93
  553.1 48.2 %collective-permute-start.65 = (bf16[256,2048]{1,0:T(8,128)(2,1)S(1)}, bf16[256,2048]{1,0:T(8,128)(2,1)}, u32[]{:S(2)}, u32[]{:S(2)}) collective-permute-start(bf16[256,2048]{1,0:T(8,128)(2,1)S(1)} %collective-permute-done.61.refs_0_), channel_id=1, source_target_pairs={{0,1},{1,0},{2,3},{3,2},{4,5},{5,4},{6,7},{7,6},{8,9},{9,8},{10,11... | collective-permute-start | bytes 3145736 | tf_op jit(solution)/shard_map/ppermute | solution.py:93
  575.6 48.5 %collective-permute-start.80 = (bf16[2,272,2048]{2,1,0:T(8,128)(2,1)}, bf16[2,272,2048]{2,1,0:T(8,128)(2,1)S(1)}, u32[]{:S(2)}, u32[]{:S(2)}) collective-permute-start(bf16[2,272,2048]{2,1,0:T(8,128)(2,1)} %get-tuple-element.349), channel_id=1, source_target_pairs={{0,1},{1,0},{2,3},{3,2},{4,5},{5,4},{6,7},{7,6},{8,9},{9,8},{10,11... | collective-permute-start | bytes 6684680 | tf_op jit(solution)/shard_map/ppermute | solution.py:93
  575.7 25.6 %collective-permute-start.74 = (bf16[256,2048]{1,0:T(8,128)(2,1)S(1)}, bf16[256,2048]{1,0:T(8,128)(2,1)S(1)}, u32[]{:S(2)}, u32[]{:S(2)}) collective-permute-start(bf16[256,2048]{1,0:T(8,128)(2,1)S(1)} %collective-permute-done.63.refs_0_), channel_id=1, source_target_pairs={{0,2},{1,3},{2,0},{3,1},{4,6},{5,7},{6,4},{7,5},{8,10},{9,11},{10,... | collective-permute-start | bytes 3145736 | tf_op jit(solution)/shard_map/ppermute | solution.py:93
  577.3 51.3 %collective-permute-start.75 = (bf16[256,2048]{1,0:T(8,128)(2,1)S(1)}, bf16[256,2048]{1,0:T(8,128)(2,1)}, u32[]{:S(2)}, u32[]{:S(2)}) collective-permute-start(bf16[256,2048]{1,0:T(8,128)(2,1)S(1)} %collective-permute-done.63.refs_0_), channel_id=1, source_target_pairs={{0,1},{1,0},{2,3},{3,2},{4,5},{5,4},{6,7},{7,6},{8,9},{9,8},{10,11... | collective-permute-start | bytes 3145736 | tf_op jit(solution)/shard_map/ppermute | solution.py:93
  601.3 48.6 %collective-permute-start.72 = (bf16[2,272,2048]{2,1,0:T(8,128)(2,1)}, bf16[2,272,2048]{2,1,0:T(8,128)(2,1)}, u32[]{:S(2)}, u32[]{:S(2)}) collective-permute-start(bf16[2,272,2048]{2,1,0:T(8,128)(2,1)} %get-tuple-element.332), channel_id=1, source_target_pairs={{0,1},{1,0},{2,3},{3,2},{4,5},{5,4},{6,7},{7,6},{8,9},{9,8},{10,11... | collective-permute-start | bytes 6684680 | tf_op jit(solution)/shard_map/ppermute | solution.py:93
  601.3 27.4 %collective-permute-start.76 = (bf16[256,2048]{1,0:T(8,128)(2,1)S(1)}, bf16[256,2048]{1,0:T(8,128)(2,1)}, u32[]{:S(2)}, u32[]{:S(2)}) collective-permute-start(bf16[256,2048]{1,0:T(8,128)(2,1)S(1)} %collective-permute-done.74.refs_1_), channel_id=1, source_target_pairs={{0,1},{1,0},{2,3},{3,2},{4,5},{5,4},{6,7},{7,6},{8,9},{9,8},{10,11... | collective-permute-start | bytes 3145736 | tf_op jit(solution)/shard_map/ppermute | solution.py:93
  624.0 30.8 %collective-permute-start.71 = (bf16[2,272,2048]{2,1,0:T(8,128)(2,1)}, bf16[2,272,2048]{2,1,0:T(8,128)(2,1)}, u32[]{:S(2)}, u32[]{:S(2)}) collective-permute-start(bf16[2,272,2048]{2,1,0:T(8,128)(2,1)} %get-tuple-element.330), channel_id=1, source_target_pairs={{0,1},{1,0},{2,3},{3,2},{4,5},{5,4},{6,7},{7,6},{8,9},{9,8},{10,11... | collective-permute-start | bytes 6684680 | tf_op jit(solution)/shard_map/ppermute | solution.py:93
  649.4 30.8 %collective-permute-start.77 = (bf16[2,272,2048]{2,1,0:T(8,128)(2,1)}, bf16[2,272,2048]{2,1,0:T(8,128)(2,1)S(1)}, u32[]{:S(2)}, u32[]{:S(2)}) collective-permute-start(bf16[2,272,2048]{2,1,0:T(8,128)(2,1)} %get-tuple-element.341), channel_id=1, source_target_pairs={{0,1},{1,0},{2,3},{3,2},{4,5},{5,4},{6,7},{7,6},{8,9},{9,8},{10,11... | collective-permute-start | bytes 6684680 | tf_op jit(solution)/shard_map/ppermute | solution.py:93
  653.2 26.6 %collective-permute-start.73 = (bf16[272,2048]{1,0:T(8,128)(2,1)S(1)}, bf16[272,2048]{1,0:T(8,128)(2,1)S(1)}, u32[]{:S(2)}, u32[]{:S(2)}) collective-permute-start(bf16[272,2048]{1,0:T(8,128)(2,1)S(1)} %fusion.43), channel_id=1, source_target_pairs={{0,2},{1,3},{2,0},{3,1},{4,6},{5,7},{6,4},{7,5},{8,10},{9,11},{10,... | collective-permute-start | bytes 3342344 | tf_op jit(solution)/shard_map/ppermute | solution.py:93
  681.0 27.7 %collective-permute-start.79 = (bf16[272,2048]{1,0:T(8,128)(2,1)S(1)}, bf16[272,2048]{1,0:T(8,128)(2,1)}, u32[]{:S(2)}, u32[]{:S(2)}) collective-permute-start(bf16[272,2048]{1,0:T(8,128)(2,1)S(1)} %fusion.14), channel_id=1, source_target_pairs={{0,4},{4,8},{8,12},{12,0},{1,5},{5,9},{9,13},{13,1},{2,6},{6,10},{... | collective-permute-start | bytes 3342344 | tf_op jit(solution)/shard_map/ppermute | solution.py:93
  681.3 27.3 %collective-permute-start.78 = (bf16[272,2048]{1,0:T(8,128)(2,1)S(1)}, bf16[272,2048]{1,0:T(8,128)(2,1)}, u32[]{:S(2)}, u32[]{:S(2)}) collective-permute-start(bf16[272,2048]{1,0:T(8,128)(2,1)S(1)} %fusion.42), channel_id=1, source_target_pairs={{0,2},{1,3},{2,0},{3,1},{4,6},{5,7},{6,4},{7,5},{8,10},{9,11},{10,... | collective-permute-start | bytes 3342344 | tf_op jit(solution)/shard_map/ppermute | solution.py:93
  702.9 35.0 %collective-permute-start.83 = (bf16[1024,512]{1,0:T(8,128)(2,1)}, bf16[1024,512]{1,0:T(8,128)(2,1)}, u32[]{:S(2)}, u32[]{:S(2)}) collective-permute-start(bf16[1024,512]{1,0:T(8,128)(2,1)} %get-tuple-element.480), channel_id=1, source_target_pairs={{0,16},{16,0},{1,17},{17,1},{2,18},{18,2},{3,19},{19,3},{4,20},{20... | collective-permute-start | bytes 3145736 | tf_op jit(solution)/shard_map/ppermute | solution.py:93
  704.4 59.7 %collective-permute-start.86 = (bf16[1024,512]{1,0:T(8,128)(2,1)}, bf16[1024,512]{1,0:T(8,128)(2,1)}, u32[]{:S(2)}, u32[]{:S(2)}) collective-permute-start(bf16[1024,512]{1,0:T(8,128)(2,1)} %get-tuple-element.479), channel_id=1, source_target_pairs={{0,16},{16,0},{1,17},{17,1},{2,18},{18,2},{3,19},{19,3},{4,20},{20... | collective-permute-start | bytes 3145736 | tf_op jit(solution)/shard_map/ppermute | solution.py:93
  710.7 26.6 %collective-permute-start.82 = (bf16[272,2048]{1,0:T(8,128)(2,1)S(1)}, bf16[272,2048]{1,0:T(8,128)(2,1)S(1)}, u32[]{:S(2)}, u32[]{:S(2)}) collective-permute-start(bf16[272,2048]{1,0:T(8,128)(2,1)S(1)} %fusion.12), channel_id=1, source_target_pairs={{0,4},{4,8},{8,12},{12,0},{1,5},{5,9},{9,13},{13,1},{2,6},{6,10},{... | collective-permute-start | bytes 3342344 | tf_op jit(solution)/shard_map/ppermute | solution.py:93
  737.9 25.7 %collective-permute-start.85 = (bf16[272,2048]{1,0:T(8,128)(2,1)S(1)}, bf16[272,2048]{1,0:T(8,128)(2,1)S(1)}, u32[]{:S(2)}, u32[]{:S(2)}) collective-permute-start(bf16[272,2048]{1,0:T(8,128)(2,1)S(1)} %fusion.16), channel_id=1, source_target_pairs={{0,4},{4,8},{8,12},{12,0},{1,5},{5,9},{9,13},{13,1},{2,6},{6,10},{... | collective-permute-start | bytes 3342344 | tf_op jit(solution)/shard_map/ppermute | solution.py:93
  774.7 32.7 %collective-permute-start.92 = (bf16[1024,512]{1,0:T(8,128)(2,1)S(1)}, bf16[1024,512]{1,0:T(8,128)(2,1)S(1)}, u32[]{:S(2)}, u32[]{:S(2)}) collective-permute-start(bf16[1024,512]{1,0:T(8,128)(2,1)S(1)} %get-tuple-element.478), channel_id=1, source_target_pairs={{0,16},{16,0},{1,17},{17,1},{2,18},{18,2},{3,19},{19,3},{4,20},{20... | collective-permute-start | bytes 3145736 | tf_op jit(solution)/shard_map/ppermute | solution.py:93
  776.2 31.2 %collective-permute-start.93 = (bf16[256,2048]{1,0:T(8,128)(2,1)}, bf16[256,2048]{1,0:T(8,128)(2,1)}, u32[]{:S(2)}, u32[]{:S(2)}) collective-permute-start(bf16[256,2048]{1,0:T(8,128)(2,1)} %get-tuple-element.461.refs_0_), channel_id=1, source_target_pairs={{0,1},{1,0},{2,3},{3,2},{4,5},{5,4},{6,7},{7,6},{8,9},{9,8},{10,11... | collective-permute-start | bytes 3145736 | tf_op jit(solution)/shard_map/ppermute | solution.py:93
  802.5 45.3 %collective-permute-start.100 = (bf16[1024,512]{1,0:T(8,128)(2,1)}, bf16[1024,512]{1,0:T(8,128)(2,1)S(1)}, u32[]{:S(2)}, u32[]{:S(2)}) collective-permute-start(bf16[1024,512]{1,0:T(8,128)(2,1)} %get-tuple-element.477), channel_id=1, source_target_pairs={{0,16},{16,0},{1,17},{17,1},{2,18},{18,2},{3,19},{19,3},{4,20},{20... | collective-permute-start | bytes 3145736 | tf_op jit(solution)/shard_map/ppermute | solution.py:93
  805.8 90.0 %collective-permute-start.102 = (bf16[256,2048]{1,0:T(8,128)(2,1)}, bf16[256,2048]{1,0:T(8,128)(2,1)S(1)}, u32[]{:S(2)}, u32[]{:S(2)}) collective-permute-start(bf16[256,2048]{1,0:T(8,128)(2,1)} %get-tuple-element.476), channel_id=1, source_target_pairs={{0,16},{16,0},{1,17},{17,1},{2,18},{18,2},{3,19},{19,3},{4,20},{20... | collective-permute-start | bytes 3145736 | tf_op jit(solution)/shard_map/ppermute | solution.py:93
  830.9 96.7 %collective-permute-start.111 = (bf16[256,2048]{1,0:T(8,128)(2,1)}, bf16[256,2048]{1,0:T(8,128)(2,1)S(1)}, u32[]{:S(2)}, u32[]{:S(2)}) collective-permute-start(bf16[256,2048]{1,0:T(8,128)(2,1)} %get-tuple-element.475), channel_id=1, source_target_pairs={{0,16},{16,0},{1,17},{17,1},{2,18},{18,2},{3,19},{19,3},{4,20},{20... | collective-permute-start | bytes 3145736 | tf_op jit(solution)/shard_map/ppermute | solution.py:93
  852.6 40.7 %collective-permute-start.101 = (f32[18,2048]{1,0:T(8,128)S(1)}, f32[18,2048]{1,0:T(8,128)S(1)}, u32[]{:S(2)}, u32[]{:S(2)}) collective-permute-start(f32[18,2048]{1,0:T(8,128)S(1)} %add_add_fusion), channel_id=1, source_target_pairs={{0,16},{16,0},{1,17},{17,1},{2,18},{18,2},{3,19},{19,3},{4,20},{20... | collective-permute-start | bytes 442376 | tf_op jit(solution)/shard_map/ppermute | solution.py:256
  853.1 45.6 %collective-permute-start.103 = (bf16[4,64,2048]{2,1,0:T(8,128)(2,1)}, bf16[4,64,2048]{2,1,0:T(8,128)(2,1)S(1)}, u32[]{:S(2)}, u32[]{:S(2)}) collective-permute-start(bf16[4,64,2048]{2,1,0:T(8,128)(2,1)} %constant_dynamic-slice_fusion.2), channel_id=1, source_target_pairs={{0,16},{16,0},{1,17},{17,1},{2,18},{18,2},{3,19},{19,3},{4,20},{20... | collective-permute-start | bytes 3145736 | tf_op jit(solution)/shard_map/ppermute | solution.py:93
  983.5 33.3 %collective-permute-start.126 = (bf16[2,256,2048]{2,1,0:T(8,128)(2,1)}, bf16[2,256,2048]{2,1,0:T(8,128)(2,1)S(1)}, u32[]{:S(2)}, u32[]{:S(2)}) collective-permute-start(bf16[2,256,2048]{2,1,0:T(8,128)(2,1)} %bitcast.64), channel_id=1, source_target_pairs={{0,1},{1,0},{2,3},{3,2},{4,5},{5,4},{6,7},{7,6},{8,9},{9,8},{10,11... | collective-permute-start | bytes 6291464 | tf_op jit(solution)/shard_map/ppermute | solution.py:93
  983.5 29.1 %collective-permute-start.120 = (bf16[64,2048]{1,0:T(8,128)(2,1)S(1)}, bf16[64,2048]{1,0:T(8,128)(2,1)S(1)}, u32[]{:S(2)}, u32[]{:S(2)}) collective-permute-start(bf16[64,2048]{1,0:T(8,128)(2,1)S(1)} %collective-permute-done.119), channel_id=1, source_target_pairs={{0,4},{4,8},{8,12},{12,0},{1,5},{5,9},{9,13},{13,1},{2,6},{6,10},{... | collective-permute-start | bytes 786440 | tf_op jit(solution)/shard_map/ppermute | solution.py:93
  1012.7 43.4 %collective-permute-start.123 = (bf16[448,2048]{1,0:T(8,128)(2,1)}, bf16[448,2048]{1,0:T(8,128)(2,1)}, u32[]{:S(2)}, u32[]{:S(2)}) collective-permute-start(bf16[448,2048]{1,0:T(8,128)(2,1)} %pad_maximum_fusion.5), channel_id=1, source_target_pairs={{0,4},{4,8},{8,12},{12,0},{1,5},{5,9},{9,13},{13,1},{2,6},{6,10},{... | collective-permute-start | bytes 5505032 | tf_op jit(solution)/shard_map/ppermute | solution.py:93
  1017.5 39.8 %collective-permute-start.122 = (bf16[256,2048]{1,0:T(8,128)(2,1)}, bf16[256,2048]{1,0:T(8,128)(2,1)S(1)}, u32[]{:S(2)}, u32[]{:S(2)}) collective-permute-start(bf16[256,2048]{1,0:T(8,128)(2,1)} %fusion.51), channel_id=1, source_target_pairs={{0,2},{1,3},{2,0},{3,1},{4,6},{5,7},{6,4},{7,5},{8,10},{9,11},{10,... | collective-permute-start | bytes 3145736 | tf_op jit(solution)/shard_map/ppermute | solution.py:93
  1019.4 42.0 %collective-permute-start.125 = (bf16[4,64,2048]{2,1,0:T(8,128)(2,1)S(1)}, bf16[4,64,2048]{2,1,0:T(8,128)(2,1)}, u32[]{:S(2)}, u32[]{:S(2)}) collective-permute-start(bf16[4,64,2048]{2,1,0:T(8,128)(2,1)S(1)} %pad_maximum_fusion.12), channel_id=1, source_target_pairs={{0,16},{16,0},{1,17},{17,1},{2,18},{18,2},{3,19},{19,3},{4,20},{20... | collective-permute-start | bytes 3145736 | tf_op jit(solution)/shard_map/ppermute | solution.py:93
  1061.4 42.4 %collective-permute-start.128 = (bf16[448,2048]{1,0:T(8,128)(2,1)}, bf16[448,2048]{1,0:T(8,128)(2,1)}, u32[]{:S(2)}, u32[]{:S(2)}) collective-permute-start(bf16[448,2048]{1,0:T(8,128)(2,1)} %pad_maximum_fusion.6), channel_id=1, source_target_pairs={{0,4},{4,8},{8,12},{12,0},{1,5},{5,9},{9,13},{13,1},{2,6},{6,10},{... | collective-permute-start | bytes 5505032 | tf_op jit(solution)/shard_map/ppermute | solution.py:93
  1065.4 40.5 %collective-permute-start.127 = (bf16[256,2048]{1,0:T(8,128)(2,1)S(1)}, bf16[256,2048]{1,0:T(8,128)(2,1)S(1)}, u32[]{:S(2)}, u32[]{:S(2)}) collective-permute-start(bf16[256,2048]{1,0:T(8,128)(2,1)S(1)} %copy-done.60), channel_id=1, source_target_pairs={{0,2},{1,3},{2,0},{3,1},{4,6},{5,7},{6,4},{7,5},{8,10},{9,11},{10,... | collective-permute-start | bytes 3145736 | tf_op jit(solution)/shard_map/ppermute | solution.py:93
  1111.2 41.6 %collective-permute-start.131 = (bf16[448,2048]{1,0:T(8,128)(2,1)}, bf16[448,2048]{1,0:T(8,128)(2,1)S(1)}, u32[]{:S(2)}, u32[]{:S(2)}) collective-permute-start(bf16[448,2048]{1,0:T(8,128)(2,1)} %pad_maximum_fusion.7), channel_id=1, source_target_pairs={{0,4},{4,8},{8,12},{12,0},{1,5},{5,9},{9,13},{13,1},{2,6},{6,10},{... | collective-permute-start | bytes 5505032 | tf_op jit(solution)/shard_map/ppermute | solution.py:93
  1119.0 37.7 %collective-permute-start.140 = (bf16[192,2048]{1,0:T(8,128)(2,1)}, bf16[192,2048]{1,0:T(8,128)(2,1)S(1)}, u32[]{:S(2)}, u32[]{:S(2)}) collective-permute-start(bf16[192,2048]{1,0:T(8,128)(2,1)} %slice.307.refs_0_), channel_id=1, source_target_pairs={{0,16},{16,0},{1,17},{17,1},{2,18},{18,2},{3,19},{19,3},{4,20},{20... | collective-permute-start | bytes 2359304 | tf_op jit(solution)/shard_map/ppermute | solution.py:93
  (215 other events, 2804.5 us)
